TPU v7x, 128 devices: a whole 4x4x4 slice. The times are simulated.
128 devices in a mesh: ctx: 32 (over y, x, core), tp: 4 (over z).
Axes of the slice: x: 4, y: 4, z: 4, core: 2. Of those that a mesh axis runs over, the one named last changes fastest.
Arguments:
- hidden_in: bfloat16 [32, 4096], P('ctx', 'tp'), may hold values from -6 to 6
- query: bfloat16 [32, 4096], P('ctx', 'tp')
- new_key: bfloat16 [32, 1024], P('ctx', 'tp'), may hold values from -8 to 8
- new_value: bfloat16 [32, 1024], P('ctx', 'tp'), may hold values from -6 to 6
- cache_keys: bfloat16 [32, 16384, 1024], P(None, 'ctx', 'tp')
- cache_values: bfloat16 [32, 16384, 1024], P(None, 'ctx', 'tp'), may hold values from -6 to 6
- lengths: int32 [32], replicated, may hold values from 1 to 16384, as said below
- out_weight: bfloat16 [4096, 4096], P('tp', 'ctx'), may hold values from -0.09375 to 0.09375
- norm_gain: float32 [4096], P('tp'), may hold values from 0.1 to 1.9
- w_gate: bfloat16 [4096, 14336], P(None, ('ctx', 'tp')), may hold values from -0.09375 to 0.09375
- w_up: bfloat16 [4096, 14336], P(None, ('ctx', 'tp')), may hold values from -0.09375 to 0.09375
- w_down: bfloat16 [14336, 4096], P(('ctx', 'tp')), may hold values from -0.1875 to 0.1875
Outputs:
- layer_out: bfloat16 [32, 4096], P('ctx', 'tp')
Inputs may be any that keep to these rules, and one draw needn't show every extreme that they name: Positions 0 to lengths[b] - 1 of sequence b hold its cached tokens; some sequence has all 16384 positions valid and another exactly one.
All inputs are finite; a program needn't handle non-finite values.
Results may differ from a plain program's by a relative error of at most 0.009.
Values may be sent and summed in bfloat16 or wider, within the bound.
No kernel may reach another device: no remote copies, remote signals or barrier semaphores. Data moves between devices by JAX's collectives and lax.ppermute only.
A program may use at most 64 MiB of HBM per device.

v0:
```python
import math

import jax
import jax.numpy as jnp
from jax import lax
from jax.sharding import PartitionSpec as P

D = 4096
HD = 128


EPSILON = 1e-05
MASKED = -1e30


def shards(
    hidden_in,
    query,
    new_key,
    new_value,
    cache_keys,
    cache_values,
    lengths,
    out_weight,
    norm_gain,
    w_gate,
    w_up,
    w_down,
):
    factor = 1.0 / math.sqrt(HD)
    seq_dev = query.shape[0]
    ctx_dev = cache_keys.shape[1]
    kv_dev = cache_keys.shape[2] // HD
    heads_dev = query.shape[1] // HD
    group_size = heads_dev // kv_dev
    ctx_rank = lax.axis_index("ctx")
    home_row = ctx_rank * seq_dev
    all_query, all_key, all_value = (
        lax.all_gather(query, "ctx", axis=0, tiled=True),
        lax.all_gather(new_key, "ctx", axis=0, tiled=True),
        lax.all_gather(new_value, "ctx", axis=0, tiled=True),
    )
    seq_count = all_query.shape[0]
    queries = all_query.reshape(seq_count, kv_dev, group_size, HD)
    keys_view = cache_keys.reshape(seq_count, ctx_dev, kv_dev, HD)
    values_view = cache_values.reshape(seq_count, ctx_dev, kv_dev, HD)
    scores = (
        jnp.einsum("bkgd,btkd->bkgt", queries, keys_view, preferred_element_type=jnp.float32)
        * factor
    )
    places = ctx_rank * ctx_dev + lax.iota(jnp.int32, ctx_dev)
    is_valid = (places[None, :] < lengths[:, None])[:, None, None, :]
    block_max = jnp.max(jnp.where(is_valid, scores, MASKED), axis=-1)
    weights = jnp.where(is_valid, jnp.exp(scores - block_max[..., None]), 0.0).astype(jnp.bfloat16)
    block_den = jnp.sum(weights.astype(jnp.float32), axis=-1)
    block_num = jnp.einsum(
        "bkgt,btkd->bkgd", weights, values_view, preferred_element_type=jnp.float32
    )
    peak_score = lax.pmax(block_max, "ctx")
    rescale = jnp.exp(block_max - peak_score)
    cache_den, cache_num = lax.psum((block_den * rescale, block_num * rescale[..., None]), "ctx")
    own_score = (
        jnp.einsum(
            "oips,ois->oip",
            queries,
            all_key.reshape(seq_count, kv_dev, HD),
            preferred_element_type=jnp.float32,
        )
        * factor
    )
    top_score = jnp.maximum(peak_score, own_score)
    keep_share = jnp.exp(peak_score - top_score)
    fresh_share = jnp.exp(own_score - top_score)
    numerator = cache_num * keep_share[..., None] + fresh_share[..., None] * all_value.astype(
        jnp.float32
    ).reshape(seq_count, kv_dev, 1, HD)
    attention = (
        (numerator / (cache_den * keep_share + fresh_share)[..., None])
        .reshape(seq_count, heads_dev * HD)
        .astype(jnp.bfloat16)
    )
    projected = jnp.dot(attention, out_weight, preferred_element_type=jnp.float32)
    regrouped = lax.all_to_all(projected, "ctx", split_axis=0, concat_axis=1, tiled=True)
    proj_share = lax.psum_scatter(regrouped, "tp", scatter_dimension=1, tiled=True)
    mid_stream = hidden_in.astype(jnp.float32) + proj_share
    square_total = lax.psum(jnp.sum(mid_stream * mid_stream, axis=1), "tp")
    normed = (mid_stream * lax.rsqrt(square_total / D + EPSILON)[:, None] * norm_gain).astype(
        jnp.bfloat16
    )
    full_rows = lax.all_gather(normed, "tp", axis=1, tiled=True)
    piece = lax.all_gather(full_rows, "ctx", axis=0, tiled=True)
    gate_out = jnp.dot(piece, w_gate, preferred_element_type=jnp.float32)
    up_out = jnp.dot(piece, w_up, preferred_element_type=jnp.float32)
    activation = (jax.nn.silu(gate_out) * up_out).astype(jnp.bfloat16)
    partial_ffn = jnp.dot(activation, w_down, preferred_element_type=jnp.float32)
    summed_all = lax.psum(partial_ffn, ("ctx", "tp"))
    col_width = hidden_in.shape[1]
    row_block = lax.dynamic_slice_in_dim(summed_all, home_row, seq_dev, 0)
    ffn_block = lax.dynamic_slice_in_dim(row_block, lax.axis_index("tp") * col_width, col_width, 1)
    return (mid_stream + ffn_block).astype(jnp.bfloat16)


def solution(mesh):
    return jax.shard_map(
        shards,
        mesh=mesh,
        in_specs=(
            P("ctx", "tp"),
            P("ctx", "tp"),
            P("ctx", "tp"),
            P("ctx", "tp"),
            P(None, "ctx", "tp"),
            P(None, "ctx", "tp"),
            P(),
            P("tp", "ctx"),
            P("tp"),
            P(None, ("ctx", "tp")),
            P(None, ("ctx", "tp")),
            P(("ctx", "tp"), None),
        ),
        out_specs=P("ctx", "tp"),
        check_vma=False,
    )
```

profile of v0, /device:TPU:0, one launch (start us, length us, event | category | flops | bytes accessed | tf_op | source)
XLA Modules:
  0.0 469.2 jit_solution(10096595805325763070)
XLA Ops:
  6.5 0.0 copy-start
  6.5 0.0 all-reduce.3.cloned.1.call-start
  6.5 25.1 %all-gather = bf16[32,1,1024]{2,1,0:T(2,128)(2,1)S(1)} all-gather(bf16[1,1,1024]{2,1,0:T(2,128)(2,1)} %bitcast.74), channel_id=1, replica_groups=mesh['ctx'=32,'tp'=4] {'ctx'}, dimensions={0}, use_global_device_ids=true | all-gather | bytes 67584 | tf_op jit(solution)/shard_map/all_gather | solution.py:39
  31.6 0.4 reduce.1
  32.0 0.0 copy-start.5
  32.1 0.8 broadcast_compare_fusion
  32.8 5.8 %select_reduce_fusion = (f32[32,2,4]{2,1,0:T(2,128)S(1)}, f32[32,2,4,512]{3,2,1,0:T(4,128)S(1)}) fusion(pred[32,512]{1,0:T(8,128)(4,1)S(1)} %broadcast_compare_fusion, bf16[32,2,4,128]{3,2,1,0:T(4,128)(2,1)S(1)} %reshape.58, bf16[32,512,256]{2,1,0:T(8,128)(2,1)} %param.16), kind=kOutput, calls=%fused_computation.13 | convolution fusion | flops 33947392 | bytes 8995840 | tf_op jit(solution)/shard_map/bkgd,btkd->bkgt/dot_general | solution.py:48
  38.6 0.0 copy-start.4
  38.6 0.0 copy-start.3
  38.6 0.1 copy.34
  38.7 65.2 %pmax.7 = f32[32,2,4]{0,2,1:T(4,128)S(1)} all-reduce(f32[32,2,4]{0,2,1:T(4,128)S(1)} %copy.34), channel_id=1, replica_groups=mesh['ctx'=32,'tp'=4] {'ctx'}, use_global_device_ids=true, to_apply=%region_1.2 | all-reduce | flops 256 | bytes 2048 | tf_op jit(solution)/shard_map/pmax | solution.py:59
  103.9 0.0 copy-done.5
  103.9 0.0 copy-start.7
  103.9 0.4 convert_reduce_fusion
  104.4 0.1 copy.38
  104.5 0.6 fusion.35
  105.1 0.0 copy-done.4
  105.1 0.0 copy-done.7
  105.1 0.7 copy.35
  105.8 0.0 copy-start.2
  105.8 0.0 copy-start.1
  105.8 5.5 %fusion.9 = f32[32,2,4,128]{3,2,1,0:T(4,128)} fusion(f32[32,2,4]{2,1,0:T(2,128)} %copy.35, f32[32,2,4,512]{3,2,1,0:T(4,128)S(1)} %get-tuple-element.11, f32[32,2,4]{2,1,0:T(2,128)} %copy-done.4, pred[32,512]{1,0:T(8,128)(4,1)S(1)} %broadcast_compare_fusion, bf16[32,512,256]{2,1,0:T(8,128)(2,1)} %param.17), kind=kOutput, calls=%fused_computation.7 | convolution fusion | flops 33980416 | bytes 9062400 | tf_op jit(solution)/shard_map/bkgt,btkd->bkgd/dot_general | solution.py:56
  111.2 0.0 copy-start.6
  111.2 0.0 all-reduce.3.cloned.1.call-update
  111.3 0.0 reduce-scatter.4.cloned.1.call-start
  111.3 20.5 %all-gather.1 = bf16[32,1,256]{2,1,0:T(2,128)(2,1)S(1)} all-gather(bf16[1,1,256]{2,1,0:T(2,128)(2,1)} %bitcast.76), channel_id=1, replica_groups=mesh['ctx'=32,'tp'=4] {'ctx'}, dimensions={0}, use_global_device_ids=true | all-gather | bytes 16896 | tf_op jit(solution)/shard_map/all_gather | solution.py:40
  131.8 1.0 fusion.22
  132.9 0.1 copy.42
  133.0 66.7 %psum.29 = f32[32,2,4]{0,2,1:T(4,128)S(1)} all-reduce(f32[32,2,4]{0,2,1:T(4,128)} %bitcast.73), channel_id=1, replica_groups=mesh['ctx'=32,'tp'=4] {'ctx'}, use_global_device_ids=true, to_apply=%region_4.5 | all-reduce | flops 256 | bytes 2048 | tf_op jit(solution)/shard_map/psum | solution.py:61
  199.7 0.7 multiply_add_fusion
  200.4 20.5 %all-gather.2 = bf16[32,1,256]{2,1,0:T(2,128)(2,1)S(1)} all-gather(bf16[1,1,256]{2,1,0:T(2,128)(2,1)} %bitcast.77), channel_id=1, replica_groups=mesh['ctx'=32,'tp'=4] {'ctx'}, dimensions={0}, use_global_device_ids=true | all-gather | bytes 16896 | tf_op jit(solution)/shard_map/all_gather | solution.py:41
  220.9 0.1 copy.39
  221.0 0.1 copy.36
  221.1 0.1 copy.37
  221.2 0.0 all-reduce.3.cloned.1.call-done
  221.2 1.2 fusion.18
  222.5 0.0 copy-done.3
  222.5 0.2 fusion.36
  222.6 13.5 %all_to_all.16 = f32[32,1,128]{2,1,0:T(1,128)S(1)} all-to-all(f32[32,1,128]{2,1,0:T(1,128)S(1)} %bitcast.68), channel_id=1, replica_groups=mesh['ctx'=32,'tp'=4] {'ctx'}, dimensions={0} | all-to-all | bytes 32768 | tf_op jit(solution)/shard_map/all_to_all | solution.py:83
  236.2 2.0 copy.43
  238.2 0.0 reduce-scatter.4.cloned.1.call-update
  238.2 0.0 all-reduce.5.cloned.1.call-start
  238.2 28.6 %reduce-scatter.4.cloned.1.call-done = f32[1024,1]{1,0:T(8,128)} async-done(((f32[4096,1]{1,0:T(8,128)}), f32[1024,1]{1,0:T(8,128)}) %reduce-scatter.4.cloned.1.call-update) | async-done | bytes 4112
  266.8 1.2 copy.44
  268.0 1.3 multiply_reduce_fusion
  269.3 9.1 %psum.30 = f32[1]{0:T(128)} all-reduce(f32[1]{0:T(128)} %bitcast.9), channel_id=1, replica_groups=mesh['ctx'=32,'tp'=4] {'tp'}, use_global_device_ids=true, to_apply=%region_7.8 | all-reduce | flops 1 | bytes 8 | tf_op jit(solution)/shard_map/psum | solution.py:86
  279.1 0.7 multiply_convert_fusion
  279.8 11.9 %all_gather.18 = bf16[1,4096]{1,0:T(2,128)(2,1)S(1)} all-gather(bf16[1,1024]{1,0:T(2,128)(2,1)S(1)} %multiply_convert_fusion), channel_id=1, replica_groups=mesh['ctx'=32,'tp'=4] {'tp'}, dimensions={1}, use_global_device_ids=true | all-gather | bytes 10240 | tf_op jit(solution)/shard_map/all_gather | solution.py:90
  291.8 24.7 %all-gather.3 = bf16[32,1,4096]{2,1,0:T(2,128)(2,1)S(1)} all-gather(bf16[1,1,4096]{2,1,0:T(2,128)(2,1)S(1)} %bitcast.67), channel_id=1, replica_groups=mesh['ctx'=32,'tp'=4] {'ctx'}, dimensions={0}, use_global_device_ids=true | all-gather | bytes 270336 | tf_op jit(solution)/shard_map/all_gather | solution.py:91
  316.5 0.0 copy-done.2
  316.5 0.5 fusion.16
  317.0 0.0 copy-done
  317.0 0.0 copy-done.1
  317.1 1.7 fusion.13
  318.7 0.0 all-reduce.5.cloned.1.call-update
  318.8 142.4 %all-reduce.5.cloned.1.call-done = f32[32,4096]{1,0:T(8,128)} async-done(((f32[32,4096]{1,0:T(8,128)}), f32[32,4096]{1,0:T(8,128)}) %all-reduce.5.cloned.1.call-update) | async-done | bytes 524304 | tf_op jit(solution)/shard_map/psum | solution.py:96
  461.2 0.0 copy-done.6
  461.2 1.4 add_convert_fusion
  (4 shorter events, 0.1 us)
Async XLA Ops:
  6.5 310.5 %copy-start = (bf16[112,4096]{1,0:T(8,128)(2,1)S(1)}, bf16[112,4096]{1,0:T(8,128)(2,1)}, u32[]{:S(2)}) copy-start(bf16[112,4096]{1,0:T(8,128)(2,1)} %param.23) | copy-start | bytes 2752516
  6.5 214.7 %all-reduce.3.cloned.1.call-start = ((), (), s32[]{:S(2)}) async-start(), calls=%async_computation.2 | async-start | bytes 262144 | tf_op jit(solution)/shard_map/psum | solution.py:61
  32.0 71.9 %copy-start.5 = (bf16[32,2,4,128]{3,2,1,0:T(4,128)(2,1)}, bf16[32,2,4,128]{3,2,1,0:T(4,128)(2,1)S(1)}, u32[]{:S(2)}) copy-start(bf16[32,2,4,128]{3,2,1,0:T(4,128)(2,1)S(1)} %reshape.58) | copy-start | bytes 196612
  38.6 66.5 %copy-start.4 = (f32[32,2,4]{2,1,0:T(2,128)}, f32[32,2,4]{2,1,0:T(2,128)S(1)}, u32[]{:S(2)}) copy-start(f32[32,2,4]{2,1,0:T(2,128)S(1)} %get-tuple-element.10) | copy-start | bytes 3076
  38.6 183.9 %copy-start.3 = (bf16[1024,128]{1,0:T(8,128)(2,1)S(1)}, bf16[1024,128]{1,0:T(8,128)(2,1)}, u32[]{:S(2)}) copy-start(bf16[1024,128]{1,0:T(8,128)(2,1)} %param.19) | copy-start | bytes 786436
  103.9 1.1 copy-start.7
  105.8 210.7 %copy-start.2 = (bf16[4096,112]{0,1:T(8,128)(2,1)S(1)}, bf16[4096,112]{0,1:T(8,128)(2,1)}, u32[]{:S(2)}) copy-start(bf16[4096,112]{0,1:T(8,128)(2,1)} %param.21) | copy-start | bytes 2752516
  105.8 211.3 %copy-start.1 = (bf16[4096,112]{0,1:T(8,128)(2,1)S(1)}, bf16[4096,112]{0,1:T(8,128)(2,1)}, u32[]{:S(2)}) copy-start(bf16[4096,112]{0,1:T(8,128)(2,1)} %param.22) | copy-start | bytes 2752516
  111.2 350.0 %copy-start.6 = (bf16[1,1024]{1,0:T(2,128)(2,1)S(1)}, bf16[1,1024]{1,0:T(2,128)(2,1)}, u32[]{:S(2)}) copy-start(bf16[1,1024]{1,0:T(2,128)(2,1)} %param.12) | copy-start | bytes 6148
  111.3 155.5 %reduce-scatter.4.cloned.1.call-start = ((), (), s32[]{:S(2)}) async-start(), calls=%async_computation.4 | async-start | bytes 2621440
  238.2 223.0 %all-reduce.5.cloned.1.call-start = ((), (), s32[]{:S(2)}) async-start(), calls=%async_computation.3 | async-start | bytes 1048576 | tf_op jit(solution)/shard_map/psum | solution.py:96
Sparse Core Ops, SparseCore 0:
  111.4 96.9 all-reduce.2
  238.3 28.4 reduce-scatter.3
  318.9 142.2 all-reduce.4
where the time goes:
time: 471 us; the launch traced here: 469 us
  blocking collectives  257 us (55%)
  waiting for transfers between devices  171 us (36%)
  matrix products  14.6 us (3%)
  between operations  13.9 us (3%)
  other arithmetic  7.53 us (2%)
    psum x1, waiting for transfers between devices, shards(): summed_all = lax.psum(partial_ffn, ('ctx', 'tp'))  142 us
    psum x1, blocking collectives, shards(): lax.psum((block_den * rescale, block_num * rescale[..., None]), 'ctx')  66.7 us
    pmax x1, blocking collectives, shards(): peak_score = lax.pmax(block_max, 'ctx')  65.2 us
    unnamed x4, waiting for transfers between devices  28.6 us
    all_gather x1, blocking collectives, shards(): lax.all_gather(query, 'ctx', axis=0, tiled=True)  25.1 us
    all_gather x1, blocking collectives, shards(): piece = lax.all_gather(full_rows, 'ctx', axis=0, tiled=True)  24.7 us
    all_gather x1, blocking collectives, shards(): lax.all_gather(new_value, 'ctx', axis=0, tiled=True)  20.5 us
    all_gather x1, blocking collectives, shards(): lax.all_gather(new_key, 'ctx', axis=0, tiled=True)  20.5 us
  transfers between devices with their start and end apart: 3, of which 2 were waited for; matrix products, arithmetic and copies ran while one was open for 0% of the time, Pallas kernels for 0%

commit v1 on v0

v1 whole, which is shorter than its diff:
```python
import math

import jax
import jax.numpy as jnp
from jax import lax
from jax.experimental import pallas as pl
from jax.experimental.pallas import tpu as pltpu
from jax.sharding import Mesh
from jax.sharding import PartitionSpec as P

D = 4096
HD = 128
EPSILON = 1e-05
MASKED = -1e30
F32 = jnp.float32
BF16 = jnp.bfloat16

CHIPS = 16
TP = 4
SEQS = 32
HALF = 16
HEADS = 8
STEP = 4
ROWS = HEADS * HALF
MSG = ROWS + 16

VMEM_LIMIT = 48 * 1024 * 1024


def pack_lse(lse_of_head):
    lane = lax.broadcasted_iota(jnp.int32, (HALF, 128), 1)
    packed = jnp.zeros((HALF, 128), F32)
    for h in range(HEADS):
        value = lse_of_head(h)
        high = value.astype(BF16).astype(F32)
        rest = value - high
        middle = rest.astype(BF16).astype(F32)
        low = rest - middle
        packed = jnp.where(lane == h, high, packed)
        packed = jnp.where(lane == HEADS + h, middle, packed)
        packed = jnp.where(lane == 2 * HEADS + h, low, packed)
    return packed.astype(BF16)


def attend_kernel(
    lengths, gathered, keys, values, own_key, own_value, sent, kept, kept_lse, hidden_part, outs, lses, rows
):
    step = pl.program_id(0)
    chip, core, plane = lax.axis_index("p"), lax.axis_index("k"), lax.axis_index("t")
    ctx_dev = keys.shape[1]
    factor = 1.0 / math.sqrt(HD)
    first = (chip * 2 + core) * ctx_dev
    head = lax.broadcasted_iota(jnp.int32, (HEADS, HD), 0)
    zero = jnp.zeros((HEADS, HD), BF16)
    for i in range(STEP):
        b = step * STEP + i
        j = step * (STEP // 2) + i // 2
        query = gathered[b][:HEADS]
        wide = jnp.concatenate(
            [jnp.where(head < HEADS // 2, query, zero), jnp.where(head >= HEADS // 2, query, zero)], axis=1
        )
        scores = (
            lax.dot_general(wide, keys[i], (((1,), (1,)), ((), ())), preferred_element_type=F32) * factor
        )
        place = first + lax.broadcasted_iota(jnp.int32, scores.shape, 1)
        valid = place < lengths[b]
        top = jnp.max(jnp.where(valid, scores, MASKED), axis=1, keepdims=True)
        weights = jnp.where(valid, jnp.exp(scores - top), 0.0).astype(BF16)
        den = jnp.sum(weights.astype(F32), axis=1, keepdims=True)
        num = jnp.dot(weights, values[i], preferred_element_type=F32)
        num = jnp.where(head < HEADS // 2, num[:, :HD], num[:, HD:])
        some = den > 0.0
        safe = jnp.where(some, den, 1.0)
        lse = jnp.where(some, top + jnp.log(safe), MASKED)
        outs[i % 2, pl.ds(j, HEADS, stride=HALF), :] = num / safe
        lses[i % 2, pl.ds(j, HEADS, stride=HALF), :] = jnp.broadcast_to(lse, (HEADS, HD))

    @pl.when(step == pl.num_programs(0) - 1)
    def _():
        query = gathered[chip * 2 + core][:HEADS].astype(F32)
        key, value = own_key[...].astype(F32), own_value[...].astype(F32)
        key = jnp.where(head < HEADS // 2, key[:, :HD], key[:, HD:])
        value = jnp.where(head < HEADS // 2, value[:, :HD], value[:, HD:])
        own = jnp.sum(query * key, axis=1, keepdims=True) * factor
        place = pl.ds(chip, HEADS, stride=HALF)
        block, block_lse = outs[core, place, :], lses[core, place, :]
        top = jnp.maximum(block_lse, own)
        keep, fresh = jnp.exp(block_lse - top), jnp.exp(own - top)
        total = keep + fresh
        outs[core, place, :] = (block * keep + value * fresh) / total
        lses[core, place, :] = top + jnp.log(total)
        kept[...] = outs[core]
        kept_lse[...] = lses[core]
        other = 1 - core
        sent[:ROWS, :] = outs[other].astype(BF16)
        sent[ROWS:, :] = pack_lse(lambda h: lses[other, h * HALF : (h + 1) * HALF, :])
        rows[...] = gathered[...].reshape(SEQS * 16, HD).astype(F32)
        column = core * 16 + HEADS + (chip % 4) * 2
        mine = plane == chip // 4
        for i in range(2):
            part = rows[pl.ds(column + i, HALF, stride=32), :]
            hidden_part[i] = jnp.where(mine, part, 0.0)


def merge_kernel(kept, kept_lse, came, message):
    packed = came[ROWS:, :].astype(F32)
    merged_lse = []
    for h in range(HEADS):
        place = slice(h * HALF, (h + 1) * HALF)
        mine = kept_lse[place, :]
        theirs = (packed[:, h : h + 1] + packed[:, HEADS + h : HEADS + h + 1]) + packed[
            :, 2 * HEADS + h : 2 * HEADS + h + 1
        ]
        top = jnp.maximum(mine, theirs)
        left, right = jnp.exp(mine - top), jnp.exp(theirs - top)
        total = left + right
        block = (kept[place, :] * left + came[place, :].astype(F32) * right) / total
        message[:, place, :] = jnp.broadcast_to(block.astype(BF16)[None], (CHIPS, HALF, HD))
        merged_lse.append(top + jnp.log(total))
    packed = pack_lse(lambda h: merged_lse[h])
    message[:, ROWS:, :] = jnp.broadcast_to(packed[None], (CHIPS, 16, HD))


def project_kernel(blocks, weight, other_weight, hidden_part, message):
    core = lax.axis_index("k")
    lse = []
    for s in range(CHIPS):
        packed = blocks[s, ROWS:, :].astype(F32)
        lse.append((packed + pltpu.roll(packed, 128 - HEADS, 1)) + pltpu.roll(packed, 128 - 2 * HEADS, 1))
    top = lse[0]
    for s in range(1, CHIPS):
        top = jnp.maximum(top, lse[s])
    share = [jnp.exp(x - top) for x in lse]
    total = share[0]
    for s in range(1, CHIPS):
        total = total + share[s]
    share = [x / total for x in share]
    columns = []
    for h in range(HEADS):
        place = slice(h * HALF, (h + 1) * HALF)
        acc = jnp.zeros((HALF, HD), F32)
        for s in range(CHIPS):
            acc = acc + share[s][:, h : h + 1] * blocks[s, place, :].astype(F32)
        columns.append(acc.astype(BF16))
    attention = jnp.concatenate(columns, axis=1)
    mine = jnp.dot(attention, weight[...], preferred_element_type=F32)
    other = jnp.dot(attention, other_weight[...], preferred_element_type=F32)
    low = jnp.where(core == 0, mine, other) + hidden_part[0]
    high = jnp.where(core == 0, other, mine) + hidden_part[1]
    message[:, :HALF, :] = jnp.broadcast_to(low.astype(BF16)[None], message[:, :HALF, :].shape)
    message[:, HALF:, :] = jnp.broadcast_to(high.astype(BF16)[None], message[:, :HALF, :].shape)


def feed_kernel(
    parts, gain0, gain1, gain2, gain3, gate0, gate1, up0, up1, down0, down1, message, mid_row, mid, gains
):
    chip, plane = lax.axis_index("p"), lax.axis_index("t")
    for i, gain in enumerate((gain0, gain1, gain2, gain3)):
        at = lax.rem(plane + i, TP) * 8
        gains[pl.ds(pl.multiple_of(at, 8), 8), :] = gain[...]
    square = jnp.zeros((HALF, HD), F32)
    for c in range(2 * CHIPS):
        place = slice((c % 2) * HALF, (c % 2 + 1) * HALF)
        piece = parts[(c // 2) * TP, place, :].astype(F32)
        for t in range(1, TP):
            piece = piece + parts[(c // 2) * TP + t, place, :].astype(F32)
        mid[c * HALF : (c + 1) * HALF, :] = piece
        square = square + piece * piece
    scale = lax.rsqrt(jnp.sum(square, axis=1, keepdims=True) / D + EPSILON)
    mid_row[...] = mid[pl.ds(plane * 8 * HALF + chip, 8, stride=HALF), :]
    normed = jnp.concatenate(
        [
            (mid[c * HALF : (c + 1) * HALF, :] * scale * gains[c : c + 1, :]).astype(BF16)
            for c in range(2 * CHIPS)
        ],
        axis=1,
    )

    def hidden_units(gate, up):
        gate_out = jnp.dot(normed, gate[...], preferred_element_type=F32)
        up_out = jnp.dot(normed, up[...], preferred_element_type=F32)
        return (gate_out / (1.0 + jnp.exp(-gate_out)) * up_out).astype(BF16)

    act0, act1 = hidden_units(gate0, up0), hidden_units(gate1, up1)
    wide = 512
    for n in range(D // wide):
        place = slice(n * wide, (n + 1) * wide)
        partial = jnp.dot(act0, down0[:, place], preferred_element_type=F32) + jnp.dot(
            act1, down1[:, place], preferred_element_type=F32
        )
        for i in range(wide // HD):
            c = n * (wide // HD) + i
            message[pl.ds(c, HALF, stride=2 * CHIPS), :] = partial[:, i * HD : (i + 1) * HD]


def sum_kernel(parts, mid_row, out):
    total = parts[0]
    for s in range(1, CHIPS * TP):
        total = total + parts[s]
    total = (mid_row[...] + total).astype(BF16)
    for r in range(8):
        out[:, r * HD : (r + 1) * HD] = total[r : r + 1, :]


def vmem():
    return pl.BlockSpec(memory_space=pltpu.VMEM)


def call(kernel, out_shape, operands, scratch=()):
    return pl.pallas_call(
        kernel,
        out_shape=out_shape,
        in_specs=[vmem()] * len(operands),
        out_specs=jax.tree.map(lambda _: vmem(), out_shape),
        scratch_shapes=list(scratch),
        compiler_params=pltpu.CompilerParams(vmem_limit_bytes=VMEM_LIMIT),
    )(*operands)


def shards(
    hidden_in,
    query,
    new_key,
    new_value,
    cache_keys,
    cache_values,
    lengths,
    out_weight,
    norm_gain,
    w_gate,
    w_up,
    w_down,
):
    def other_core(x):
        return lax.ppermute(x, "k", [(0, 1), (1, 0)])

    gain = norm_gain.reshape(8, HD)
    gains = [gain] + [lax.ppermute(gain, "t", [((i + n) % TP, i) for i in range(TP)]) for n in range(1, TP)]
    other_out_weight, other_gate, other_up, other_down = map(other_core, (out_weight, w_gate, w_up, w_down))

    own = jnp.concatenate([query.reshape(HEADS, HD), hidden_in.reshape(8, HD)], axis=0)
    gathered = lax.all_to_all(jnp.broadcast_to(own[None], (SEQS, 16, HD)), ("p", "k"), 0, 0, tiled=True)

    ctx_dev, width = cache_keys.shape[1], cache_keys.shape[2]
    sent, kept, kept_lse, hidden_part = pl.pallas_call(
        attend_kernel,
        out_shape=(
            jax.ShapeDtypeStruct((MSG, HD), BF16),
            jax.ShapeDtypeStruct((ROWS, HD), F32),
            jax.ShapeDtypeStruct((ROWS, HD), F32),
            jax.ShapeDtypeStruct((2, HALF, HD), F32),
        ),
        grid=(SEQS // STEP,),
        in_specs=[
            pl.BlockSpec(memory_space=pltpu.SMEM),
            vmem(),
            pl.BlockSpec((STEP, ctx_dev, width), lambda g: (g, 0, 0)),
            pl.BlockSpec((STEP, ctx_dev, width), lambda g: (g, 0, 0)),
            vmem(),
            vmem(),
        ],
        out_specs=(vmem(), vmem(), vmem(), vmem()),
        scratch_shapes=[
            pltpu.VMEM((2, ROWS, HD), F32),
            pltpu.VMEM((2, ROWS, HD), F32),
            pltpu.VMEM((SEQS * 16, HD), F32),
        ],
        compiler_params=pltpu.CompilerParams(vmem_limit_bytes=VMEM_LIMIT),
    )(lengths, gathered, cache_keys, cache_values, new_key, new_value)

    came = other_core(sent)
    blocks = call(merge_kernel, jax.ShapeDtypeStruct((CHIPS, MSG, HD), BF16), (kept, kept_lse, came))
    blocks = lax.all_to_all(blocks, "p", 0, 0, tiled=True)
    columns = call(
        project_kernel,
        jax.ShapeDtypeStruct((CHIPS * TP, 2 * HALF, HD), BF16),
        (blocks, out_weight, other_out_weight, hidden_part),
    )
    columns = lax.all_to_all(columns, ("p", "t"), 0, 0, tiled=True)
    partial, mid_row = call(
        feed_kernel,
        (jax.ShapeDtypeStruct((CHIPS * TP * 8, HD), F32), jax.ShapeDtypeStruct((8, HD), F32)),
        (columns, *gains, w_gate, other_gate, w_up, other_up, w_down, other_down),
        (pltpu.VMEM((2 * CHIPS * HALF, HD), F32), pltpu.VMEM((2 * CHIPS, HD), F32)),
    )
    partial = lax.all_to_all(partial.reshape(CHIPS * TP, 8, HD), ("p", "t"), 0, 0, tiled=True)
    return call(sum_kernel, jax.ShapeDtypeStruct((1, 8 * HD), BF16), (partial, mid_row))


def solution(mesh):
    cut = Mesh(mesh.devices.reshape(CHIPS, 2, TP), ("p", "k", "t"))
    ctx, tp = ("p", "k"), "t"
    return jax.shard_map(
        shards,
        mesh=cut,
        in_specs=(
            P(ctx, tp),
            P(ctx, tp),
            P(ctx, tp),
            P(ctx, tp),
            P(None, ctx, tp),
            P(None, ctx, tp),
            P(),
            P(tp, ctx),
            P(tp),
            P(None, ("p", "k", "t")),
            P(None, ("p", "k", "t")),
            P(("p", "k", "t"), None),
        ),
        out_specs=P(ctx, tp),
        check_vma=False,
    )
```

time: 471 us -> 94.3 us (0.20)
  blocking collectives: 257 us -> 32.2 us
  waiting for transfers between devices: 171 us -> 13.8 us
  Pallas kernels: 0 us -> 19.5 us
  starting transfers between devices: 0.09 us -> 18.3 us
  matrix products: 14.6 us -> 0 us
  between operations: 13.9 us -> 0.12 us
  other arithmetic: 7.53 us -> 1.42 us
    psum x2 -> x0, waiting for transfers between devices: 142 us -> none  [the longest x1 142 us: shards(): summed_all = lax.psum(partial_ffn, ('ctx', 'tp'))]
    all_gather x5 -> x0, blocking collectives: 103 us -> none  [the longest x1 25.1 us: shards(): lax.all_gather(query, 'ctx', axis=0, tiled=True)]
    psum x2 -> x0, blocking collectives: 75.8 us -> none  [the longest x1 66.7 us: shards(): lax.psum((block_den * rescale, block_num * rescale[..., None]), 'ctx')]
    pmax x1 -> x0, blocking collectives: 65.2 us -> none  [shards(): peak_score = lax.pmax(block_max, 'ctx')]
    unnamed x4 -> x0, waiting for transfers between devices: 28.6 us -> none
    pallas_call x0 -> x5, Pallas kernels: none -> 19.5 us  [the longest x1 13.2 us: shards(): pl.pallas_call(attend_kernel, out_shape=(jax.ShapeDtypeStruct((MSG, HD),...]
    all_to_all x1 -> x2, blocking collectives: 13.5 us -> 32.2 us  [the longest x1 17.2 us: shards(): lax.all_to_all(partial.reshape(CHIPS * TP, 8, HD), ('p', 't'), 0, 0, tile...]
    dot_general x6 -> x0, matrix products: 14.6 us -> none  [the longest x1 5.76 us: shards(): jnp.einsum('bkgd,btkd->bkgt', queries, keys_view, preferred_element_type=...]
  transfers between devices with their start and end apart: 3 -> 10, of which waited for: 2 -> 4; matrix products, arithmetic and copies ran while one was open for 0% -> 7% of each run, Pallas kernels for 0% -> 2%
where the time goes in v1:
time: 94.3 us; the launch traced here: 93.6 us
  blocking collectives  32.2 us (34%)
  Pallas kernels  19.5 us (21%)
  starting transfers between devices  18.3 us (19%)
  waiting for transfers between devices  13.8 us (15%)
  local copies, waits for them, and re-layouts  8.16 us (9%)
  other arithmetic  1.42 us (2%)
    all_to_all x1, blocking collectives, shards(): lax.all_to_all(partial.reshape(CHIPS * TP, 8, HD), ('p', 't'), 0, 0, tile...  17.2 us
    all_to_all x1, blocking collectives, shards(): lax.all_to_all(jnp.broadcast_to(own[None], (SEQS, 16, HD)), ('p', 'k'), 0...  15 us
    pallas_call x1, Pallas kernels, shards(): pl.pallas_call(attend_kernel, out_shape=(jax.ShapeDtypeStruct((MSG, HD),...  13.2 us
    all_to_all x1, waiting for transfers between devices, shards(): blocks = lax.all_to_all(blocks, 'p', 0, 0, tiled=True)  9.49 us
    all_to_all x1, starting transfers between devices, shards(): columns = lax.all_to_all(columns, ('p', 't'), 0, 0, tiled=True)  7.73 us
    pallas_call x4, Pallas kernels, call(): pl.pallas_call(kernel, out_shape=out_shape, in_specs=[vmem()] * len(opera...  6.33 us
    ppermute x3, starting transfers between devices, shards(): lax.ppermute(gain, 't', [((i + n) % TP, i) for i in range(TP)])  5.7 us
    unnamed x14, local copies, waits for them, and re-layouts  4.28 us
  transfers between devices with their start and end apart: 10, of which 4 were waited for; matrix products, arithmetic and copies ran while one was open for 7% of the time, Pallas kernels for 2%

profile of v1, /device:TPU:0, one launch (start us, length us, event | category | flops | bytes accessed | tf_op | source)
XLA Modules:
  0.0 93.6 jit_solution(5101969981552424572)
XLA Ops:
  0.0 0.7 reduce.1
  0.7 0.7 reduce
  1.5 15.0 %all_to_all.20.gathered = bf16[32,16,128]{2,1,0:T(8,128)(2,1)S(1)} all-to-all(bf16[32,16,128]{2,1,0:T(8,128)(2,1)S(1)} %broadcast_in_dim.2), channel_id=1, replica_groups=mesh['p'=16,'k'=2,'t'=4] {'p','k'}, dimensions={0} | all-to-all | bytes 262144 | tf_op jit(solution)/shard_map/all_to_all | solution.py:242
  16.5 0.0 copy-start.2
  16.5 0.7 copy-done.2
  17.1 0.0 copy-start.3
  17.1 0.7 copy-done.3
  17.8 0.0 copy-start.4
  17.8 0.7 copy-done.4
  18.5 0.0 copy-start.5
  18.5 0.0 copy-start
  18.5 0.0 copy-start.1
  18.5 13.2 %shard_map.118 = (bf16[144,128]{1,0:T(8,128)(2,1)S(1)}, f32[128,128]{1,0:T(8,128)S(1)}, f32[128,128]{1,0:T(8,128)S(1)}, f32[2,16,128]{2,1,0:T(8,128)S(1)}) custom-call(s32[32]{0:T(128)S(1)} %copy-done.4, bf16[32,16,128]{2,1,0:T(8,128)(2,1)S(1)} %all_to_all.20.gathered, bf16[32,512,256]{2,1,0:T(8,128)(2,1)} %keys.1, bf16[32,512,256]{2,1,0:T(8,128)(2,1)} %values.1, ...), custom_call_target="tpu_custom_call" | custom-call | tf_op jit(solution)/shard_map/pallas_call | solution.py:245
  31.7 0.2 collective-permute-start
  31.9 1.1 %collective-permute-done.came = bf16[144,128]{1,0:T(8,128)(2,1)S(1)} collective-permute-done((bf16[144,128]{1,0:T(8,128)(2,1)S(1)}, bf16[144,128]{1,0:T(8,128)(2,1)S(1)}, u32[]{:S(2)}, u32[]{:S(2)}) %collective-permute-start) | collective-permute-done | bytes 36896 | tf_op jit(solution)/shard_map/ppermute | solution.py:235
  33.0 1.0 %shard_map.119 = bf16[16,144,128]{2,1,0:T(8,128)(2,1)} custom-call(f32[128,128]{1,0:T(8,128)S(1)} %get-tuple-element.11.kept, f32[128,128]{1,0:T(8,128)S(1)} %get-tuple-element.12.kept_lse, bf16[144,128]{1,0:T(8,128)(2,1)S(1)} %collective-permute-done.came), custom_call_target="tpu_custom_call" | custom-call | tf_op jit(solution)/shard_map/pallas_call | solution.py:210
  34.0 3.6 %all-to-all-start.1 = ((bf16[16,144,128]{2,1,0:T(8,128)(2,1)}), bf16[16,144,128]{2,1,0:T(8,128)(2,1)S(1)}, u32[]{:S(2)}, u32[]{:S(2)}) async-start(bf16[16,144,128]{2,1,0:T(8,128)(2,1)} %shard_map.119), calls=%async_computation.1 | async-start | bytes 1179648 | tf_op jit(solution)/shard_map/all_to_all | solution.py:273
  37.6 0.0 copy-done.5
  37.6 0.2 collective-permute-start.5
  37.8 0.3 collective-permute-start.6
  38.2 0.2 collective-permute-start.7
  38.4 0.0 copy-done
  38.4 0.3 collective-permute-start.1
  38.7 2.2 %collective-permute-done.1.other_weight = bf16[1024,128]{1,0:T(8,128)(2,1)S(1)} collective-permute-done((bf16[1024,128]{1,0:T(8,128)(2,1)S(1)}, bf16[1024,128]{1,0:T(8,128)(2,1)S(1)}, u32[]{:S(2)}, u32[]{:S(2)}) %collective-permute-start.1) | collective-permute-done | bytes 262176 | tf_op jit(solution)/shard_map/ppermute | solution.py:235
  40.9 9.5 %all-to-all-done.1.blocks = bf16[16,144,128]{2,1,0:T(8,128)(2,1)S(1)} async-done(((bf16[16,144,128]{2,1,0:T(8,128)(2,1)}), bf16[16,144,128]{2,1,0:T(8,128)(2,1)S(1)}, u32[]{:S(2)}, u32[]{:S(2)}) %all-to-all-start.1) | async-done | bytes 589856 | tf_op jit(solution)/shard_map/all_to_all | solution.py:273
  50.4 1.5 %shard_map.120 = bf16[64,32,128]{2,1,0:T(8,128)(2,1)} custom-call(bf16[16,144,128]{2,1,0:T(8,128)(2,1)S(1)} %all-to-all-done.1.blocks, bf16[1024,128]{1,0:T(8,128)(2,1)S(1)} %copy-done, bf16[1024,128]{1,0:T(8,128)(2,1)S(1)} %collective-permute-done.1.other_weight, f32[2,16,128]{2,1,0:T(8,128)S(1)} %get-tuple-element.14.hidden_part), custom_call_target="tpu_custom_call" | custom-call | tf_op jit(solution)/shard_map/pallas_call | solution.py:210
  51.9 7.7 %all-to-all-start.2 = ((bf16[64,32,128]{2,1,0:T(8,128)(2,1)}), bf16[64,32,128]{2,1,0:T(8,128)(2,1)}, u32[]{:S(2)}, u32[]{:S(2)}) async-start(bf16[64,32,128]{2,1,0:T(8,128)(2,1)} %shard_map.120), calls=%async_computation.2 | async-start | bytes 1048576 | tf_op jit(solution)/shard_map/all_to_all | solution.py:279
  59.7 0.0 copy-done.1
  59.7 1.6 %collective-permute-start.4 = (f32[8,128]{1,0:T(8,128)S(1)}, f32[8,128]{1,0:T(8,128)S(1)}, u32[]{:S(2)}, u32[]{:S(2)}) collective-permute-start(f32[8,128]{1,0:T(8,128)S(1)} %bitcast.5), channel_id=1, source_target_pairs={{3,0},{0,1},{1,2},{2,3},{7,4},{4,5},{5,6},{6,7},{11,8},{8,9},{9,10... | collective-permute-start | bytes 12296 | tf_op jit(solution)/shard_map/ppermute | solution.py:238
  61.3 2.7 %collective-permute-start.3 = (f32[8,128]{1,0:T(8,128)S(1)}, f32[8,128]{1,0:T(8,128)S(1)}, u32[]{:S(2)}, u32[]{:S(2)}) collective-permute-start(f32[8,128]{1,0:T(8,128)S(1)} %bitcast.6), channel_id=1, source_target_pairs={{2,0},{3,1},{0,2},{1,3},{6,4},{7,5},{4,6},{5,7},{10,8},{11,9},{8,1... | collective-permute-start | bytes 12296 | tf_op jit(solution)/shard_map/ppermute | solution.py:238
  63.9 0.0 collective-permute-done.5
  63.9 1.5 %collective-permute-start.2 = (f32[8,128]{1,0:T(8,128)S(1)}, f32[8,128]{1,0:T(8,128)S(1)}, u32[]{:S(2)}, u32[]{:S(2)}) collective-permute-start(f32[8,128]{1,0:T(8,128)S(1)} %bitcast.7), channel_id=1, source_target_pairs={{1,0},{2,1},{3,2},{0,3},{5,4},{6,5},{7,6},{4,7},{9,8},{10,9},{11,1... | collective-permute-start | bytes 12296 | tf_op jit(solution)/shard_map/ppermute | solution.py:238
  65.4 0.7 copy.17.gate0
  66.1 1.6 %copy.19.up0 = bf16[4096,112]{1,0:T(8,128)(2,1)S(1)} copy(bf16[4096,112]{0,1:T(8,128)(2,1)} %param.22) | data formatting | bytes 1835008 | tf_op args[10]
  67.7 1.6 %copy.18.gate1 = bf16[4096,112]{1,0:T(8,128)(2,1)S(1)} copy(bf16[4096,112]{0,1:T(8,128)(2,1)} %collective-permute-done.5) | data formatting | bytes 1835008 | tf_op jit(solution)/shard_map/ppermute | solution.py:235
  69.3 0.0 collective-permute-done.6
  69.3 2.3 %copy.20.up1 = bf16[4096,112]{1,0:T(8,128)(2,1)} copy(bf16[4096,112]{0,1:T(8,128)(2,1)} %collective-permute-done.6) | data formatting | bytes 1835008 | tf_op jit(solution)/shard_map/ppermute | solution.py:235
  71.5 0.0 collective-permute-done.4.gain3
  71.6 0.0 collective-permute-done.3.gain2
  71.6 0.0 collective-permute-done.2.gain1
  71.6 0.0 collective-permute-done.7.down1
  71.6 1.0 %all-to-all-done.2.parts = bf16[64,32,128]{2,1,0:T(8,128)(2,1)} async-done(((bf16[64,32,128]{2,1,0:T(8,128)(2,1)}), bf16[64,32,128]{2,1,0:T(8,128)(2,1)}, u32[]{:S(2)}, u32[]{:S(2)}) %all-to-all-start.2) | async-done | bytes 524320 | tf_op jit(solution)/shard_map/all_to_all | solution.py:279
  72.5 3.1 %shard_map.121 = (f32[512,128]{1,0:T(8,128)S(1)}, f32[8,128]{1,0:T(8,128)S(1)}) custom-call(bf16[64,32,128]{2,1,0:T(8,128)(2,1)} %all-to-all-done.2.parts, f32[8,128]{1,0:T(8,128)S(1)} %bitcast.8, f32[8,128]{1,0:T(8,128)S(1)} %collective-permute-done.2.gain1, f32[8,128]{1,0:T(8,128)S(1)} %collective-permute-done.3.gain2, ...), custom_call_target="tpu_custom_call" | custom-call | tf_op jit(solution)/shard_map/pallas_call | solution.py:210
  75.7 17.2 %all_to_all.21.parts = f32[64,8,128]{2,1,0:T(8,128)S(1)} all-to-all(f32[64,8,128]{2,1,0:T(8,128)S(1)} %bitcast.4), channel_id=1, replica_groups=mesh['p'=16,'k'=2,'t'=4] {'p','t'}, dimensions={0} | all-to-all | bytes 524288 | tf_op jit(solution)/shard_map/all_to_all | solution.py:286
  92.9 0.7 shard_map.122
  (2 shorter events, 0.0 us)
Async XLA Ops:
  16.5 0.7 copy-start.2
  17.1 0.7 copy-start.3
  17.8 0.7 copy-start.4
  18.5 19.1 %copy-start.5 = (bf16[4096,112]{0,1:T(8,128)(2,1)S(1)}, bf16[4096,112]{0,1:T(8,128)(2,1)}, u32[]{:S(2)}) copy-start(bf16[4096,112]{0,1:T(8,128)(2,1)} %param.21) | copy-start | bytes 2752516
  18.5 19.9 %copy-start = (bf16[1024,128]{1,0:T(8,128)(2,1)S(1)}, bf16[1024,128]{1,0:T(8,128)(2,1)}, u32[]{:S(2)}) copy-start(bf16[1024,128]{1,0:T(8,128)(2,1)} %weight.1) | copy-start | bytes 786436
  18.5 41.2 %copy-start.1 = (f32[1024]{0:T(1024)S(1)}, f32[1024]{0:T(1024)}, u32[]{:S(2)}) copy-start(f32[1024]{0:T(1024)} %param.20) | copy-start | bytes 12292
  31.7 1.3 %collective-permute-start = (bf16[144,128]{1,0:T(8,128)(2,1)S(1)}, bf16[144,128]{1,0:T(8,128)(2,1)S(1)}, u32[]{:S(2)}, u32[]{:S(2)}) collective-permute-start(bf16[144,128]{1,0:T(8,128)(2,1)S(1)} %get-tuple-element.13), channel_id=1, source_target_pairs={{0,4},{4,0},{1,5},{5,1},{2,6},{6,2},{3,7},{7,3},{8,12},{12,8},{9,1... | collective-permute-start | bytes 110600 | tf_op jit(solution)/shard_map/ppermute | solution.py:235
  34.0 16.4 %all-to-all-start.1 = ((bf16[16,144,128]{2,1,0:T(8,128)(2,1)}), bf16[16,144,128]{2,1,0:T(8,128)(2,1)S(1)}, u32[]{:S(2)}, u32[]{:S(2)}) async-start(bf16[16,144,128]{2,1,0:T(8,128)(2,1)} %shard_map.119), calls=%async_computation.1 | async-start | bytes 1179648 | tf_op jit(solution)/shard_map/all_to_all | solution.py:273
  37.6 26.3 %collective-permute-start.5 = (bf16[4096,112]{0,1:T(8,128)(2,1)S(1)}, bf16[4096,112]{0,1:T(8,128)(2,1)}, u32[]{:S(2)}, u32[]{:S(2)}) collective-permute-start(bf16[4096,112]{0,1:T(8,128)(2,1)S(1)} %copy-done.5), channel_id=1, source_target_pairs={{0,4},{4,0},{1,5},{5,1},{2,6},{6,2},{3,7},{7,3},{8,12},{12,8},{9,1... | collective-permute-start | bytes 2752520 | tf_op jit(solution)/shard_map/ppermute | solution.py:235
  37.8 31.4 %collective-permute-start.6 = (bf16[4096,112]{0,1:T(8,128)(2,1)}, bf16[4096,112]{0,1:T(8,128)(2,1)}, u32[]{:S(2)}, u32[]{:S(2)}) collective-permute-start(bf16[4096,112]{0,1:T(8,128)(2,1)} %param.22), channel_id=1, source_target_pairs={{0,4},{4,0},{1,5},{5,1},{2,6},{6,2},{3,7},{7,3},{8,12},{12,8},{9,1... | collective-permute-start | bytes 2752520 | tf_op jit(solution)/shard_map/ppermute | solution.py:235
  38.2 33.4 %collective-permute-start.7 = (bf16[112,4096]{1,0:T(8,128)(2,1)}, bf16[112,4096]{1,0:T(8,128)(2,1)}, u32[]{:S(2)}, u32[]{:S(2)}) collective-permute-start(bf16[112,4096]{1,0:T(8,128)(2,1)} %down0.1), channel_id=1, source_target_pairs={{0,4},{4,0},{1,5},{5,1},{2,6},{6,2},{3,7},{7,3},{8,12},{12,8},{9,1... | collective-permute-start | bytes 2752520 | tf_op jit(solution)/shard_map/ppermute | solution.py:235
  38.4 2.5 %collective-permute-start.1 = (bf16[1024,128]{1,0:T(8,128)(2,1)S(1)}, bf16[1024,128]{1,0:T(8,128)(2,1)S(1)}, u32[]{:S(2)}, u32[]{:S(2)}) collective-permute-start(bf16[1024,128]{1,0:T(8,128)(2,1)S(1)} %copy-done), channel_id=1, source_target_pairs={{0,4},{4,0},{1,5},{5,1},{2,6},{6,2},{3,7},{7,3},{8,12},{12,8},{9,1... | collective-permute-start | bytes 786440 | tf_op jit(solution)/shard_map/ppermute | solution.py:235
  51.9 20.6 %all-to-all-start.2 = ((bf16[64,32,128]{2,1,0:T(8,128)(2,1)}), bf16[64,32,128]{2,1,0:T(8,128)(2,1)}, u32[]{:S(2)}, u32[]{:S(2)}) async-start(bf16[64,32,128]{2,1,0:T(8,128)(2,1)} %shard_map.120), calls=%async_computation.2 | async-start | bytes 1048576 | tf_op jit(solution)/shard_map/all_to_all | solution.py:279
  59.7 11.9 %collective-permute-start.4 = (f32[8,128]{1,0:T(8,128)S(1)}, f32[8,128]{1,0:T(8,128)S(1)}, u32[]{:S(2)}, u32[]{:S(2)}) collective-permute-start(f32[8,128]{1,0:T(8,128)S(1)} %bitcast.5), channel_id=1, source_target_pairs={{3,0},{0,1},{1,2},{2,3},{7,4},{4,5},{5,6},{6,7},{11,8},{8,9},{9,10... | collective-permute-start | bytes 12296 | tf_op jit(solution)/shard_map/ppermute | solution.py:238
  61.3 10.3 %collective-permute-start.3 = (f32[8,128]{1,0:T(8,128)S(1)}, f32[8,128]{1,0:T(8,128)S(1)}, u32[]{:S(2)}, u32[]{:S(2)}) collective-permute-start(f32[8,128]{1,0:T(8,128)S(1)} %bitcast.6), channel_id=1, source_target_pairs={{2,0},{3,1},{0,2},{1,3},{6,4},{7,5},{4,6},{5,7},{10,8},{11,9},{8,1... | collective-permute-start | bytes 12296 | tf_op jit(solution)/shard_map/ppermute | solution.py:238
  63.9 7.6 %collective-permute-start.2 = (f32[8,128]{1,0:T(8,128)S(1)}, f32[8,128]{1,0:T(8,128)S(1)}, u32[]{:S(2)}, u32[]{:S(2)}) collective-permute-start(f32[8,128]{1,0:T(8,128)S(1)} %bitcast.7), channel_id=1, source_target_pairs={{1,0},{2,1},{3,2},{0,3},{5,4},{6,5},{7,6},{4,7},{9,8},{10,9},{11,1... | collective-permute-start | bytes 12296 | tf_op jit(solution)/shard_map/ppermute | solution.py:238

commit v2 on v1

v2 whole, which is shorter than its diff:
```python
import functools
import math

import jax
import jax.numpy as jnp
from jax import lax
from jax.experimental import pallas as pl
from jax.experimental.pallas import tpu as pltpu
from jax.sharding import Mesh
from jax.sharding import PartitionSpec as P

D = 4096
HD = 128
EPSILON = 1e-05
MASKED = -1e30
F32 = jnp.float32
BF16 = jnp.bfloat16

CHIPS = 16
TP = 4
SEQS = 32
HALF = 16
HEADS = 8
GROUPS = (6, 8, 8, 6, 4)
ROWS = HEADS * HALF
MSG = ROWS + 16

SMALL = 8 * 1024 * 1024
LARGE = 24 * 1024 * 1024


def pack_lse(lse_of_head):
    lane = lax.broadcasted_iota(jnp.int32, (HALF, 128), 1)
    packed = jnp.zeros((HALF, 128), F32)
    for h in range(HEADS):
        for i, part in enumerate(addends(lse_of_head(h))):
            packed = jnp.where(lane == i * HEADS + h, part, packed)
    return packed.astype(BF16)


def addends(x):
    high = x.astype(BF16).astype(F32)
    middle = (x - high).astype(BF16).astype(F32)
    return high, middle, x - high - middle


def copy_in(sources, targets, arrived):
    copies = [pltpu.make_async_copy(a, b, arrived.at[i]) for i, (a, b) in enumerate(zip(sources, targets))]
    for copy in copies:
        copy.start()
    return copies


def start_kernel(*refs):
    sources, (message, own, limits), landed, arrived = refs[:5], refs[5:8], refs[8:13], refs[13]
    for copy in copy_in(sources, landed, arrived):
        copy.wait()
    query, hidden, own_key, own_value, lengths = landed

    def rows(x):
        x = x[...].astype(F32)
        return jnp.concatenate([x[:, r * HD : (r + 1) * HD] for r in range(8)], axis=0)

    def heads(x):
        x = x[...].astype(F32)
        return jnp.concatenate([x[:, (h // 4) * HD : (h // 4 + 1) * HD] for h in range(HEADS)], axis=0)

    queries = rows(query)
    both = jnp.concatenate([queries, rows(hidden)], axis=0).astype(BF16)
    message[...] = jnp.broadcast_to(both[None], message.shape)
    score = jnp.sum(queries * heads(own_key), axis=1, keepdims=True) * (1.0 / math.sqrt(HD))
    own[0] = jnp.broadcast_to(score, (HEADS, HD))
    own[1] = heads(own_value)
    for b in range(SEQS):
        limits[b : b + 1, :] = jnp.full((1, HD), lengths[b], jnp.int32)


def first_kernel(keys, values, first_keys, first_values, arrived):
    count = first_keys.shape[0]
    for copy in copy_in((keys.at[:count], values.at[:count]), (first_keys, first_values), arrived):
        copy.wait()


def attend_kernel(
    limits,
    gathered,
    own,
    first_keys,
    first_values,
    cache_keys,
    cache_values,
    sent,
    kept,
    kept_lse,
    hidden_part,
    later_keys,
    later_values,
    outs,
    lses,
    rows,
    arrived,
):
    chip, core, plane = lax.axis_index("p"), lax.axis_index("k"), lax.axis_index("t")
    first, ctx_dev = first_keys.shape[:2]
    factor = 1.0 / math.sqrt(HD)
    copies, at = [()], first
    for n, group in enumerate(GROUPS[1:]):
        source, target = pl.ds(at, group), pl.ds(at - first, group)
        copies.append(
            copy_in(
                (cache_keys.at[source], cache_values.at[source]),
                (later_keys.at[target], later_values.at[target]),
                arrived.at[n],
            )
        )
        at += group

    def block(b, early, later):
        return early[b] if b < first else later[b - first]

    head = lax.broadcasted_iota(jnp.int32, (HEADS, HD), 0)
    zero = jnp.zeros((HEADS, HD), BF16)
    places = (chip * 2 + core) * ctx_dev + lax.broadcasted_iota(jnp.int32, (HEADS, ctx_dev), 1)

    def score(b):
        query = gathered[b][:HEADS]
        wide = jnp.concatenate(
            [jnp.where(head < HEADS // 2, query, zero), jnp.where(head >= HEADS // 2, query, zero)], axis=1
        )
        return lax.dot_general(wide, block(b, first_keys, later_keys), (((1,), (1,)), ((), ())), preferred_element_type=F32) * factor

    def soften(b, scores):
        limit = limits[b : b + 1, :]
        valid = places < jnp.concatenate([limit] * (ctx_dev // HD), axis=1)
        top = jnp.max(jnp.where(valid, scores, MASKED), axis=1, keepdims=True)
        weights = jnp.where(valid, jnp.exp(scores - top), 0.0).astype(BF16)
        return top, weights, jnp.sum(weights.astype(F32), axis=1, keepdims=True)

    def collect(b, top, weights, den):
        num = jnp.dot(weights, block(b, first_values, later_values), preferred_element_type=F32)
        num = jnp.where(head < HEADS // 2, num[:, :HD], num[:, HD:])
        some = den > 0.0
        safe = jnp.where(some, den, 1.0)
        return num / safe, jnp.where(some, top + jnp.log(safe), MASKED)

    at = 0
    for group, pair in zip(GROUPS, copies):
        for copy in pair:
            copy.wait()
        sequences = range(at, at + group)
        at += group
        scores = [score(b) for b in sequences]
        softened = [soften(b, x) for b, x in zip(sequences, scores)]
        collected = [collect(b, *x) for b, x in zip(sequences, softened)]
        for b, (out, lse) in zip(sequences, collected):
            outs[b % 2, pl.ds(b // 2, HEADS, stride=HALF), :] = out
            lses[b % 2, pl.ds(b // 2, HEADS, stride=HALF), :] = jnp.broadcast_to(lse, (HEADS, HD))

    fresh_score, value = own[0], own[1]
    place = pl.ds(chip, HEADS, stride=HALF)
    cached, block_lse = outs[core, place, :], lses[core, place, :]
    top = jnp.maximum(block_lse, fresh_score)
    keep, fresh = jnp.exp(block_lse - top), jnp.exp(fresh_score - top)
    total = keep + fresh
    outs[core, place, :] = (cached * keep + value * fresh) / total
    lses[core, place, :] = top + jnp.log(total)
    kept[...] = outs[core]
    kept_lse[...] = lses[core]
    other = 1 - core
    sent[:ROWS, :] = outs[other].astype(BF16)
    sent[ROWS:, :] = pack_lse(lambda h: lses[other, h * HALF : (h + 1) * HALF, :])
    rows[...] = gathered[...].reshape(SEQS * 16, HD).astype(F32)
    column = core * 16 + HEADS + (chip % 4) * 2
    for i in range(2):
        part = rows[pl.ds(column + i, HALF, stride=32), :]
        hidden_part[i] = jnp.where(plane == chip // 4, part, 0.0)


def merge_kernel(kept, kept_lse, came, gain, message, gain_out):
    gain_out[...] = gain[...]
    packed = came[ROWS:, :].astype(F32)
    merged_lse = []
    for h in range(HEADS):
        place = slice(h * HALF, (h + 1) * HALF)
        mine = kept_lse[place, :]
        theirs = (packed[:, h : h + 1] + packed[:, HEADS + h : HEADS + h + 1]) + packed[
            :, 2 * HEADS + h : 2 * HEADS + h + 1
        ]
        top = jnp.maximum(mine, theirs)
        left, right = jnp.exp(mine - top), jnp.exp(theirs - top)
        total = left + right
        block = (kept[place, :] * left + came[place, :].astype(F32) * right) / total
        message[:, place, :] = jnp.broadcast_to(block.astype(BF16)[None], (CHIPS, HALF, HD))
        merged_lse.append(top + jnp.log(total))
    packed = pack_lse(lambda h: merged_lse[h])
    message[:, ROWS:, :] = jnp.broadcast_to(packed[None], (CHIPS, 16, HD))


def project_kernel(blocks, hidden_part, gain0, gain1, gain2, gain3, *refs):
    sources, message, gains, landed, arrived = refs[:8], refs[8], refs[9], refs[10:18], refs[18]
    copies = copy_in(sources, landed, arrived)
    weight, other_weight = landed[6:]
    core, plane = lax.axis_index("k"), lax.axis_index("t")
    for i, gain in enumerate((gain0, gain1, gain2, gain3)):
        at = pl.multiple_of(lax.rem(plane + i, TP) * 8, 8)
        gains[pl.ds(at, 8), :] = gain[...]
    lse = []
    for s in range(CHIPS):
        packed = blocks[s, ROWS:, :].astype(F32)
        lse.append((packed + pltpu.roll(packed, 128 - HEADS, 1)) + pltpu.roll(packed, 128 - 2 * HEADS, 1))
    top = lse[0]
    for s in range(1, CHIPS):
        top = jnp.maximum(top, lse[s])
    share = [jnp.exp(x - top) for x in lse]
    total = share[0]
    for s in range(1, CHIPS):
        total = total + share[s]
    share = [x / total for x in share]
    columns = []
    for h in range(HEADS):
        place = slice(h * HALF, (h + 1) * HALF)
        acc = jnp.zeros((HALF, HD), F32)
        for s in range(CHIPS):
            acc = acc + share[s][:, h : h + 1] * blocks[s, place, :].astype(F32)
        columns.append(acc.astype(BF16))
    attention = jnp.concatenate(columns, axis=1)
    for copy in copies:
        copy.wait()
    mine = jnp.dot(attention, weight[...], preferred_element_type=F32)
    other = jnp.dot(attention, other_weight[...], preferred_element_type=F32)
    low, high = jnp.where(core == 0, mine, other), jnp.where(core == 0, other, mine)
    for i, rows in enumerate((low, high)):
        rows = (rows + hidden_part[i]).astype(BF16)
        message[:, i * HALF : (i + 1) * HALF, :] = jnp.broadcast_to(rows[None], (CHIPS * TP, HALF, HD))


def feed_kernel(parts, gains, gate0, up0, gate1, up1, down0, down1, message, mid_row, mid):
    chip, plane = lax.axis_index("p"), lax.axis_index("t")
    square = jnp.zeros((HALF, HD), F32)
    for c in range(2 * CHIPS):
        place = slice((c % 2) * HALF, (c % 2 + 1) * HALF)
        piece = parts[(c // 2) * TP, place, :].astype(F32)
        for t in range(1, TP):
            piece = piece + parts[(c // 2) * TP + t, place, :].astype(F32)
        mid[c * HALF : (c + 1) * HALF, :] = piece
        square = square + piece * piece
    scale = lax.rsqrt(jnp.sum(square, axis=1, keepdims=True) / D + EPSILON)
    mid_row[...] = mid[pl.ds(plane * 8 * HALF + chip, 8, stride=HALF), :]

    def normed_columns(c):
        return (mid[c * HALF : (c + 1) * HALF, :] * scale * gains[c : c + 1, :]).astype(BF16)

    normed = jnp.concatenate([normed_columns(c) for c in range(2 * CHIPS)], axis=1)

    def hidden_units(gate, up):
        over = (((1,), (1,)), ((), ()))
        gate_out = lax.dot_general(normed, gate[...], over, preferred_element_type=F32)
        up_out = lax.dot_general(normed, up[...], over, preferred_element_type=F32)
        return (gate_out / (1.0 + jnp.exp(-gate_out)) * up_out).astype(BF16)

    act0, act1 = hidden_units(gate0, up0), hidden_units(gate1, up1)
    wide = 512
    for n in range(D // wide):
        place = slice(n * wide, (n + 1) * wide)
        partial = jnp.dot(act0, down0[:, place], preferred_element_type=F32) + jnp.dot(
            act1, down1[:, place], preferred_element_type=F32
        )
        for i in range(wide // HD):
            c = n * (wide // HD) + i
            message[pl.ds(c, HALF, stride=2 * CHIPS), :] = partial[:, i * HD : (i + 1) * HD]


def sum_kernel(parts, mid_row, out):
    total = parts[0]
    for s in range(1, CHIPS * TP):
        total = total + parts[s]
    total = (mid_row[...] + total).astype(BF16)
    for r in range(8):
        out[:, r * HD : (r + 1) * HD] = total[r : r + 1, :]


def in_vmem(shape, dtype):
    return pltpu.VMEM(shape, dtype)


def stay(x):
    return pltpu.with_memory_space_constraint(x, pltpu.HBM)


def call(kernel, out_shape, operands, scratch=(), far=(), pinned=(), limit=SMALL, cost=None):
    vmem = pl.BlockSpec(memory_space=pltpu.VMEM)
    specs = [pl.BlockSpec(memory_space=pl.ANY) if i in far else vmem for i in range(len(operands))]
    return pl.pallas_call(
        kernel,
        out_shape=out_shape,
        in_specs=specs,
        out_specs=jax.tree.map(lambda _: vmem, out_shape, is_leaf=lambda x: not isinstance(x, tuple)),
        scratch_shapes=list(scratch),
        compiler_params=pltpu.CompilerParams(vmem_limit_bytes=limit),
        cost_estimate=cost,
    )(*(stay(x) if i in pinned else x for i, x in enumerate(operands)))


def shards(
    hidden_in,
    query,
    new_key,
    new_value,
    cache_keys,
    cache_values,
    lengths,
    out_weight,
    norm_gain,
    w_gate,
    w_up,
    w_down,
):
    def other_core(x):
        return lax.ppermute(x, "k", [(0, 1), (1, 0)])

    w_gate, w_up = w_gate.T, w_up.T
    other_out_weight, other_gate, other_up, other_down = map(other_core, (out_weight, w_gate, w_up, w_down))

    inputs = (query, hidden_in, new_key, new_value, lengths)
    message, own, limits = call(
        start_kernel,
        (in_vmem((SEQS, 16, HD), BF16), in_vmem((2, HEADS, HD), F32), in_vmem((SEQS, HD), jnp.int32)),
        inputs,
        [
            *(pltpu.VMEM(x.shape, x.dtype) for x in inputs[:4]),
            pltpu.SMEM(lengths.shape, jnp.int32),
            pltpu.SemaphoreType.DMA((5,)),
        ],
        far=range(5),
        pinned=range(5),
    )
    gathered = lax.all_to_all(message, ("p", "k"), 0, 0, tiled=True)
    first = (GROUPS[0], *cache_keys.shape[1:])
    later = (SEQS - GROUPS[0], *cache_keys.shape[1:])
    first_keys, first_values = call(
        first_kernel,
        (in_vmem(first, BF16), in_vmem(first, BF16)),
        (cache_keys, cache_values),
        [pltpu.SemaphoreType.DMA((2,))],
        far=range(2),
        pinned=range(2),
        cost=pl.CostEstimate(flops=0, bytes_accessed=4 * math.prod(first), transcendentals=0),
    )
    sent, kept, kept_lse, hidden_part = call(
        attend_kernel,
        (
            in_vmem((MSG, HD), BF16),
            in_vmem((ROWS, HD), F32),
            in_vmem((ROWS, HD), F32),
            in_vmem((2, HALF, HD), F32),
        ),
        (limits, gathered, own, first_keys, first_values, cache_keys, cache_values),
        [
            pltpu.VMEM(later, BF16),
            pltpu.VMEM(later, BF16),
            pltpu.VMEM((2, ROWS, HD), F32),
            pltpu.VMEM((2, ROWS, HD), F32),
            pltpu.VMEM((SEQS * 16, HD), F32),
            pltpu.SemaphoreType.DMA((len(GROUPS) - 1, 2)),
        ],
        far=(5, 6),
        pinned=(5, 6),
        limit=LARGE,
    )
    came = other_core(sent)
    blocks, gain = call(
        merge_kernel,
        (jax.ShapeDtypeStruct((CHIPS, MSG, HD), BF16), in_vmem((8, HD), F32)),
        (kept, kept_lse, came, norm_gain.reshape(8, HD)),
    )
    blocks = lax.all_to_all(blocks, "p", 0, 0, tiled=True)
    gains = [gain] + [lax.ppermute(gain, "t", [((i + n) % TP, i) for i in range(TP)]) for n in range(1, TP)]
    weights = (w_gate, w_up, other_gate, other_up, w_down, other_down)
    columns, gains, *weights = call(
        project_kernel,
        (
            in_vmem((CHIPS * TP, 2 * HALF, HD), BF16),
            in_vmem((TP * 8, HD), F32),
            *(in_vmem(w_down.shape, BF16) for _ in weights),
        ),
        (blocks, hidden_part, *gains, *weights, out_weight, other_out_weight),
        [*(pltpu.VMEM(out_weight.shape, BF16) for _ in range(2)), pltpu.SemaphoreType.DMA((8,))],
        far=range(6, 14),
        pinned=(6, 7, 10, 12),
    )
    columns = lax.all_to_all(columns, ("p", "t"), 0, 0, tiled=True)
    partial, mid_row = call(
        feed_kernel,
        (in_vmem((CHIPS * TP * 8, HD), F32), in_vmem((8, HD), F32)),
        (columns, gains, *weights),
        [pltpu.VMEM((2 * CHIPS * HALF, HD), F32)],
    )
    partial = lax.all_to_all(partial.reshape(CHIPS * TP, 8, HD), ("p", "t"), 0, 0, tiled=True)
    return call(sum_kernel, jax.ShapeDtypeStruct((1, 8 * HD), BF16), (partial, mid_row))


def solution(mesh):
    cut = Mesh(mesh.devices.reshape(CHIPS, 2, TP), ("p", "k", "t"))
    ctx, tp = ("p", "k"), "t"
    return jax.shard_map(
        shards,
        mesh=cut,
        in_specs=(
            P(ctx, tp),
            P(ctx, tp),
            P(ctx, tp),
            P(ctx, tp),
            P(None, ctx, tp),
            P(None, ctx, tp),
            P(),
            P(tp, ctx),
            P(tp),
            P(None, ("p", "k", "t")),
            P(None, ("p", "k", "t")),
            P(("p", "k", "t"), None),
        ),
        out_specs=P(ctx, tp),
        check_vma=False,
    )
```

time: 94.3 us -> 87 us (0.923)
  local copies, waits for them, and re-layouts: 8.16 us -> 0.01 us
  blocking collectives: 32.2 us -> 37.4 us
  Pallas kernels: 19.5 us -> 15.7 us
  waiting for transfers between devices: 13.8 us -> 15.5 us
  other arithmetic: 1.42 us -> 0 us
    all_to_all x1, waiting for transfers between devices: 9.49 us -> 0.01 us  [shards(): blocks = lax.all_to_all(blocks, 'p', 0, 0, tiled=True)]
    ppermute x3, waiting for transfers between devices: 0.01 us -> 8.54 us  [shards(): lax.ppermute(gain, 't', [((i + n) % TP, i) for i in range(TP)])]
    all_to_all x1, blocking collectives: 15 us -> 22.2 us  [shards(): columns = lax.all_to_all(columns, ('p', 't'), 0, 0, tiled=True)]
    all_to_all x1, waiting for transfers between devices: 0.96 us -> 5.89 us  [shards(): gathered = lax.all_to_all(message, ('p', 'k'), 0, 0, tiled=True)]
    unnamed x14 -> x2, local copies, waits for them, and re-layouts: 4.28 us -> 0.01 us
    ppermute x2 -> x0, local copies, waits for them, and re-layouts: 3.86 us -> none  [other_core(): return lax.ppermute(x, 'k', [(0, 1), (1, 0)])]
    pallas_call x5 -> x7, Pallas kernels: 19.5 us -> 15.7 us  [call(): pl.pallas_call(kernel, out_shape=out_shape, in_specs=specs, out_specs=jax...]
    ppermute x5, waiting for transfers between devices: 3.31 us -> 1.12 us  [other_core(): return lax.ppermute(x, 'k', [(0, 1), (1, 0)])]
  transfers between devices with their start and end apart: 10 -> 10, of which waited for: 4 -> 5; matrix products, arithmetic and copies ran while one was open for 7% -> 0% of each run, Pallas kernels for 2% -> 12%
where the time goes in v2:
time: 87 us; the launch traced here: 86.6 us
  blocking collectives  37.4 us (43%)
  starting transfers between devices  17.9 us (21%)
  Pallas kernels  15.7 us (18%)
  waiting for transfers between devices  15.5 us (18%)
    all_to_all x1, blocking collectives, shards(): columns = lax.all_to_all(columns, ('p', 't'), 0, 0, tiled=True)  22.2 us
    pallas_call x7, Pallas kernels, call(): pl.pallas_call(kernel, out_shape=out_shape, in_specs=specs, out_specs=jax...  15.7 us
    all_to_all x1, blocking collectives, shards(): lax.all_to_all(partial.reshape(CHIPS * TP, 8, HD), ('p', 't'), 0, 0, tile...  15.2 us
    ppermute x3, waiting for transfers between devices, shards(): lax.ppermute(gain, 't', [((i + n) % TP, i) for i in range(TP)])  8.54 us
    all_to_all x1, starting transfers between devices, shards(): gathered = lax.all_to_all(message, ('p', 'k'), 0, 0, tiled=True)  7.53 us
    all_to_all x1, waiting for transfers between devices, shards(): gathered = lax.all_to_all(message, ('p', 'k'), 0, 0, tiled=True)  5.89 us
    ppermute x3, starting transfers between devices, shards(): lax.ppermute(gain, 't', [((i + n) % TP, i) for i in range(TP)])  5.8 us
    all_to_all x1, starting transfers between devices, shards(): blocks = lax.all_to_all(blocks, 'p', 0, 0, tiled=True)  3.58 us
  transfers between devices with their start and end apart: 10, of which 5 were waited for; matrix products, arithmetic and copies ran while one was open for 0% of the time, Pallas kernels for 12%

profile of v2, /device:TPU:0, one launch (start us, length us, event | category | flops | bytes accessed | tf_op | source)
XLA Modules:
  0.0 86.6 jit_solution(9088959203641035524)
XLA Ops:
  0.0 0.0 collective-permute-start.4
  0.0 0.5 collective-permute-start.5
  0.5 0.0 collective-permute-start.6
  0.5 1.5 %shard_map.118 = (bf16[32,16,128]{2,1,0:T(8,128)(2,1)}, f32[2,8,128]{2,1,0:T(8,128)S(1)}, s32[32,128]{1,0:T(8,128)S(1)}) custom-call(bf16[1,1024]{1,0:T(2,128)(2,1)} %refs_0_.1, bf16[1,1024]{1,0:T(2,128)(2,1)} %refs_1_.1, bf16[1,256]{1,0:T(2,128)(2,1)} %refs_2_.1, bf16[1,256]{1,0:T(2,128)(2,1)} %refs_3_.1, s32[32]{0:T(128)} %refs_4_.2), custom_call_target="tpu_custom_call" | custom-call | tf_op jit(solution)/shard_map/pallas_call | solution.py:293
  2.0 7.5 %all-to-all-start = ((bf16[32,16,128]{2,1,0:T(8,128)(2,1)}), bf16[32,16,128]{2,1,0:T(8,128)(2,1)S(1)}, u32[]{:S(2)}, u32[]{:S(2)}) async-start(bf16[32,16,128]{2,1,0:T(8,128)(2,1)} %get-tuple-element.27), calls=%async_computation | async-start | bytes 262144 | tf_op jit(solution)/shard_map/all_to_all | solution.py:337
  9.6 1.9 %shard_map.119 = (bf16[6,512,256]{2,1,0:T(8,128)(2,1)S(1)}, bf16[6,512,256]{2,1,0:T(8,128)(2,1)S(1)}) custom-call(bf16[32,512,256]{2,1,0:T(8,128)(2,1)} %cache_keys.1, bf16[32,512,256]{2,1,0:T(8,128)(2,1)} %cache_values.1), custom_call_target="tpu_custom_call" | custom-call | bytes 3145728 | tf_op jit(solution)/shard_map/pallas_call | solution.py:293
  11.5 5.9 %all-to-all-done.gathered = bf16[32,16,128]{2,1,0:T(8,128)(2,1)S(1)} async-done(((bf16[32,16,128]{2,1,0:T(8,128)(2,1)}), bf16[32,16,128]{2,1,0:T(8,128)(2,1)S(1)}, u32[]{:S(2)}, u32[]{:S(2)}) %all-to-all-start) | async-done | bytes 131104 | tf_op jit(solution)/shard_map/all_to_all | solution.py:337
  17.4 0.0 copy-start
  17.4 6.1 %shard_map.120 = (bf16[144,128]{1,0:T(8,128)(2,1)S(1)}, f32[128,128]{1,0:T(8,128)S(1)}, f32[128,128]{1,0:T(8,128)S(1)}, f32[2,16,128]{2,1,0:T(8,128)S(1)}) custom-call(s32[32,128]{1,0:T(8,128)S(1)} %get-tuple-element.26.limits, bf16[32,16,128]{2,1,0:T(8,128)(2,1)S(1)} %all-to-all-done.gathered, f32[2,8,128]{2,1,0:T(8,128)S(1)} %get-tuple-element.28.own, ...), custom_call_target="tpu_custom_call" | custom-call | tf_op jit(solution)/shard_map/pallas_call | solution.py:293
  23.5 0.2 collective-permute-start
  23.7 1.1 %collective-permute-done.came = bf16[144,128]{1,0:T(8,128)(2,1)S(1)} collective-permute-done((bf16[144,128]{1,0:T(8,128)(2,1)S(1)}, bf16[144,128]{1,0:T(8,128)(2,1)S(1)}, u32[]{:S(2)}, u32[]{:S(2)}) %collective-permute-start) | collective-permute-done | bytes 36896 | tf_op jit(solution)/shard_map/ppermute | solution.py:319
  24.8 0.0 copy-done
  24.8 1.0 %shard_map.121 = (bf16[16,144,128]{2,1,0:T(8,128)(2,1)}, f32[8,128]{1,0:T(8,128)S(1)}) custom-call(f32[128,128]{1,0:T(8,128)S(1)} %get-tuple-element.31.kept, f32[128,128]{1,0:T(8,128)S(1)} %get-tuple-element.32.kept_lse, bf16[144,128]{1,0:T(8,128)(2,1)S(1)} %collective-permute-done.came, f32[8,128]{1,0:T(8,128)S(1)} %bitcast.5), custom_call_target="tpu_custom_call" | custom-call | tf_op jit(solution)/shard_map/pallas_call | solution.py:293
  25.9 3.6 %all-to-all-start.1 = ((bf16[16,144,128]{2,1,0:T(8,128)(2,1)}), bf16[16,144,128]{2,1,0:T(8,128)(2,1)S(1)}, u32[]{:S(2)}, u32[]{:S(2)}) async-start(bf16[16,144,128]{2,1,0:T(8,128)(2,1)} %get-tuple-element.34), calls=%async_computation.1 | async-start | bytes 1179648 | tf_op jit(solution)/shard_map/all_to_all | solution.py:376
  29.4 0.2 collective-permute-start.7
  29.7 1.9 %collective-permute-start.3 = (f32[8,128]{1,0:T(8,128)S(1)}, f32[8,128]{1,0:T(8,128)S(1)}, u32[]{:S(2)}, u32[]{:S(2)}) collective-permute-start(f32[8,128]{1,0:T(8,128)S(1)} %get-tuple-element.36.gain0), channel_id=1, source_target_pairs={{3,0},{0,1},{1,2},{2,3},{7,4},{4,5},{5,6},{6,7},{11,8},{8,9},{9,10... | collective-permute-start | bytes 12296 | tf_op jit(solution)/shard_map/ppermute | solution.py:377
  31.6 3.7 %collective-permute-done.3.gain3 = f32[8,128]{1,0:T(8,128)S(1)} collective-permute-done((f32[8,128]{1,0:T(8,128)S(1)}, f32[8,128]{1,0:T(8,128)S(1)}, u32[]{:S(2)}, u32[]{:S(2)}) %collective-permute-start.3) | collective-permute-done | bytes 4128 | tf_op jit(solution)/shard_map/ppermute | solution.py:377
  35.3 1.9 %collective-permute-start.2 = (f32[8,128]{1,0:T(8,128)S(1)}, f32[8,128]{1,0:T(8,128)S(1)}, u32[]{:S(2)}, u32[]{:S(2)}) collective-permute-start(f32[8,128]{1,0:T(8,128)S(1)} %get-tuple-element.36.gain0), channel_id=1, source_target_pairs={{2,0},{3,1},{0,2},{1,3},{6,4},{7,5},{4,6},{5,7},{10,8},{11,9},{8,1... | collective-permute-start | bytes 12296 | tf_op jit(solution)/shard_map/ppermute | solution.py:377
  37.2 3.2 %collective-permute-done.2.gain2 = f32[8,128]{1,0:T(8,128)S(1)} collective-permute-done((f32[8,128]{1,0:T(8,128)S(1)}, f32[8,128]{1,0:T(8,128)S(1)}, u32[]{:S(2)}, u32[]{:S(2)}) %collective-permute-start.2) | collective-permute-done | bytes 4128 | tf_op jit(solution)/shard_map/ppermute | solution.py:377
  40.4 2.0 %collective-permute-start.1 = (f32[8,128]{1,0:T(8,128)S(1)}, f32[8,128]{1,0:T(8,128)S(1)}, u32[]{:S(2)}, u32[]{:S(2)}) collective-permute-start(f32[8,128]{1,0:T(8,128)S(1)} %get-tuple-element.36.gain0), channel_id=1, source_target_pairs={{1,0},{2,1},{3,2},{0,3},{5,4},{6,5},{7,6},{4,7},{9,8},{10,9},{11,1... | collective-permute-start | bytes 12296 | tf_op jit(solution)/shard_map/ppermute | solution.py:377
  42.4 1.6 %collective-permute-done.1.gain1 = f32[8,128]{1,0:T(8,128)S(1)} collective-permute-done((f32[8,128]{1,0:T(8,128)S(1)}, f32[8,128]{1,0:T(8,128)S(1)}, u32[]{:S(2)}, u32[]{:S(2)}) %collective-permute-start.1) | collective-permute-done | bytes 4128 | tf_op jit(solution)/shard_map/ppermute | solution.py:377
  44.0 0.0 collective-permute-done.7.refs_7_
  44.0 0.0 all-to-all-done.1.blocks
  44.0 0.0 collective-permute-done.4.refs_2_
  44.0 0.0 collective-permute-done.5.refs_3_
  44.1 0.0 collective-permute-done.6.refs_5_
  44.1 2.9 %shard_map.122 = (bf16[64,32,128]{2,1,0:T(8,128)(2,1)S(1)}, f32[32,128]{1,0:T(8,128)S(1)}, bf16[112,4096]{1,0:T(8,128)(2,1)S(1)}, bf16[112,4096]{1,0:T(8,128)(2,...) custom-call(bf16[16,144,128]{2,1,0:T(8,128)(2,1)S(1)} %all-to-all-do, ...), custom_call_target="tpu_custom_call" | custom-call | tf_op jit(solution)/shard_map/pallas_call | solution.py:293
  47.0 22.2 %all_to_all.20.parts = bf16[64,32,128]{2,1,0:T(8,128)(2,1)S(1)} all-to-all(bf16[64,32,128]{2,1,0:T(8,128)(2,1)S(1)} %get-tuple-element.37), channel_id=1, replica_groups=mesh['p'=16,'k'=2,'t'=4] {'p','t'}, dimensions={0} | all-to-all | bytes 1048576 | tf_op jit(solution)/shard_map/all_to_all | solution.py:391
  69.2 1.6 %shard_map.123 = (f32[512,128]{1,0:T(8,128)S(1)}, f32[8,128]{1,0:T(8,128)S(1)}) custom-call(bf16[64,32,128]{2,1,0:T(8,128)(2,1)S(1)} %all_to_all.20.parts, f32[32,128]{1,0:T(8,128)S(1)} %get-tuple-element.38.gains, bf16[112,4096]{1,0:T(8,128)(2,1)S(1)} %get-tuple-element.39.gate0, bf16[112,4096]{1,0:T(8,128)(2,1)S(1)} %get-tuple-element.40.up0, ...), custom_call_target="tpu_custom_call" | custom-call | tf_op jit(solution)/shard_map/pallas_call | solution.py:293
  70.8 15.2 %all_to_all.21.parts = f32[64,8,128]{2,1,0:T(8,128)S(1)} all-to-all(f32[64,8,128]{2,1,0:T(8,128)S(1)} %bitcast.4), channel_id=1, replica_groups=mesh['p'=16,'k'=2,'t'=4] {'p','t'}, dimensions={0} | all-to-all | bytes 524288 | tf_op jit(solution)/shard_map/all_to_all | solution.py:398
  86.0 0.7 shard_map.124
Async XLA Ops:
  0.0 44.0 %collective-permute-start.4 = (bf16[112,4096]{1,0:T(8,128)(2,1)}, bf16[112,4096]{1,0:T(8,128)(2,1)}, u32[]{:S(2)}, u32[]{:S(2)}) collective-permute-start(bf16[112,4096]{1,0:T(8,128)(2,1)} %bitcast.6), channel_id=1, source_target_pairs={{0,4},{4,0},{1,5},{5,1},{2,6},{6,2},{3,7},{7,3},{8,12},{12,8},{9,1... | collective-permute-start | bytes 2752520 | tf_op jit(solution)/shard_map/ppermute | solution.py:319
  0.0 44.0 %collective-permute-start.5 = (bf16[112,4096]{1,0:T(8,128)(2,1)}, bf16[112,4096]{1,0:T(8,128)(2,1)}, u32[]{:S(2)}, u32[]{:S(2)}) collective-permute-start(bf16[112,4096]{1,0:T(8,128)(2,1)} %bitcast.8), channel_id=1, source_target_pairs={{0,4},{4,0},{1,5},{5,1},{2,6},{6,2},{3,7},{7,3},{8,12},{12,8},{9,1... | collective-permute-start | bytes 2752520 | tf_op jit(solution)/shard_map/ppermute | solution.py:319
  0.5 43.5 %collective-permute-start.6 = (bf16[112,4096]{1,0:T(8,128)(2,1)}, bf16[112,4096]{1,0:T(8,128)(2,1)}, u32[]{:S(2)}, u32[]{:S(2)}) collective-permute-start(bf16[112,4096]{1,0:T(8,128)(2,1)} %refs_4_.3), channel_id=1, source_target_pairs={{0,4},{4,0},{1,5},{5,1},{2,6},{6,2},{3,7},{7,3},{8,12},{12,8},{9,1... | collective-permute-start | bytes 2752520 | tf_op jit(solution)/shard_map/ppermute | solution.py:319
  2.0 15.3 %all-to-all-start = ((bf16[32,16,128]{2,1,0:T(8,128)(2,1)}), bf16[32,16,128]{2,1,0:T(8,128)(2,1)S(1)}, u32[]{:S(2)}, u32[]{:S(2)}) async-start(bf16[32,16,128]{2,1,0:T(8,128)(2,1)} %get-tuple-element.27), calls=%async_computation | async-start | bytes 262144 | tf_op jit(solution)/shard_map/all_to_all | solution.py:337
  17.4 7.5 %copy-start = (f32[1024]{0:T(1024)S(1)}, f32[1024]{0:T(1024)}, u32[]{:S(2)}) copy-start(f32[1024]{0:T(1024)} %param.20) | copy-start | bytes 12292
  23.5 1.3 %collective-permute-start = (bf16[144,128]{1,0:T(8,128)(2,1)S(1)}, bf16[144,128]{1,0:T(8,128)(2,1)S(1)}, u32[]{:S(2)}, u32[]{:S(2)}) collective-permute-start(bf16[144,128]{1,0:T(8,128)(2,1)S(1)} %get-tuple-element.33), channel_id=1, source_target_pairs={{0,4},{4,0},{1,5},{5,1},{2,6},{6,2},{3,7},{7,3},{8,12},{12,8},{9,1... | collective-permute-start | bytes 110600 | tf_op jit(solution)/shard_map/ppermute | solution.py:319
  25.9 18.2 %all-to-all-start.1 = ((bf16[16,144,128]{2,1,0:T(8,128)(2,1)}), bf16[16,144,128]{2,1,0:T(8,128)(2,1)S(1)}, u32[]{:S(2)}, u32[]{:S(2)}) async-start(bf16[16,144,128]{2,1,0:T(8,128)(2,1)} %get-tuple-element.34), calls=%async_computation.1 | async-start | bytes 1179648 | tf_op jit(solution)/shard_map/all_to_all | solution.py:376
  29.4 14.6 %collective-permute-start.7 = (bf16[1024,128]{1,0:T(8,128)(2,1)}, bf16[1024,128]{1,0:T(8,128)(2,1)S(1)}, u32[]{:S(2)}, u32[]{:S(2)}) collective-permute-start(bf16[1024,128]{1,0:T(8,128)(2,1)} %refs_6_.1), channel_id=1, source_target_pairs={{0,4},{4,0},{1,5},{5,1},{2,6},{6,2},{3,7},{7,3},{8,12},{12,8},{9,1... | collective-permute-start | bytes 786440 | tf_op jit(solution)/shard_map/ppermute | solution.py:319
  29.7 5.6 %collective-permute-start.3 = (f32[8,128]{1,0:T(8,128)S(1)}, f32[8,128]{1,0:T(8,128)S(1)}, u32[]{:S(2)}, u32[]{:S(2)}) collective-permute-start(f32[8,128]{1,0:T(8,128)S(1)} %get-tuple-element.36.gain0), channel_id=1, source_target_pairs={{3,0},{0,1},{1,2},{2,3},{7,4},{4,5},{5,6},{6,7},{11,8},{8,9},{9,10... | collective-permute-start | bytes 12296 | tf_op jit(solution)/shard_map/ppermute | solution.py:377
  35.3 5.1 %collective-permute-start.2 = (f32[8,128]{1,0:T(8,128)S(1)}, f32[8,128]{1,0:T(8,128)S(1)}, u32[]{:S(2)}, u32[]{:S(2)}) collective-permute-start(f32[8,128]{1,0:T(8,128)S(1)} %get-tuple-element.36.gain0), channel_id=1, source_target_pairs={{2,0},{3,1},{0,2},{1,3},{6,4},{7,5},{4,6},{5,7},{10,8},{11,9},{8,1... | collective-permute-start | bytes 12296 | tf_op jit(solution)/shard_map/ppermute | solution.py:377
  40.4 3.6 %collective-permute-start.1 = (f32[8,128]{1,0:T(8,128)S(1)}, f32[8,128]{1,0:T(8,128)S(1)}, u32[]{:S(2)}, u32[]{:S(2)}) collective-permute-start(f32[8,128]{1,0:T(8,128)S(1)} %get-tuple-element.36.gain0), channel_id=1, source_target_pairs={{1,0},{2,1},{3,2},{0,3},{5,4},{6,5},{7,6},{4,7},{9,8},{10,9},{11,1... | collective-permute-start | bytes 12296 | tf_op jit(solution)/shard_map/ppermute | solution.py:377

commit v3 on v2

--- a/solution.py
+++ b/solution.py
@@ -21,12 +21,11 @@
 SEQS = 32
 HALF = 16
 HEADS = 8
-GROUPS = (6, 8, 8, 6, 4)
+GROUP = 8
 ROWS = HEADS * HALF
 MSG = ROWS + 16
 
 SMALL = 8 * 1024 * 1024
-LARGE = 24 * 1024 * 1024
 
 
 def pack_lse(lse_of_head):
@@ -52,7 +51,7 @@
 
 
 def start_kernel(*refs):
-    sources, (message, own, limits), landed, arrived = refs[:5], refs[5:8], refs[8:13], refs[13]
+    sources, (message, own, limits), landed, arrived = refs[:5], refs[7:10], refs[10:15], refs[15]
     for copy in copy_in(sources, landed, arrived):
         copy.wait()
     query, hidden, own_key, own_value, lengths = landed
@@ -75,49 +74,10 @@
         limits[b : b + 1, :] = jnp.full((1, HD), lengths[b], jnp.int32)
 
 
-def first_kernel(keys, values, first_keys, first_values, arrived):
-    count = first_keys.shape[0]
-    for copy in copy_in((keys.at[:count], values.at[:count]), (first_keys, first_values), arrived):
-        copy.wait()
-
-
-def attend_kernel(
-    limits,
-    gathered,
-    own,
-    first_keys,
-    first_values,
-    cache_keys,
-    cache_values,
-    sent,
-    kept,
-    kept_lse,
-    hidden_part,
-    later_keys,
-    later_values,
-    outs,
-    lses,
-    rows,
-    arrived,
-):
+def attend_kernel(limits, gathered, own, keys, values, sent, kept, kept_lse, hidden_part, outs, lses, rows):
     chip, core, plane = lax.axis_index("p"), lax.axis_index("k"), lax.axis_index("t")
-    first, ctx_dev = first_keys.shape[:2]
+    ctx_dev = keys.shape[1]
     factor = 1.0 / math.sqrt(HD)
-    copies, at = [()], first
-    for n, group in enumerate(GROUPS[1:]):
-        source, target = pl.ds(at, group), pl.ds(at - first, group)
-        copies.append(
-            copy_in(
-                (cache_keys.at[source], cache_values.at[source]),
-                (later_keys.at[target], later_values.at[target]),
-                arrived.at[n],
-            )
-        )
-        at += group
-
-    def block(b, early, later):
-        return early[b] if b < first else later[b - first]
-
     head = lax.broadcasted_iota(jnp.int32, (HEADS, HD), 0)
     zero = jnp.zeros((HEADS, HD), BF16)
     places = (chip * 2 + core) * ctx_dev + lax.broadcasted_iota(jnp.int32, (HEADS, ctx_dev), 1)
@@ -127,7 +87,7 @@
         wide = jnp.concatenate(
             [jnp.where(head < HEADS // 2, query, zero), jnp.where(head >= HEADS // 2, query, zero)], axis=1
         )
-        return lax.dot_general(wide, block(b, first_keys, later_keys), (((1,), (1,)), ((), ())), preferred_element_type=F32) * factor
+        return lax.dot_general(wide, keys[b], (((1,), (1,)), ((), ())), preferred_element_type=F32) * factor
 
     def soften(b, scores):
         limit = limits[b : b + 1, :]
@@ -137,18 +97,14 @@
         return top, weights, jnp.sum(weights.astype(F32), axis=1, keepdims=True)
 
     def collect(b, top, weights, den):
-        num = jnp.dot(weights, block(b, first_values, later_values), preferred_element_type=F32)
+        num = jnp.dot(weights, values[b], preferred_element_type=F32)
         num = jnp.where(head < HEADS // 2, num[:, :HD], num[:, HD:])
         some = den > 0.0
         safe = jnp.where(some, den, 1.0)
         return num / safe, jnp.where(some, top + jnp.log(safe), MASKED)
 
-    at = 0
-    for group, pair in zip(GROUPS, copies):
-        for copy in pair:
-            copy.wait()
-        sequences = range(at, at + group)
-        at += group
+    for at in range(0, SEQS, GROUP):
+        sequences = range(at, at + GROUP)
         scores = [score(b) for b in sequences]
         softened = [soften(b, x) for b, x in zip(sequences, scores)]
         collected = [collect(b, *x) for b, x in zip(sequences, softened)]
@@ -176,8 +132,7 @@
         hidden_part[i] = jnp.where(plane == chip // 4, part, 0.0)
 
 
-def merge_kernel(kept, kept_lse, came, gain, message, gain_out):
-    gain_out[...] = gain[...]
+def merge_kernel(kept, kept_lse, came, message):
     packed = came[ROWS:, :].astype(F32)
     merged_lse = []
     for h in range(HEADS):
@@ -196,14 +151,8 @@
     message[:, ROWS:, :] = jnp.broadcast_to(packed[None], (CHIPS, 16, HD))
 
 
-def project_kernel(blocks, hidden_part, gain0, gain1, gain2, gain3, *refs):
-    sources, message, gains, landed, arrived = refs[:8], refs[8], refs[9], refs[10:18], refs[18]
-    copies = copy_in(sources, landed, arrived)
-    weight, other_weight = landed[6:]
-    core, plane = lax.axis_index("k"), lax.axis_index("t")
-    for i, gain in enumerate((gain0, gain1, gain2, gain3)):
-        at = pl.multiple_of(lax.rem(plane + i, TP) * 8, 8)
-        gains[pl.ds(at, 8), :] = gain[...]
+def project_kernel(blocks, hidden_part, gain, weight, other_weight, message):
+    chip, core, plane = lax.axis_index("p"), lax.axis_index("k"), lax.axis_index("t")
     lse = []
     for s in range(CHIPS):
         packed = blocks[s, ROWS:, :].astype(F32)
@@ -224,18 +173,24 @@
             acc = acc + share[s][:, h : h + 1] * blocks[s, place, :].astype(F32)
         columns.append(acc.astype(BF16))
     attention = jnp.concatenate(columns, axis=1)
-    for copy in copies:
-        copy.wait()
     mine = jnp.dot(attention, weight[...], preferred_element_type=F32)
     other = jnp.dot(attention, other_weight[...], preferred_element_type=F32)
     low, high = jnp.where(core == 0, mine, other), jnp.where(core == 0, other, mine)
     for i, rows in enumerate((low, high)):
         rows = (rows + hidden_part[i]).astype(BF16)
         message[:, i * HALF : (i + 1) * HALF, :] = jnp.broadcast_to(rows[None], (CHIPS * TP, HALF, HD))
-
-
-def feed_kernel(parts, gains, gate0, up0, gate1, up1, down0, down1, message, mid_row, mid):
+    rows = jnp.concatenate([*addends(gain[pl.ds((chip % 4) * 2, 2), :]), jnp.zeros((2, HD), F32)], axis=0)
+    rows = jnp.where(plane == chip // 4, rows, 0.0).astype(BF16)
+    message[:, 2 * HALF :, :] = jnp.broadcast_to(rows[None], (CHIPS * TP, 8, HD))
+
+
+def feed_kernel(
+    parts, gate0, up0, gate1, up1, down0, down1, message, mid_row, mid, sums, gains
+):
     chip, plane = lax.axis_index("p"), lax.axis_index("t")
+    for c in range(CHIPS):
+        rows = parts[c * TP + c // 4, 2 * HALF :, :].astype(F32)
+        gains[c * 8 : (c + 1) * 8, :] = (rows + pltpu.roll(rows, 6, 0)) + pltpu.roll(rows, 4, 0)
     square = jnp.zeros((HALF, HD), F32)
     for c in range(2 * CHIPS):
         place = slice((c % 2) * HALF, (c % 2 + 1) * HALF)
@@ -248,7 +203,7 @@
     mid_row[...] = mid[pl.ds(plane * 8 * HALF + chip, 8, stride=HALF), :]
 
     def normed_columns(c):
-        return (mid[c * HALF : (c + 1) * HALF, :] * scale * gains[c : c + 1, :]).astype(BF16)
+        return (mid[c * HALF : (c + 1) * HALF, :] * scale * gains[c // 2 * 8 + c % 2 : c // 2 * 8 + c % 2 + 1, :]).astype(BF16)
 
     normed = jnp.concatenate([normed_columns(c) for c in range(2 * CHIPS)], axis=1)
 
@@ -267,13 +222,14 @@
         )
         for i in range(wide // HD):
             c = n * (wide // HD) + i
-            message[pl.ds(c, HALF, stride=2 * CHIPS), :] = partial[:, i * HD : (i + 1) * HD]
+            sums[pl.ds(c, HALF, stride=2 * CHIPS), :] = partial[:, i * HD : (i + 1) * HD]
+    message[...] = sums[...].astype(BF16)
 
 
 def sum_kernel(parts, mid_row, out):
-    total = parts[0]
+    total = parts[0].astype(F32)
     for s in range(1, CHIPS * TP):
-        total = total + parts[s]
+        total = total + parts[s].astype(F32)
     total = (mid_row[...] + total).astype(BF16)
     for r in range(8):
         out[:, r * HD : (r + 1) * HD] = total[r : r + 1, :]
@@ -285,6 +241,10 @@
 
 def stay(x):
     return pltpu.with_memory_space_constraint(x, pltpu.HBM)
+
+
+def held(x):
+    return pltpu.with_memory_space_constraint(x, pltpu.VMEM)
 
 
 def call(kernel, out_shape, operands, scratch=(), far=(), pinned=(), limit=SMALL, cost=None):
@@ -319,33 +279,22 @@
         return lax.ppermute(x, "k", [(0, 1), (1, 0)])
 
     w_gate, w_up = w_gate.T, w_up.T
-    other_out_weight, other_gate, other_up, other_down = map(other_core, (out_weight, w_gate, w_up, w_down))
-
     inputs = (query, hidden_in, new_key, new_value, lengths)
     message, own, limits = call(
         start_kernel,
         (in_vmem((SEQS, 16, HD), BF16), in_vmem((2, HEADS, HD), F32), in_vmem((SEQS, HD), jnp.int32)),
-        inputs,
+        (*inputs, cache_keys, cache_values),
         [
             *(pltpu.VMEM(x.shape, x.dtype) for x in inputs[:4]),
             pltpu.SMEM(lengths.shape, jnp.int32),
             pltpu.SemaphoreType.DMA((5,)),
         ],
-        far=range(5),
-        pinned=range(5),
+        far=range(7),
+        pinned=range(7),
     )
     gathered = lax.all_to_all(message, ("p", "k"), 0, 0, tiled=True)
-    first = (GROUPS[0], *cache_keys.shape[1:])
-    later = (SEQS - GROUPS[0], *cache_keys.shape[1:])
-    first_keys, first_values = call(
-        first_kernel,
-        (in_vmem(first, BF16), in_vmem(first, BF16)),
-        (cache_keys, cache_values),
-        [pltpu.SemaphoreType.DMA((2,))],
-        far=range(2),
-        pinned=range(2),
-        cost=pl.CostEstimate(flops=0, bytes_accessed=4 * math.prod(first), transcendentals=0),
-    )
+    *exchanged, gathered = lax.optimization_barrier((out_weight, w_gate, w_up, w_down, gathered))
+    other_out_weight, other_gate, other_up, other_down = map(other_core, exchanged)
     sent, kept, kept_lse, hidden_part = call(
         attend_kernel,
         (
@@ -354,46 +303,34 @@
             in_vmem((ROWS, HD), F32),
             in_vmem((2, HALF, HD), F32),
         ),
-        (limits, gathered, own, first_keys, first_values, cache_keys, cache_values),
+        (limits, gathered, own, held(cache_keys), held(cache_values)),
         [
-            pltpu.VMEM(later, BF16),
-            pltpu.VMEM(later, BF16),
             pltpu.VMEM((2, ROWS, HD), F32),
             pltpu.VMEM((2, ROWS, HD), F32),
             pltpu.VMEM((SEQS * 16, HD), F32),
-            pltpu.SemaphoreType.DMA((len(GROUPS) - 1, 2)),
         ],
-        far=(5, 6),
-        pinned=(5, 6),
-        limit=LARGE,
     )
     came = other_core(sent)
-    blocks, gain = call(
-        merge_kernel,
-        (jax.ShapeDtypeStruct((CHIPS, MSG, HD), BF16), in_vmem((8, HD), F32)),
-        (kept, kept_lse, came, norm_gain.reshape(8, HD)),
+    blocks = call(merge_kernel, in_vmem((CHIPS, MSG, HD), BF16), (kept, kept_lse, came))
+    blocks, other_gate, other_up, other_down, other_out_weight = lax.optimization_barrier(
+        (blocks, other_gate, other_up, other_down, other_out_weight)
     )
     blocks = lax.all_to_all(blocks, "p", 0, 0, tiled=True)
-    gains = [gain] + [lax.ppermute(gain, "t", [((i + n) % TP, i) for i in range(TP)]) for n in range(1, TP)]
-    weights = (w_gate, w_up, other_gate, other_up, w_down, other_down)
-    columns, gains, *weights = call(
+    columns = call(
         project_kernel,
-        (
-            in_vmem((CHIPS * TP, 2 * HALF, HD), BF16),
-            in_vmem((TP * 8, HD), F32),
-            *(in_vmem(w_down.shape, BF16) for _ in weights),
-        ),
-        (blocks, hidden_part, *gains, *weights, out_weight, other_out_weight),
-        [*(pltpu.VMEM(out_weight.shape, BF16) for _ in range(2)), pltpu.SemaphoreType.DMA((8,))],
-        far=range(6, 14),
-        pinned=(6, 7, 10, 12),
+        in_vmem((CHIPS * TP, 2 * HALF + 8, HD), BF16),
+        (blocks, hidden_part, norm_gain.reshape(8, HD), out_weight, other_out_weight),
     )
     columns = lax.all_to_all(columns, ("p", "t"), 0, 0, tiled=True)
     partial, mid_row = call(
         feed_kernel,
-        (in_vmem((CHIPS * TP * 8, HD), F32), in_vmem((8, HD), F32)),
-        (columns, gains, *weights),
-        [pltpu.VMEM((2 * CHIPS * HALF, HD), F32)],
+        (in_vmem((CHIPS * TP * 8, HD), BF16), in_vmem((8, HD), F32)),
+        (columns, w_gate, w_up, other_gate, other_up, w_down, other_down),
+        [
+            pltpu.VMEM((2 * CHIPS * HALF, HD), F32),
+            pltpu.VMEM((CHIPS * TP * 8, HD), F32),
+            pltpu.VMEM((CHIPS * 8, HD), F32),
+        ],
     )
     partial = lax.all_to_all(partial.reshape(CHIPS * TP, 8, HD), ("p", "t"), 0, 0, tiled=True)
     return call(sum_kernel, jax.ShapeDtypeStruct((1, 8 * HD), BF16), (partial, mid_row))

time: 87 us -> 77.3 us (0.89)
  blocking collectives: 37.4 us -> 66.9 us
  starting transfers between devices: 17.9 us -> 1.2 us
  waiting for transfers between devices: 15.5 us -> 1.12 us
  Pallas kernels: 15.7 us -> 7.68 us
    all_to_all x0 -> x2, blocking collectives: none -> 31.1 us  [the longest x1 15.8 us: shards(): blocks = lax.all_to_all(blocks, 'p', 0, 0, tiled=True)]
    all_to_all x2 -> x0, starting transfers between devices: 11.1 us -> none  [the longest x1 7.53 us: shards(): gathered = lax.all_to_all(message, ('p', 'k'), 0, 0, tiled=True)]
    ppermute x3 -> x0, waiting for transfers between devices: 8.54 us -> none  [shards(): lax.ppermute(gain, 't', [((i + n) % TP, i) for i in range(TP)])]
    pallas_call x7 -> x6, Pallas kernels: 15.7 us -> 7.68 us  [call(): pl.pallas_call(kernel, out_shape=out_shape, in_specs=specs, out_specs=jax...]
    all_to_all x2 -> x0, waiting for transfers between devices: 5.89 us -> none  [the longest x1 5.89 us: shards(): gathered = lax.all_to_all(message, ('p', 'k'), 0, 0, tiled=True)]
    ppermute x3 -> x0, starting transfers between devices: 5.8 us -> none  [shards(): lax.ppermute(gain, 't', [((i + n) % TP, i) for i in range(TP)])]
  transfers between devices with their start and end apart: 10 -> 5, of which waited for: 5 -> 1; matrix products, arithmetic and copies ran while one was open for 0% -> 0% of each run, Pallas kernels for 12% -> 5%
where the time goes in v3:
time: 77.3 us; the launch traced here: 77.1 us
  blocking collectives  66.9 us (87%)
  Pallas kernels  7.68 us (10%)
  starting transfers between devices  1.2 us (2%)
  waiting for transfers between devices  1.12 us (1%)
    all_to_all x1, blocking collectives, shards(): columns = lax.all_to_all(columns, ('p', 't'), 0, 0, tiled=True)  21.4 us
    all_to_all x1, blocking collectives, shards(): blocks = lax.all_to_all(blocks, 'p', 0, 0, tiled=True)  15.8 us
    all_to_all x1, blocking collectives, shards(): gathered = lax.all_to_all(message, ('p', 'k'), 0, 0, tiled=True)  15.3 us
    all_to_all x1, blocking collectives, shards(): lax.all_to_all(partial.reshape(CHIPS * TP, 8, HD), ('p', 't'), 0, 0, tile...  14.5 us
    pallas_call x6, Pallas kernels, call(): pl.pallas_call(kernel, out_shape=out_shape, in_specs=specs, out_specs=jax...  7.68 us
  transfers between devices with their start and end apart: 5, of which 1 were waited for; matrix products, arithmetic and copies ran while one was open for 0% of the time, Pallas kernels for 5%

profile of v3, /device:TPU:0, one launch (start us, length us, event | category | flops | bytes accessed | tf_op | source)
XLA Modules:
  0.0 77.1 jit_solution(853838283167349957)
XLA Ops:
  0.0 0.0 copy-start.1
  0.0 0.0 copy-start
  0.0 0.0 copy-start.5
  0.0 1.0 %shard_map.118 = (bf16[32,16,128]{2,1,0:T(8,128)(2,1)S(1)}, f32[2,8,128]{2,1,0:T(8,128)S(1)}, s32[32,128]{1,0:T(8,128)S(1)}) custom-call(bf16[1,1024]{1,0:T(2,128)(2,1)} %refs_0_.1, bf16[1,1024]{1,0:T(2,128)(2,1)} %refs_1_.1, bf16[1,256]{1,0:T(2,128)(2,1)} %refs_2_.1, bf16[1,256]{1,0:T(2,128)(2,1)} %refs_3_.1, s32[32]{0:T(128)} %refs_4_.1, ...), custom_call_target="tpu_custom_call" | custom-call | tf_op jit(solution)/shard_map/pallas_call | solution.py:253
  1.0 15.3 %all_to_all.20.gathered = bf16[32,16,128]{2,1,0:T(8,128)(2,1)S(1)} all-to-all(bf16[32,16,128]{2,1,0:T(8,128)(2,1)S(1)} %get-tuple-element.25), channel_id=1, replica_groups=mesh['p'=16,'k'=2,'t'=4] {'p','k'}, dimensions={0} | all-to-all | bytes 262144 | tf_op jit(solution)/shard_map/all_to_all | solution.py:295
  16.3 0.1 collective-permute-start.1
  16.4 0.4 collective-permute-start.2
  16.8 0.1 collective-permute-start.3
  16.9 0.0 copy-done.5
  16.9 0.4 collective-permute-start.4
  17.3 0.0 copy-done.1
  17.3 0.0 copy-done
  17.3 0.0 copy-start.6
  17.3 0.0 copy-start.2
  17.3 0.0 copy-start.3
  17.4 0.0 copy-start.4
  17.4 3.5 %shard_map.119 = (bf16[144,128]{1,0:T(8,128)(2,1)S(1)}, f32[128,128]{1,0:T(8,128)S(1)}, f32[128,128]{1,0:T(8,128)S(1)}, f32[2,16,128]{2,1,0:T(8,128)S(1)}) custom-call(s32[32,128]{1,0:T(8,128)S(1)} %get-tuple-element.24.limits, bf16[32,16,128]{2,1,0:T(8,128)(2,1)S(1)} %all_to_all.20.gathered, f32[2,8,128]{2,1,0:T(8,128)S(1)} %get-tuple-element.27.own, ...), custom_call_target="tpu_custom_call" | custom-call | tf_op jit(solution)/shard_map/pallas_call | solution.py:253
  20.8 0.2 collective-permute-start
  21.0 1.1 %collective-permute-done.came = bf16[144,128]{1,0:T(8,128)(2,1)S(1)} collective-permute-done((bf16[144,128]{1,0:T(8,128)(2,1)S(1)}, bf16[144,128]{1,0:T(8,128)(2,1)S(1)}, u32[]{:S(2)}, u32[]{:S(2)}) %collective-permute-start) | collective-permute-done | bytes 36896 | tf_op jit(solution)/shard_map/ppermute | solution.py:279
  22.1 0.2 shard_map.120
  22.3 0.0 collective-permute-done.4.other_weight
  22.4 0.0 collective-permute-done.1.gate1
  22.4 0.0 collective-permute-done.2.up1
  22.4 0.0 collective-permute-done.3.down1
  22.4 15.8 %all_to_all.21.blocks = bf16[16,144,128]{2,1,0:T(8,128)(2,1)S(1)} all-to-all(bf16[16,144,128]{2,1,0:T(8,128)(2,1)S(1)} %shard_map.120), channel_id=1, replica_groups=mesh['p'=16,'k'=2,'t'=4] {'p'}, dimensions={0} | all-to-all | bytes 1179648 | tf_op jit(solution)/shard_map/all_to_all | solution.py:318
  38.2 0.0 copy-done.6
  38.2 0.7 shard_map.121
  38.9 21.4 %all_to_all.22.parts = bf16[64,40,128]{2,1,0:T(8,128)(2,1)S(1)} all-to-all(bf16[64,40,128]{2,1,0:T(8,128)(2,1)S(1)} %shard_map.121), channel_id=1, replica_groups=mesh['p'=16,'k'=2,'t'=4] {'p','t'}, dimensions={0} | all-to-all | bytes 1310720 | tf_op jit(solution)/shard_map/all_to_all | solution.py:324
  60.3 0.0 copy-done.2
  60.3 0.0 copy-done.3
  60.3 0.0 copy-done.4
  60.3 1.6 %shard_map.122 = (bf16[512,128]{1,0:T(8,128)(2,1)S(1)}, f32[8,128]{1,0:T(8,128)S(1)}) custom-call(bf16[64,40,128]{2,1,0:T(8,128)(2,1)S(1)} %all_to_all.22.parts, bf16[112,4096]{1,0:T(8,128)(2,1)S(1)} %bitcast.5, bf16[112,4096]{1,0:T(8,128)(2,1)S(1)} %bitcast.7, bf16[112,4096]{1,0:T(8,128)(2,1)S(1)} %collective-permute-done.1.gate1, ...), custom_call_target="tpu_custom_call" | custom-call | tf_op jit(solution)/shard_map/pallas_call | solution.py:253
  61.9 14.5 %all_to_all.23.parts = bf16[64,8,128]{2,1,0:T(8,128)(2,1)S(1)} all-to-all(bf16[64,8,128]{2,1,0:T(8,128)(2,1)S(1)} %bitcast.8), channel_id=1, replica_groups=mesh['p'=16,'k'=2,'t'=4] {'p','t'}, dimensions={0} | all-to-all | bytes 262144 | tf_op jit(solution)/shard_map/all_to_all | solution.py:335
  76.4 0.7 shard_map.123
Async XLA Ops:
  0.0 17.3 %copy-start.1 = (bf16[32,512,256]{2,1,0:T(8,128)(2,1)S(1)}, bf16[32,512,256]{2,1,0:T(8,128)(2,1)}, u32[]{:S(2)}) copy-start(bf16[32,512,256]{2,1,0:T(8,128)(2,1)} %values.1) | copy-start | bytes 25165828
  0.0 17.3 %copy-start = (bf16[32,512,256]{2,1,0:T(8,128)(2,1)S(1)}, bf16[32,512,256]{2,1,0:T(8,128)(2,1)}, u32[]{:S(2)}) copy-start(bf16[32,512,256]{2,1,0:T(8,128)(2,1)} %keys.1) | copy-start | bytes 25165828
  0.0 16.9 %copy-start.5 = (bf16[1024,128]{1,0:T(8,128)(2,1)S(1)}, bf16[1024,128]{1,0:T(8,128)(2,1)}, u32[]{:S(2)}) copy-start(bf16[1024,128]{1,0:T(8,128)(2,1)} %weight.1) | copy-start | bytes 786436
  16.3 6.0 %collective-permute-start.1 = (bf16[112,4096]{1,0:T(8,128)(2,1)}, bf16[112,4096]{1,0:T(8,128)(2,1)S(1)}, u32[]{:S(2)}, u32[]{:S(2)}) collective-permute-start(bf16[112,4096]{1,0:T(8,128)(2,1)} %bitcast.4), channel_id=1, source_target_pairs={{0,4},{4,0},{1,5},{5,1},{2,6},{6,2},{3,7},{7,3},{8,12},{12,8},{9,1... | collective-permute-start | bytes 2752520 | tf_op jit(solution)/shard_map/ppermute | solution.py:279
  16.4 6.0 %collective-permute-start.2 = (bf16[112,4096]{1,0:T(8,128)(2,1)}, bf16[112,4096]{1,0:T(8,128)(2,1)S(1)}, u32[]{:S(2)}, u32[]{:S(2)}) collective-permute-start(bf16[112,4096]{1,0:T(8,128)(2,1)} %bitcast.6), channel_id=1, source_target_pairs={{0,4},{4,0},{1,5},{5,1},{2,6},{6,2},{3,7},{7,3},{8,12},{12,8},{9,1... | collective-permute-start | bytes 2752520 | tf_op jit(solution)/shard_map/ppermute | solution.py:279
  16.8 5.6 %collective-permute-start.3 = (bf16[112,4096]{1,0:T(8,128)(2,1)}, bf16[112,4096]{1,0:T(8,128)(2,1)S(1)}, u32[]{:S(2)}, u32[]{:S(2)}) collective-permute-start(bf16[112,4096]{1,0:T(8,128)(2,1)} %down0.1), channel_id=1, source_target_pairs={{0,4},{4,0},{1,5},{5,1},{2,6},{6,2},{3,7},{7,3},{8,12},{12,8},{9,1... | collective-permute-start | bytes 2752520 | tf_op jit(solution)/shard_map/ppermute | solution.py:279
  16.9 5.4 %collective-permute-start.4 = (bf16[1024,128]{1,0:T(8,128)(2,1)S(1)}, bf16[1024,128]{1,0:T(8,128)(2,1)S(1)}, u32[]{:S(2)}, u32[]{:S(2)}) collective-permute-start(bf16[1024,128]{1,0:T(8,128)(2,1)S(1)} %copy-done.5), channel_id=1, source_target_pairs={{0,4},{4,0},{1,5},{5,1},{2,6},{6,2},{3,7},{7,3},{8,12},{12,8},{9,1... | collective-permute-start | bytes 786440 | tf_op jit(solution)/shard_map/ppermute | solution.py:279
  17.3 20.8 %copy-start.6 = (f32[1024]{0:T(1024)S(1)}, f32[1024]{0:T(1024)}, u32[]{:S(2)}) copy-start(f32[1024]{0:T(1024)} %param.20) | copy-start | bytes 12292
  17.3 43.0 %copy-start.2 = (bf16[4096,112]{0,1:T(8,128)(2,1)S(1)}, bf16[4096,112]{0,1:T(8,128)(2,1)}, u32[]{:S(2)}) copy-start(bf16[4096,112]{0,1:T(8,128)(2,1)} %param.21) | copy-start | bytes 2752516
  17.3 43.0 %copy-start.3 = (bf16[4096,112]{0,1:T(8,128)(2,1)S(1)}, bf16[4096,112]{0,1:T(8,128)(2,1)}, u32[]{:S(2)}) copy-start(bf16[4096,112]{0,1:T(8,128)(2,1)} %param.22) | copy-start | bytes 2752516
  17.4 43.0 %copy-start.4 = (bf16[112,4096]{1,0:T(8,128)(2,1)S(1)}, bf16[112,4096]{1,0:T(8,128)(2,1)}, u32[]{:S(2)}) copy-start(bf16[112,4096]{1,0:T(8,128)(2,1)} %down0.1) | copy-start | bytes 2752516
  20.8 1.3 %collective-permute-start = (bf16[144,128]{1,0:T(8,128)(2,1)S(1)}, bf16[144,128]{1,0:T(8,128)(2,1)S(1)}, u32[]{:S(2)}, u32[]{:S(2)}) collective-permute-start(bf16[144,128]{1,0:T(8,128)(2,1)S(1)} %get-tuple-element.30), channel_id=1, source_target_pairs={{0,4},{4,0},{1,5},{5,1},{2,6},{6,2},{3,7},{7,3},{8,12},{12,8},{9,1... | collective-permute-start | bytes 110600 | tf_op jit(solution)/shard_map/ppermute | solution.py:279

commit v4 on v3

--- a/solution.py
+++ b/solution.py
@@ -23,7 +23,7 @@
 HEADS = 8
 GROUP = 8
 ROWS = HEADS * HALF
-MSG = ROWS + 16
+MSG = ROWS + 8
 
 SMALL = 8 * 1024 * 1024
 
@@ -34,7 +34,13 @@
     for h in range(HEADS):
         for i, part in enumerate(addends(lse_of_head(h))):
             packed = jnp.where(lane == i * HEADS + h, part, packed)
-    return packed.astype(BF16)
+    return (packed[:8] + pltpu.roll(packed[8:], 3 * HEADS, 1)).astype(BF16)
+
+
+def unpack_lse(packed):
+    packed = packed.astype(F32)
+    packed = jnp.concatenate([packed, pltpu.roll(packed, 128 - 3 * HEADS, 1)], axis=0)
+    return (packed + pltpu.roll(packed, 128 - HEADS, 1)) + pltpu.roll(packed, 128 - 2 * HEADS, 1)
 
 
 def addends(x):
@@ -74,8 +80,8 @@
         limits[b : b + 1, :] = jnp.full((1, HD), lengths[b], jnp.int32)
 
 
-def attend_kernel(limits, gathered, own, keys, values, sent, kept, kept_lse, hidden_part, outs, lses, rows):
-    chip, core, plane = lax.axis_index("p"), lax.axis_index("k"), lax.axis_index("t")
+def attend(parity, limits, gathered, keys, values, outs, lses):
+    chip, core = lax.axis_index("p"), lax.axis_index("k")
     ctx_dev = keys.shape[1]
     factor = 1.0 / math.sqrt(HD)
     head = lax.broadcasted_iota(jnp.int32, (HEADS, HD), 0)
@@ -90,7 +96,7 @@
         return lax.dot_general(wide, keys[b], (((1,), (1,)), ((), ())), preferred_element_type=F32) * factor
 
     def soften(b, scores):
-        limit = limits[b : b + 1, :]
+        limit = limits[pl.ds(b, 1), :]
         valid = places < jnp.concatenate([limit] * (ctx_dev // HD), axis=1)
         top = jnp.max(jnp.where(valid, scores, MASKED), axis=1, keepdims=True)
         weights = jnp.where(valid, jnp.exp(scores - top), 0.0).astype(BF16)
@@ -103,28 +109,33 @@
         safe = jnp.where(some, den, 1.0)
         return num / safe, jnp.where(some, top + jnp.log(safe), MASKED)
 
-    for at in range(0, SEQS, GROUP):
-        sequences = range(at, at + GROUP)
+    for at in range(0, HALF, GROUP):
+        sequences = [2 * j + parity for j in range(at, at + GROUP)]
         scores = [score(b) for b in sequences]
         softened = [soften(b, x) for b, x in zip(sequences, scores)]
         collected = [collect(b, *x) for b, x in zip(sequences, softened)]
-        for b, (out, lse) in zip(sequences, collected):
-            outs[b % 2, pl.ds(b // 2, HEADS, stride=HALF), :] = out
-            lses[b % 2, pl.ds(b // 2, HEADS, stride=HALF), :] = jnp.broadcast_to(lse, (HEADS, HD))
-
+        for i, (out, lse) in enumerate(collected):
+            outs[pl.ds(at + i, HEADS, stride=HALF), :] = out
+            lses[pl.ds(at + i, HEADS, stride=HALF), :] = jnp.broadcast_to(lse, (HEADS, HD))
+
+
+def other_kernel(limits, gathered, keys, values, sent, outs, lses):
+    attend(1 - lax.axis_index("k"), limits, gathered, keys, values, outs, lses)
+    sent[:ROWS, :] = outs[...].astype(BF16)
+    sent[ROWS:, :] = pack_lse(lambda h: lses[h * HALF : (h + 1) * HALF, :])
+
+
+def kept_kernel(limits, gathered, own, keys, values, kept, kept_lse, hidden_part, rows):
+    chip, core, plane = lax.axis_index("p"), lax.axis_index("k"), lax.axis_index("t")
+    attend(core, limits, gathered, keys, values, kept, kept_lse)
     fresh_score, value = own[0], own[1]
     place = pl.ds(chip, HEADS, stride=HALF)
-    cached, block_lse = outs[core, place, :], lses[core, place, :]
+    cached, block_lse = kept[place, :], kept_lse[place, :]
     top = jnp.maximum(block_lse, fresh_score)
     keep, fresh = jnp.exp(block_lse - top), jnp.exp(fresh_score - top)
     total = keep + fresh
-    outs[core, place, :] = (cached * keep + value * fresh) / total
-    lses[core, place, :] = top + jnp.log(total)
-    kept[...] = outs[core]
-    kept_lse[...] = lses[core]
-    other = 1 - core
-    sent[:ROWS, :] = outs[other].astype(BF16)
-    sent[ROWS:, :] = pack_lse(lambda h: lses[other, h * HALF : (h + 1) * HALF, :])
+    kept[place, :] = (cached * keep + value * fresh) / total
+    kept_lse[place, :] = top + jnp.log(total)
     rows[...] = gathered[...].reshape(SEQS * 16, HD).astype(F32)
     column = core * 16 + HEADS + (chip % 4) * 2
     for i in range(2):
@@ -133,14 +144,12 @@
 
 
 def merge_kernel(kept, kept_lse, came, message):
-    packed = came[ROWS:, :].astype(F32)
+    came_lse = unpack_lse(came[ROWS:, :])
     merged_lse = []
     for h in range(HEADS):
         place = slice(h * HALF, (h + 1) * HALF)
         mine = kept_lse[place, :]
-        theirs = (packed[:, h : h + 1] + packed[:, HEADS + h : HEADS + h + 1]) + packed[
-            :, 2 * HEADS + h : 2 * HEADS + h + 1
-        ]
+        theirs = came_lse[:, h : h + 1]
         top = jnp.maximum(mine, theirs)
         left, right = jnp.exp(mine - top), jnp.exp(theirs - top)
         total = left + right
@@ -148,15 +157,14 @@
         message[:, place, :] = jnp.broadcast_to(block.astype(BF16)[None], (CHIPS, HALF, HD))
         merged_lse.append(top + jnp.log(total))
     packed = pack_lse(lambda h: merged_lse[h])
-    message[:, ROWS:, :] = jnp.broadcast_to(packed[None], (CHIPS, 16, HD))
+    message[:, ROWS:, :] = jnp.broadcast_to(packed[None], (CHIPS, 8, HD))
 
 
 def project_kernel(blocks, hidden_part, gain, weight, other_weight, message):
     chip, core, plane = lax.axis_index("p"), lax.axis_index("k"), lax.axis_index("t")
     lse = []
     for s in range(CHIPS):
-        packed = blocks[s, ROWS:, :].astype(F32)
-        lse.append((packed + pltpu.roll(packed, 128 - HEADS, 1)) + pltpu.roll(packed, 128 - 2 * HEADS, 1))
+        lse.append(unpack_lse(blocks[s, ROWS:, :]))
     top = lse[0]
     for s in range(1, CHIPS):
         top = jnp.maximum(top, lse[s])
@@ -295,22 +303,20 @@
     gathered = lax.all_to_all(message, ("p", "k"), 0, 0, tiled=True)
     *exchanged, gathered = lax.optimization_barrier((out_weight, w_gate, w_up, w_down, gathered))
     other_out_weight, other_gate, other_up, other_down = map(other_core, exchanged)
-    sent, kept, kept_lse, hidden_part = call(
-        attend_kernel,
-        (
-            in_vmem((MSG, HD), BF16),
-            in_vmem((ROWS, HD), F32),
-            in_vmem((ROWS, HD), F32),
-            in_vmem((2, HALF, HD), F32),
-        ),
-        (limits, gathered, own, held(cache_keys), held(cache_values)),
-        [
-            pltpu.VMEM((2, ROWS, HD), F32),
-            pltpu.VMEM((2, ROWS, HD), F32),
-            pltpu.VMEM((SEQS * 16, HD), F32),
-        ],
+    cache = held(cache_keys), held(cache_values)
+    sent = call(
+        other_kernel,
+        in_vmem((MSG, HD), BF16),
+        (limits, gathered, *cache),
+        [pltpu.VMEM((ROWS, HD), F32), pltpu.VMEM((ROWS, HD), F32)],
     )
     came = other_core(sent)
+    kept, kept_lse, hidden_part = call(
+        kept_kernel,
+        (in_vmem((ROWS, HD), F32), in_vmem((ROWS, HD), F32), in_vmem((2, HALF, HD), F32)),
+        (limits, gathered, own, *cache),
+        [pltpu.VMEM((SEQS * 16, HD), F32)],
+    )
     blocks = call(merge_kernel, in_vmem((CHIPS, MSG, HD), BF16), (kept, kept_lse, came))
     blocks, other_gate, other_up, other_down, other_out_weight = lax.optimization_barrier(
         (blocks, other_gate, other_up, other_down, other_out_weight)

time: 77.3 us -> 76.7 us (level)
    pallas_call x6 -> x7, Pallas kernels: 7.68 us -> 7.99 us  [call(): pl.pallas_call(kernel, out_shape=out_shape, in_specs=specs, out_specs=jax...]
where the time goes in v4:
time: 76.7 us; the launch traced here: 76.5 us
  blocking collectives  66.6 us (87%)
  Pallas kernels  7.99 us (10%)
  starting transfers between devices  1.2 us (2%)
    all_to_all x1, blocking collectives, shards(): columns = lax.all_to_all(columns, ('p', 't'), 0, 0, tiled=True)  21.4 us
    all_to_all x1, blocking collectives, shards(): blocks = lax.all_to_all(blocks, 'p', 0, 0, tiled=True)  15.5 us
    all_to_all x1, blocking collectives, shards(): gathered = lax.all_to_all(message, ('p', 'k'), 0, 0, tiled=True)  15.3 us
    all_to_all x1, blocking collectives, shards(): lax.all_to_all(partial.reshape(CHIPS * TP, 8, HD), ('p', 't'), 0, 0, tile...  14.5 us
    pallas_call x7, Pallas kernels, call(): pl.pallas_call(kernel, out_shape=out_shape, in_specs=specs, out_specs=jax...  7.99 us
  transfers between devices with their start and end apart: 5, of which 1 were waited for; matrix products, arithmetic and copies ran while one was open for 0% of the time, Pallas kernels for 5%

profile of v4, /device:TPU:0, one launch (start us, length us, event | category | flops | bytes accessed | tf_op | source)
XLA Modules:
  0.0 76.5 jit_solution(6432639257360254858)
XLA Ops:
  0.0 0.0 copy-start.1
  0.0 0.0 copy-start
  0.0 0.0 copy-start.5
  0.0 1.0 %shard_map.118 = (bf16[32,16,128]{2,1,0:T(8,128)(2,1)S(1)}, f32[2,8,128]{2,1,0:T(8,128)S(1)}, s32[32,128]{1,0:T(8,128)S(1)}) custom-call(bf16[1,1024]{1,0:T(2,128)(2,1)} %refs_0_.1, bf16[1,1024]{1,0:T(2,128)(2,1)} %refs_1_.1, bf16[1,256]{1,0:T(2,128)(2,1)} %refs_2_.1, bf16[1,256]{1,0:T(2,128)(2,1)} %refs_3_.1, s32[32]{0:T(128)} %refs_4_.1, ...), custom_call_target="tpu_custom_call" | custom-call | tf_op jit(solution)/shard_map/pallas_call | solution.py:261
  1.0 15.3 %all_to_all.20.gathered = bf16[32,16,128]{2,1,0:T(8,128)(2,1)S(1)} all-to-all(bf16[32,16,128]{2,1,0:T(8,128)(2,1)S(1)} %get-tuple-element.24), channel_id=1, replica_groups=mesh['p'=16,'k'=2,'t'=4] {'p','k'}, dimensions={0} | all-to-all | bytes 262144 | tf_op jit(solution)/shard_map/all_to_all | solution.py:303
  16.3 0.1 collective-permute-start.1
  16.4 0.4 collective-permute-start.2
  16.8 0.1 collective-permute-start.3
  16.9 0.0 copy-done.5
  16.9 0.4 collective-permute-start.4
  17.3 0.0 copy-done.1
  17.3 0.0 copy-done
  17.3 1.8 %shard_map.120 = bf16[136,128]{1,0:T(8,128)(2,1)S(1)} custom-call(s32[32,128]{1,0:T(8,128)S(1)} %get-tuple-element.23.limits, bf16[32,16,128]{2,1,0:T(8,128)(2,1)S(1)} %all_to_all.20.gathered, bf16[32,512,256]{2,1,0:T(8,128)(2,1)S(1)} %copy-done, bf16[32,512,256]{2,1,0:T(8,128)(2,1)S(1)} %copy-done.1), custom_call_target="tpu_custom_call" | custom-call | tf_op jit(solution)/shard_map/pallas_call | solution.py:261
  19.1 0.2 collective-permute-start
  19.3 0.0 copy-start.6
  19.3 0.0 copy-start.2
  19.3 0.0 copy-start.3
  19.3 0.0 copy-start.4
  19.3 1.8 %shard_map.119 = (f32[128,128]{1,0:T(8,128)S(1)}, f32[128,128]{1,0:T(8,128)S(1)}, f32[2,16,128]{2,1,0:T(8,128)S(1)}) custom-call(s32[32,128]{1,0:T(8,128)S(1)} %get-tuple-element.23.limits, bf16[32,16,128]{2,1,0:T(8,128)(2,1)S(1)} %all_to_all.20.gathered, f32[2,8,128]{2,1,0:T(8,128)S(1)} %get-tuple-element.26.own, bf16[32,512,256]{2,1,0:T(8,128)(2,1)S(1)} %copy-done, ...), custom_call_target="tpu_custom_call" | custom-call | tf_op jit(solution)/shard_map/pallas_call | solution.py:261
  21.1 0.0 collective-permute-done.came
  21.1 0.4 shard_map.121
  21.5 0.0 collective-permute-done.4.other_weight
  21.5 0.0 collective-permute-done.1.gate1
  21.5 0.0 collective-permute-done.2.up1
  21.5 0.6 collective-permute-done.3.down1
  22.0 15.5 %all_to_all.21.blocks = bf16[16,136,128]{2,1,0:T(8,128)(2,1)S(1)} all-to-all(bf16[16,136,128]{2,1,0:T(8,128)(2,1)S(1)} %shard_map.121), channel_id=1, replica_groups=mesh['p'=16,'k'=2,'t'=4] {'p'}, dimensions={0} | all-to-all | bytes 1114112 | tf_op jit(solution)/shard_map/all_to_all | solution.py:324
  37.5 0.0 copy-done.6
  37.5 0.8 %shard_map.122 = bf16[64,40,128]{2,1,0:T(8,128)(2,1)S(1)} custom-call(bf16[16,136,128]{2,1,0:T(8,128)(2,1)S(1)} %all_to_all.21.blocks, f32[2,16,128]{2,1,0:T(8,128)S(1)} %get-tuple-element.34.hidden_part, f32[8,128]{1,0:T(8,128)S(1)} %bitcast.9, bf16[1024,128]{1,0:T(8,128)(2,1)S(1)} %copy-done.5, bf16[1024,128]{1,0:T(8,128)(2,1)S(1)} %collective-permute-done.4.other_weight), custom_call_target="tpu_custom_call" | custom-call | tf_op jit(solution)/shard_map/pallas_call | solution.py:261
  38.4 21.4 %all_to_all.22.parts = bf16[64,40,128]{2,1,0:T(8,128)(2,1)S(1)} all-to-all(bf16[64,40,128]{2,1,0:T(8,128)(2,1)S(1)} %shard_map.122), channel_id=1, replica_groups=mesh['p'=16,'k'=2,'t'=4] {'p','t'}, dimensions={0} | all-to-all | bytes 1310720 | tf_op jit(solution)/shard_map/all_to_all | solution.py:330
  59.7 0.0 copy-done.2
  59.7 0.0 copy-done.3
  59.7 0.0 copy-done.4
  59.7 1.6 %shard_map.123 = (bf16[512,128]{1,0:T(8,128)(2,1)S(1)}, f32[8,128]{1,0:T(8,128)S(1)}) custom-call(bf16[64,40,128]{2,1,0:T(8,128)(2,1)S(1)} %all_to_all.22.parts, bf16[112,4096]{1,0:T(8,128)(2,1)S(1)} %bitcast.5, bf16[112,4096]{1,0:T(8,128)(2,1)S(1)} %bitcast.7, bf16[112,4096]{1,0:T(8,128)(2,1)S(1)} %collective-permute-done.1.gate1, ...), custom_call_target="tpu_custom_call" | custom-call | tf_op jit(solution)/shard_map/pallas_call | solution.py:261
  61.3 14.5 %all_to_all.23.parts = bf16[64,8,128]{2,1,0:T(8,128)(2,1)S(1)} all-to-all(bf16[64,8,128]{2,1,0:T(8,128)(2,1)S(1)} %bitcast.8), channel_id=1, replica_groups=mesh['p'=16,'k'=2,'t'=4] {'p','t'}, dimensions={0} | all-to-all | bytes 262144 | tf_op jit(solution)/shard_map/all_to_all | solution.py:341
  75.8 0.7 shard_map.124
Async XLA Ops:
  0.0 17.3 %copy-start.1 = (bf16[32,512,256]{2,1,0:T(8,128)(2,1)S(1)}, bf16[32,512,256]{2,1,0:T(8,128)(2,1)}, u32[]{:S(2)}) copy-start(bf16[32,512,256]{2,1,0:T(8,128)(2,1)} %values.3) | copy-start | bytes 25165828
  0.0 17.3 %copy-start = (bf16[32,512,256]{2,1,0:T(8,128)(2,1)S(1)}, bf16[32,512,256]{2,1,0:T(8,128)(2,1)}, u32[]{:S(2)}) copy-start(bf16[32,512,256]{2,1,0:T(8,128)(2,1)} %keys.3) | copy-start | bytes 25165828
  0.0 16.9 %copy-start.5 = (bf16[1024,128]{1,0:T(8,128)(2,1)S(1)}, bf16[1024,128]{1,0:T(8,128)(2,1)}, u32[]{:S(2)}) copy-start(bf16[1024,128]{1,0:T(8,128)(2,1)} %weight.1) | copy-start | bytes 786436
  16.3 5.2 %collective-permute-start.1 = (bf16[112,4096]{1,0:T(8,128)(2,1)}, bf16[112,4096]{1,0:T(8,128)(2,1)S(1)}, u32[]{:S(2)}, u32[]{:S(2)}) collective-permute-start(bf16[112,4096]{1,0:T(8,128)(2,1)} %bitcast.4), channel_id=1, source_target_pairs={{0,4},{4,0},{1,5},{5,1},{2,6},{6,2},{3,7},{7,3},{8,12},{12,8},{9,1... | collective-permute-start | bytes 2752520 | tf_op jit(solution)/shard_map/ppermute | solution.py:287
  16.4 5.1 %collective-permute-start.2 = (bf16[112,4096]{1,0:T(8,128)(2,1)}, bf16[112,4096]{1,0:T(8,128)(2,1)S(1)}, u32[]{:S(2)}, u32[]{:S(2)}) collective-permute-start(bf16[112,4096]{1,0:T(8,128)(2,1)} %bitcast.6), channel_id=1, source_target_pairs={{0,4},{4,0},{1,5},{5,1},{2,6},{6,2},{3,7},{7,3},{8,12},{12,8},{9,1... | collective-permute-start | bytes 2752520 | tf_op jit(solution)/shard_map/ppermute | solution.py:287
  16.8 5.2 %collective-permute-start.3 = (bf16[112,4096]{1,0:T(8,128)(2,1)}, bf16[112,4096]{1,0:T(8,128)(2,1)S(1)}, u32[]{:S(2)}, u32[]{:S(2)}) collective-permute-start(bf16[112,4096]{1,0:T(8,128)(2,1)} %down0.1), channel_id=1, source_target_pairs={{0,4},{4,0},{1,5},{5,1},{2,6},{6,2},{3,7},{7,3},{8,12},{12,8},{9,1... | collective-permute-start | bytes 2752520 | tf_op jit(solution)/shard_map/ppermute | solution.py:287
  16.9 4.5 %collective-permute-start.4 = (bf16[1024,128]{1,0:T(8,128)(2,1)S(1)}, bf16[1024,128]{1,0:T(8,128)(2,1)S(1)}, u32[]{:S(2)}, u32[]{:S(2)}) collective-permute-start(bf16[1024,128]{1,0:T(8,128)(2,1)S(1)} %copy-done.5), channel_id=1, source_target_pairs={{0,4},{4,0},{1,5},{5,1},{2,6},{6,2},{3,7},{7,3},{8,12},{12,8},{9,1... | collective-permute-start | bytes 786440 | tf_op jit(solution)/shard_map/ppermute | solution.py:287
  19.1 2.0 %collective-permute-start = (bf16[136,128]{1,0:T(8,128)(2,1)S(1)}, bf16[136,128]{1,0:T(8,128)(2,1)S(1)}, u32[]{:S(2)}, u32[]{:S(2)}) collective-permute-start(bf16[136,128]{1,0:T(8,128)(2,1)S(1)} %shard_map.120), channel_id=1, source_target_pairs={{0,4},{4,0},{1,5},{5,1},{2,6},{6,2},{3,7},{7,3},{8,12},{12,8},{9,1... | collective-permute-start | bytes 104456 | tf_op jit(solution)/shard_map/ppermute | solution.py:287
  19.3 18.3 %copy-start.6 = (f32[1024]{0:T(1024)S(1)}, f32[1024]{0:T(1024)}, u32[]{:S(2)}) copy-start(f32[1024]{0:T(1024)} %param.20) | copy-start | bytes 12292
  19.3 40.4 %copy-start.2 = (bf16[4096,112]{0,1:T(8,128)(2,1)S(1)}, bf16[4096,112]{0,1:T(8,128)(2,1)}, u32[]{:S(2)}) copy-start(bf16[4096,112]{0,1:T(8,128)(2,1)} %param.21) | copy-start | bytes 2752516
  19.3 40.4 %copy-start.3 = (bf16[4096,112]{0,1:T(8,128)(2,1)S(1)}, bf16[4096,112]{0,1:T(8,128)(2,1)}, u32[]{:S(2)}) copy-start(bf16[4096,112]{0,1:T(8,128)(2,1)} %param.22) | copy-start | bytes 2752516
  19.3 40.4 %copy-start.4 = (bf16[112,4096]{1,0:T(8,128)(2,1)S(1)}, bf16[112,4096]{1,0:T(8,128)(2,1)}, u32[]{:S(2)}) copy-start(bf16[112,4096]{1,0:T(8,128)(2,1)} %down0.1) | copy-start | bytes 2752516

commit v5 on v4

--- a/solution.py
+++ b/solution.py
@@ -125,18 +125,20 @@
     sent[ROWS:, :] = pack_lse(lambda h: lses[h * HALF : (h + 1) * HALF, :])
 
 
-def kept_kernel(limits, gathered, own, keys, values, kept, kept_lse, hidden_part, rows):
+def kept_kernel(limits, gathered, own, keys, values, kept, kept_lse, hidden_part, outs, lses, rows):
     chip, core, plane = lax.axis_index("p"), lax.axis_index("k"), lax.axis_index("t")
-    attend(core, limits, gathered, keys, values, kept, kept_lse)
+    attend(core, limits, gathered, keys, values, outs, lses)
     fresh_score, value = own[0], own[1]
     place = pl.ds(chip, HEADS, stride=HALF)
-    cached, block_lse = kept[place, :], kept_lse[place, :]
+    cached, block_lse = outs[place, :], lses[place, :]
     top = jnp.maximum(block_lse, fresh_score)
     keep, fresh = jnp.exp(block_lse - top), jnp.exp(fresh_score - top)
     total = keep + fresh
-    kept[place, :] = (cached * keep + value * fresh) / total
-    kept_lse[place, :] = top + jnp.log(total)
-    rows[...] = gathered[...].reshape(SEQS * 16, HD).astype(F32)
+    outs[place, :] = (cached * keep + value * fresh) / total
+    lses[place, :] = top + jnp.log(total)
+    kept[...] = outs[:ROWS, :]
+    kept_lse[...] = lses[:ROWS, :]
+    rows[: SEQS * 16, :] = gathered[...].reshape(SEQS * 16, HD).astype(F32)
     column = core * 16 + HEADS + (chip % 4) * 2
     for i in range(2):
         part = rows[pl.ds(column + i, HALF, stride=32), :]
@@ -315,7 +317,11 @@
         kept_kernel,
         (in_vmem((ROWS, HD), F32), in_vmem((ROWS, HD), F32), in_vmem((2, HALF, HD), F32)),
         (limits, gathered, own, *cache),
-        [pltpu.VMEM((SEQS * 16, HD), F32)],
+        [
+            pltpu.VMEM((ROWS + HALF, HD), F32),
+            pltpu.VMEM((ROWS + HALF, HD), F32),
+            pltpu.VMEM((SEQS * 16 + 32, HD), F32),
+        ],
     )
     blocks = call(merge_kernel, in_vmem((CHIPS, MSG, HD), BF16), (kept, kept_lse, came))
     blocks, other_gate, other_up, other_down, other_out_weight = lax.optimization_barrier(
@@ -333,7 +339,7 @@
         (in_vmem((CHIPS * TP * 8, HD), BF16), in_vmem((8, HD), F32)),
         (columns, w_gate, w_up, other_gate, other_up, w_down, other_down),
         [
-            pltpu.VMEM((2 * CHIPS * HALF, HD), F32),
+            pltpu.VMEM((2 * CHIPS * HALF + HALF, HD), F32),
             pltpu.VMEM((CHIPS * TP * 8, HD), F32),
             pltpu.VMEM((CHIPS * 8, HD), F32),
         ],

time: 76.7 us -> 76.7 us (level)
  no operation moved by 1% of the time
where the time goes in v5:
time: 76.7 us; the launch traced here: 76.5 us
  blocking collectives  66.6 us (87%)
  Pallas kernels  8 us (10%)
  starting transfers between devices  1.2 us (2%)
    all_to_all x1, blocking collectives, shards(): columns = lax.all_to_all(columns, ('p', 't'), 0, 0, tiled=True)  21.4 us
    all_to_all x1, blocking collectives, shards(): blocks = lax.all_to_all(blocks, 'p', 0, 0, tiled=True)  15.5 us
    all_to_all x1, blocking collectives, shards(): gathered = lax.all_to_all(message, ('p', 'k'), 0, 0, tiled=True)  15.3 us
    all_to_all x1, blocking collectives, shards(): lax.all_to_all(partial.reshape(CHIPS * TP, 8, HD), ('p', 't'), 0, 0, tile...  14.5 us
    pallas_call x7, Pallas kernels, call(): pl.pallas_call(kernel, out_shape=out_shape, in_specs=specs, out_specs=jax...  8 us
  transfers between devices with their start and end apart: 5, of which 1 were waited for; matrix products, arithmetic and copies ran while one was open for 0% of the time, Pallas kernels for 5%

profile of v5, /device:TPU:0, one launch (start us, length us, event | category | flops | bytes accessed | tf_op | source)
XLA Modules:
  0.0 76.5 jit_solution(14341818205215719251)
XLA Ops:
  0.0 0.0 copy-start.1
  0.0 0.0 copy-start
  0.0 0.0 copy-start.5
  0.0 1.0 %shard_map.118 = (bf16[32,16,128]{2,1,0:T(8,128)(2,1)S(1)}, f32[2,8,128]{2,1,0:T(8,128)S(1)}, s32[32,128]{1,0:T(8,128)S(1)}) custom-call(bf16[1,1024]{1,0:T(2,128)(2,1)} %refs_0_.1, bf16[1,1024]{1,0:T(2,128)(2,1)} %refs_1_.1, bf16[1,256]{1,0:T(2,128)(2,1)} %refs_2_.1, bf16[1,256]{1,0:T(2,128)(2,1)} %refs_3_.1, s32[32]{0:T(128)} %refs_4_.1, ...), custom_call_target="tpu_custom_call" | custom-call | tf_op jit(solution)/shard_map/pallas_call | solution.py:263
  1.0 15.3 %all_to_all.20.gathered = bf16[32,16,128]{2,1,0:T(8,128)(2,1)S(1)} all-to-all(bf16[32,16,128]{2,1,0:T(8,128)(2,1)S(1)} %get-tuple-element.24), channel_id=1, replica_groups=mesh['p'=16,'k'=2,'t'=4] {'p','k'}, dimensions={0} | all-to-all | bytes 262144 | tf_op jit(solution)/shard_map/all_to_all | solution.py:305
  16.3 0.1 collective-permute-start.1
  16.4 0.4 collective-permute-start.2
  16.8 0.1 collective-permute-start.3
  16.9 0.0 copy-done.5
  16.9 0.4 collective-permute-start.4
  17.3 0.0 copy-done.1
  17.3 0.0 copy-done
  17.3 1.8 %shard_map.120 = bf16[136,128]{1,0:T(8,128)(2,1)S(1)} custom-call(s32[32,128]{1,0:T(8,128)S(1)} %get-tuple-element.23.limits, bf16[32,16,128]{2,1,0:T(8,128)(2,1)S(1)} %all_to_all.20.gathered, bf16[32,512,256]{2,1,0:T(8,128)(2,1)S(1)} %copy-done, bf16[32,512,256]{2,1,0:T(8,128)(2,1)S(1)} %copy-done.1), custom_call_target="tpu_custom_call" | custom-call | tf_op jit(solution)/shard_map/pallas_call | solution.py:263
  19.1 0.2 collective-permute-start
  19.3 0.0 copy-start.6
  19.3 0.0 copy-start.2
  19.3 0.0 copy-start.3
  19.3 0.0 copy-start.4
  19.3 1.8 %shard_map.119 = (f32[128,128]{1,0:T(8,128)S(1)}, f32[128,128]{1,0:T(8,128)S(1)}, f32[2,16,128]{2,1,0:T(8,128)S(1)}) custom-call(s32[32,128]{1,0:T(8,128)S(1)} %get-tuple-element.23.limits, bf16[32,16,128]{2,1,0:T(8,128)(2,1)S(1)} %all_to_all.20.gathered, f32[2,8,128]{2,1,0:T(8,128)S(1)} %get-tuple-element.26.own, bf16[32,512,256]{2,1,0:T(8,128)(2,1)S(1)} %copy-done, ...), custom_call_target="tpu_custom_call" | custom-call | tf_op jit(solution)/shard_map/pallas_call | solution.py:263
  21.1 0.0 collective-permute-done.came
  21.1 0.4 shard_map.121
  21.5 0.0 collective-permute-done.4.other_weight
  21.5 0.0 collective-permute-done.1.gate1
  21.5 0.0 collective-permute-done.2.up1
  21.5 0.6 collective-permute-done.3.down1
  22.0 15.5 %all_to_all.21.blocks = bf16[16,136,128]{2,1,0:T(8,128)(2,1)S(1)} all-to-all(bf16[16,136,128]{2,1,0:T(8,128)(2,1)S(1)} %shard_map.121), channel_id=1, replica_groups=mesh['p'=16,'k'=2,'t'=4] {'p'}, dimensions={0} | all-to-all | bytes 1114112 | tf_op jit(solution)/shard_map/all_to_all | solution.py:330
  37.5 0.0 copy-done.6
  37.5 0.8 %shard_map.122 = bf16[64,40,128]{2,1,0:T(8,128)(2,1)S(1)} custom-call(bf16[16,136,128]{2,1,0:T(8,128)(2,1)S(1)} %all_to_all.21.blocks, f32[2,16,128]{2,1,0:T(8,128)S(1)} %get-tuple-element.34.hidden_part, f32[8,128]{1,0:T(8,128)S(1)} %bitcast.9, bf16[1024,128]{1,0:T(8,128)(2,1)S(1)} %copy-done.5, bf16[1024,128]{1,0:T(8,128)(2,1)S(1)} %collective-permute-done.4.other_weight), custom_call_target="tpu_custom_call" | custom-call | tf_op jit(solution)/shard_map/pallas_call | solution.py:263
  38.4 21.4 %all_to_all.22.parts = bf16[64,40,128]{2,1,0:T(8,128)(2,1)S(1)} all-to-all(bf16[64,40,128]{2,1,0:T(8,128)(2,1)S(1)} %shard_map.122), channel_id=1, replica_groups=mesh['p'=16,'k'=2,'t'=4] {'p','t'}, dimensions={0} | all-to-all | bytes 1310720 | tf_op jit(solution)/shard_map/all_to_all | solution.py:336
  59.7 0.0 copy-done.2
  59.7 0.0 copy-done.3
  59.7 0.0 copy-done.4
  59.7 1.6 %shard_map.123 = (bf16[512,128]{1,0:T(8,128)(2,1)S(1)}, f32[8,128]{1,0:T(8,128)S(1)}) custom-call(bf16[64,40,128]{2,1,0:T(8,128)(2,1)S(1)} %all_to_all.22.parts, bf16[112,4096]{1,0:T(8,128)(2,1)S(1)} %bitcast.5, bf16[112,4096]{1,0:T(8,128)(2,1)S(1)} %bitcast.7, bf16[112,4096]{1,0:T(8,128)(2,1)S(1)} %collective-permute-done.1.gate1, ...), custom_call_target="tpu_custom_call" | custom-call | tf_op jit(solution)/shard_map/pallas_call | solution.py:263
  61.3 14.5 %all_to_all.23.parts = bf16[64,8,128]{2,1,0:T(8,128)(2,1)S(1)} all-to-all(bf16[64,8,128]{2,1,0:T(8,128)(2,1)S(1)} %bitcast.8), channel_id=1, replica_groups=mesh['p'=16,'k'=2,'t'=4] {'p','t'}, dimensions={0} | all-to-all | bytes 262144 | tf_op jit(solution)/shard_map/all_to_all | solution.py:347
  75.8 0.7 shard_map.124
Async XLA Ops:
  0.0 17.3 %copy-start.1 = (bf16[32,512,256]{2,1,0:T(8,128)(2,1)S(1)}, bf16[32,512,256]{2,1,0:T(8,128)(2,1)}, u32[]{:S(2)}) copy-start(bf16[32,512,256]{2,1,0:T(8,128)(2,1)} %values.3) | copy-start | bytes 25165828
  0.0 17.3 %copy-start = (bf16[32,512,256]{2,1,0:T(8,128)(2,1)S(1)}, bf16[32,512,256]{2,1,0:T(8,128)(2,1)}, u32[]{:S(2)}) copy-start(bf16[32,512,256]{2,1,0:T(8,128)(2,1)} %keys.3) | copy-start | bytes 25165828
  0.0 16.9 %copy-start.5 = (bf16[1024,128]{1,0:T(8,128)(2,1)S(1)}, bf16[1024,128]{1,0:T(8,128)(2,1)}, u32[]{:S(2)}) copy-start(bf16[1024,128]{1,0:T(8,128)(2,1)} %weight.1) | copy-start | bytes 786436
  16.3 5.2 %collective-permute-start.1 = (bf16[112,4096]{1,0:T(8,128)(2,1)}, bf16[112,4096]{1,0:T(8,128)(2,1)S(1)}, u32[]{:S(2)}, u32[]{:S(2)}) collective-permute-start(bf16[112,4096]{1,0:T(8,128)(2,1)} %bitcast.4), channel_id=1, source_target_pairs={{0,4},{4,0},{1,5},{5,1},{2,6},{6,2},{3,7},{7,3},{8,12},{12,8},{9,1... | collective-permute-start | bytes 2752520 | tf_op jit(solution)/shard_map/ppermute | solution.py:289
  16.4 5.1 %collective-permute-start.2 = (bf16[112,4096]{1,0:T(8,128)(2,1)}, bf16[112,4096]{1,0:T(8,128)(2,1)S(1)}, u32[]{:S(2)}, u32[]{:S(2)}) collective-permute-start(bf16[112,4096]{1,0:T(8,128)(2,1)} %bitcast.6), channel_id=1, source_target_pairs={{0,4},{4,0},{1,5},{5,1},{2,6},{6,2},{3,7},{7,3},{8,12},{12,8},{9,1... | collective-permute-start | bytes 2752520 | tf_op jit(solution)/shard_map/ppermute | solution.py:289
  16.8 5.2 %collective-permute-start.3 = (bf16[112,4096]{1,0:T(8,128)(2,1)}, bf16[112,4096]{1,0:T(8,128)(2,1)S(1)}, u32[]{:S(2)}, u32[]{:S(2)}) collective-permute-start(bf16[112,4096]{1,0:T(8,128)(2,1)} %down0.1), channel_id=1, source_target_pairs={{0,4},{4,0},{1,5},{5,1},{2,6},{6,2},{3,7},{7,3},{8,12},{12,8},{9,1... | collective-permute-start | bytes 2752520 | tf_op jit(solution)/shard_map/ppermute | solution.py:289
  16.9 4.5 %collective-permute-start.4 = (bf16[1024,128]{1,0:T(8,128)(2,1)S(1)}, bf16[1024,128]{1,0:T(8,128)(2,1)S(1)}, u32[]{:S(2)}, u32[]{:S(2)}) collective-permute-start(bf16[1024,128]{1,0:T(8,128)(2,1)S(1)} %copy-done.5), channel_id=1, source_target_pairs={{0,4},{4,0},{1,5},{5,1},{2,6},{6,2},{3,7},{7,3},{8,12},{12,8},{9,1... | collective-permute-start | bytes 786440 | tf_op jit(solution)/shard_map/ppermute | solution.py:289
  19.1 2.0 %collective-permute-start = (bf16[136,128]{1,0:T(8,128)(2,1)S(1)}, bf16[136,128]{1,0:T(8,128)(2,1)S(1)}, u32[]{:S(2)}, u32[]{:S(2)}) collective-permute-start(bf16[136,128]{1,0:T(8,128)(2,1)S(1)} %shard_map.120), channel_id=1, source_target_pairs={{0,4},{4,0},{1,5},{5,1},{2,6},{6,2},{3,7},{7,3},{8,12},{12,8},{9,1... | collective-permute-start | bytes 104456 | tf_op jit(solution)/shard_map/ppermute | solution.py:289
  19.3 18.3 %copy-start.6 = (f32[1024]{0:T(1024)S(1)}, f32[1024]{0:T(1024)}, u32[]{:S(2)}) copy-start(f32[1024]{0:T(1024)} %param.20) | copy-start | bytes 12292
  19.3 40.4 %copy-start.2 = (bf16[4096,112]{0,1:T(8,128)(2,1)S(1)}, bf16[4096,112]{0,1:T(8,128)(2,1)}, u32[]{:S(2)}) copy-start(bf16[4096,112]{0,1:T(8,128)(2,1)} %param.21) | copy-start | bytes 2752516
  19.3 40.4 %copy-start.3 = (bf16[4096,112]{0,1:T(8,128)(2,1)S(1)}, bf16[4096,112]{0,1:T(8,128)(2,1)}, u32[]{:S(2)}) copy-start(bf16[4096,112]{0,1:T(8,128)(2,1)} %param.22) | copy-start | bytes 2752516
  19.3 40.4 %copy-start.4 = (bf16[112,4096]{1,0:T(8,128)(2,1)S(1)}, bf16[112,4096]{1,0:T(8,128)(2,1)}, u32[]{:S(2)}) copy-start(bf16[112,4096]{1,0:T(8,128)(2,1)} %down0.1) | copy-start | bytes 2752516

commit v6 on v5

--- a/solution.py
+++ b/solution.py
@@ -213,7 +213,7 @@
     mid_row[...] = mid[pl.ds(plane * 8 * HALF + chip, 8, stride=HALF), :]
 
     def normed_columns(c):
-        return (mid[c * HALF : (c + 1) * HALF, :] * scale * gains[c // 2 * 8 + c % 2 : c // 2 * 8 + c % 2 + 1, :]).astype(BF16)
+        return (mid[c * HALF : (c + 1) * HALF, :] * gains[c // 2 * 8 + c % 2 : c // 2 * 8 + c % 2 + 1, :]).astype(BF16)
 
     normed = jnp.concatenate([normed_columns(c) for c in range(2 * CHIPS)], axis=1)
 
@@ -221,6 +221,7 @@
         over = (((1,), (1,)), ((), ()))
         gate_out = lax.dot_general(normed, gate[...], over, preferred_element_type=F32)
         up_out = lax.dot_general(normed, up[...], over, preferred_element_type=F32)
+        gate_out, up_out = gate_out * scale, up_out * scale
         return (gate_out / (1.0 + jnp.exp(-gate_out)) * up_out).astype(BF16)
 
     act0, act1 = hidden_units(gate0, up0), hidden_units(gate1, up1)
@@ -324,8 +325,8 @@
         ],
     )
     blocks = call(merge_kernel, in_vmem((CHIPS, MSG, HD), BF16), (kept, kept_lse, came))
-    blocks, other_gate, other_up, other_down, other_out_weight = lax.optimization_barrier(
-        (blocks, other_gate, other_up, other_down, other_out_weight)
+    blocks, other_gate, other_up, other_out_weight = lax.optimization_barrier(
+        (blocks, other_gate, other_up, other_out_weight)
     )
     blocks = lax.all_to_all(blocks, "p", 0, 0, tiled=True)
     columns = call(
@@ -333,6 +334,7 @@
         in_vmem((CHIPS * TP, 2 * HALF + 8, HD), BF16),
         (blocks, hidden_part, norm_gain.reshape(8, HD), out_weight, other_out_weight),
     )
+    columns, other_down = lax.optimization_barrier((columns, other_down))
     columns = lax.all_to_all(columns, ("p", "t"), 0, 0, tiled=True)
     partial, mid_row = call(
         feed_kernel,

time: 76.7 us -> 76.5 us (level)
  transfers between devices with their start and end apart: 5 -> 5, of which waited for: 1 -> 0; matrix products, arithmetic and copies ran while one was open for 0% -> 0% of each run, Pallas kernels for 5% -> 6%
where the time goes in v6:
time: 76.5 us; the launch traced here: 76.3 us
  blocking collectives  67.1 us (88%)
  Pallas kernels  7.88 us (10%)
  starting transfers between devices  1.2 us (2%)
    all_to_all x1, blocking collectives, shards(): columns = lax.all_to_all(columns, ('p', 't'), 0, 0, tiled=True)  21.6 us
    all_to_all x1, blocking collectives, shards(): blocks = lax.all_to_all(blocks, 'p', 0, 0, tiled=True)  15.8 us
    all_to_all x1, blocking collectives, shards(): gathered = lax.all_to_all(message, ('p', 'k'), 0, 0, tiled=True)  15.3 us
    all_to_all x1, blocking collectives, shards(): lax.all_to_all(partial.reshape(CHIPS * TP, 8, HD), ('p', 't'), 0, 0, tile...  14.5 us
    pallas_call x7, Pallas kernels, call(): pl.pallas_call(kernel, out_shape=out_shape, in_specs=specs, out_specs=jax...  7.88 us
  transfers between devices with their start and end apart: 5, of which 0 were waited for; matrix products, arithmetic and copies ran while one was open for 0% of the time, Pallas kernels for 6%

profile of v6, /device:TPU:0, one launch (start us, length us, event | category | flops | bytes accessed | tf_op | source)
XLA Modules:
  0.0 76.3 jit_solution(14213570910082746139)
XLA Ops:
  0.0 0.0 copy-start.1
  0.0 0.0 copy-start
  0.0 0.0 copy-start.5
  0.0 1.0 %shard_map.118 = (bf16[32,16,128]{2,1,0:T(8,128)(2,1)S(1)}, f32[2,8,128]{2,1,0:T(8,128)S(1)}, s32[32,128]{1,0:T(8,128)S(1)}) custom-call(bf16[1,1024]{1,0:T(2,128)(2,1)} %refs_0_.1, bf16[1,1024]{1,0:T(2,128)(2,1)} %refs_1_.1, bf16[1,256]{1,0:T(2,128)(2,1)} %refs_2_.1, bf16[1,256]{1,0:T(2,128)(2,1)} %refs_3_.1, s32[32]{0:T(128)} %refs_4_.1, ...), custom_call_target="tpu_custom_call" | custom-call | tf_op jit(solution)/shard_map/pallas_call | solution.py:264
  1.0 15.3 %all_to_all.20.gathered = bf16[32,16,128]{2,1,0:T(8,128)(2,1)S(1)} all-to-all(bf16[32,16,128]{2,1,0:T(8,128)(2,1)S(1)} %get-tuple-element.25), channel_id=1, replica_groups=mesh['p'=16,'k'=2,'t'=4] {'p','k'}, dimensions={0} | all-to-all | bytes 262144 | tf_op jit(solution)/shard_map/all_to_all | solution.py:306
  16.3 0.1 collective-permute-start.1
  16.4 0.4 collective-permute-start.2
  16.8 0.1 collective-permute-start.4
  16.9 0.0 copy-done.5
  16.9 0.4 collective-permute-start.3
  17.3 0.0 copy-done.1
  17.3 0.0 copy-done
  17.3 1.8 %shard_map.120 = bf16[136,128]{1,0:T(8,128)(2,1)S(1)} custom-call(s32[32,128]{1,0:T(8,128)S(1)} %get-tuple-element.24.limits, bf16[32,16,128]{2,1,0:T(8,128)(2,1)S(1)} %all_to_all.20.gathered, bf16[32,512,256]{2,1,0:T(8,128)(2,1)S(1)} %copy-done, bf16[32,512,256]{2,1,0:T(8,128)(2,1)S(1)} %copy-done.1), custom_call_target="tpu_custom_call" | custom-call | tf_op jit(solution)/shard_map/pallas_call | solution.py:264
  19.1 0.2 collective-permute-start
  19.3 0.0 copy-start.6
  19.3 0.0 copy-start.2
  19.3 0.0 copy-start.3
  19.3 0.0 copy-start.4
  19.3 1.8 %shard_map.119 = (f32[128,128]{1,0:T(8,128)S(1)}, f32[128,128]{1,0:T(8,128)S(1)}, f32[2,16,128]{2,1,0:T(8,128)S(1)}) custom-call(s32[32,128]{1,0:T(8,128)S(1)} %get-tuple-element.24.limits, bf16[32,16,128]{2,1,0:T(8,128)(2,1)S(1)} %all_to_all.20.gathered, f32[2,8,128]{2,1,0:T(8,128)S(1)} %get-tuple-element.27.own, bf16[32,512,256]{2,1,0:T(8,128)(2,1)S(1)} %copy-done, ...), custom_call_target="tpu_custom_call" | custom-call | tf_op jit(solution)/shard_map/pallas_call | solution.py:264
  21.1 0.0 collective-permute-done.came
  21.1 0.4 shard_map.121
  21.5 0.0 collective-permute-done.3.other_weight
  21.5 0.0 collective-permute-done.1.gate1
  21.5 0.0 collective-permute-done.2.up1
  21.5 15.8 %all_to_all.21.blocks = bf16[16,136,128]{2,1,0:T(8,128)(2,1)S(1)} all-to-all(bf16[16,136,128]{2,1,0:T(8,128)(2,1)S(1)} %shard_map.121), channel_id=1, replica_groups=mesh['p'=16,'k'=2,'t'=4] {'p'}, dimensions={0} | all-to-all | bytes 1114112 | tf_op jit(solution)/shard_map/all_to_all | solution.py:331
  37.3 0.0 copy-done.6
  37.3 0.8 %shard_map.122 = bf16[64,40,128]{2,1,0:T(8,128)(2,1)S(1)} custom-call(bf16[16,136,128]{2,1,0:T(8,128)(2,1)S(1)} %all_to_all.21.blocks, f32[2,16,128]{2,1,0:T(8,128)S(1)} %get-tuple-element.34.hidden_part, f32[8,128]{1,0:T(8,128)S(1)} %bitcast.9, bf16[1024,128]{1,0:T(8,128)(2,1)S(1)} %copy-done.5, bf16[1024,128]{1,0:T(8,128)(2,1)S(1)} %collective-permute-done.3.other_weight), custom_call_target="tpu_custom_call" | custom-call | tf_op jit(solution)/shard_map/pallas_call | solution.py:264
  38.1 0.0 collective-permute-done.4.down1
  38.1 21.6 %all_to_all.22.parts = bf16[64,40,128]{2,1,0:T(8,128)(2,1)S(1)} all-to-all(bf16[64,40,128]{2,1,0:T(8,128)(2,1)S(1)} %shard_map.122), channel_id=1, replica_groups=mesh['p'=16,'k'=2,'t'=4] {'p','t'}, dimensions={0} | all-to-all | bytes 1310720 | tf_op jit(solution)/shard_map/all_to_all | solution.py:338
  59.7 0.0 copy-done.2
  59.7 0.0 copy-done.3
  59.7 0.0 copy-done.4
  59.7 1.5 %shard_map.123 = (bf16[512,128]{1,0:T(8,128)(2,1)S(1)}, f32[8,128]{1,0:T(8,128)S(1)}) custom-call(bf16[64,40,128]{2,1,0:T(8,128)(2,1)S(1)} %all_to_all.22.parts, bf16[112,4096]{1,0:T(8,128)(2,1)S(1)} %bitcast.5, bf16[112,4096]{1,0:T(8,128)(2,1)S(1)} %bitcast.7, bf16[112,4096]{1,0:T(8,128)(2,1)S(1)} %collective-permute-done.1.gate1, ...), custom_call_target="tpu_custom_call" | custom-call | tf_op jit(solution)/shard_map/pallas_call | solution.py:264
  61.1 14.5 %all_to_all.23.parts = bf16[64,8,128]{2,1,0:T(8,128)(2,1)S(1)} all-to-all(bf16[64,8,128]{2,1,0:T(8,128)(2,1)S(1)} %bitcast.8), channel_id=1, replica_groups=mesh['p'=16,'k'=2,'t'=4] {'p','t'}, dimensions={0} | all-to-all | bytes 262144 | tf_op jit(solution)/shard_map/all_to_all | solution.py:349
  75.6 0.7 shard_map.124
Async XLA Ops:
  0.0 17.3 %copy-start.1 = (bf16[32,512,256]{2,1,0:T(8,128)(2,1)S(1)}, bf16[32,512,256]{2,1,0:T(8,128)(2,1)}, u32[]{:S(2)}) copy-start(bf16[32,512,256]{2,1,0:T(8,128)(2,1)} %values.3) | copy-start | bytes 25165828
  0.0 17.3 %copy-start = (bf16[32,512,256]{2,1,0:T(8,128)(2,1)S(1)}, bf16[32,512,256]{2,1,0:T(8,128)(2,1)}, u32[]{:S(2)}) copy-start(bf16[32,512,256]{2,1,0:T(8,128)(2,1)} %keys.3) | copy-start | bytes 25165828
  0.0 16.9 %copy-start.5 = (bf16[1024,128]{1,0:T(8,128)(2,1)S(1)}, bf16[1024,128]{1,0:T(8,128)(2,1)}, u32[]{:S(2)}) copy-start(bf16[1024,128]{1,0:T(8,128)(2,1)} %weight.1) | copy-start | bytes 786436
  16.3 5.2 %collective-permute-start.1 = (bf16[112,4096]{1,0:T(8,128)(2,1)}, bf16[112,4096]{1,0:T(8,128)(2,1)S(1)}, u32[]{:S(2)}, u32[]{:S(2)}) collective-permute-start(bf16[112,4096]{1,0:T(8,128)(2,1)} %bitcast.4), channel_id=1, source_target_pairs={{0,4},{4,0},{1,5},{5,1},{2,6},{6,2},{3,7},{7,3},{8,12},{12,8},{9,1... | collective-permute-start | bytes 2752520 | tf_op jit(solution)/shard_map/ppermute | solution.py:290
  16.4 5.1 %collective-permute-start.2 = (bf16[112,4096]{1,0:T(8,128)(2,1)}, bf16[112,4096]{1,0:T(8,128)(2,1)S(1)}, u32[]{:S(2)}, u32[]{:S(2)}) collective-permute-start(bf16[112,4096]{1,0:T(8,128)(2,1)} %bitcast.6), channel_id=1, source_target_pairs={{0,4},{4,0},{1,5},{5,1},{2,6},{6,2},{3,7},{7,3},{8,12},{12,8},{9,1... | collective-permute-start | bytes 2752520 | tf_op jit(solution)/shard_map/ppermute | solution.py:290
  16.8 21.3 %collective-permute-start.4 = (bf16[112,4096]{1,0:T(8,128)(2,1)}, bf16[112,4096]{1,0:T(8,128)(2,1)S(1)}, u32[]{:S(2)}, u32[]{:S(2)}) collective-permute-start(bf16[112,4096]{1,0:T(8,128)(2,1)} %down0.1), channel_id=1, source_target_pairs={{0,4},{4,0},{1,5},{5,1},{2,6},{6,2},{3,7},{7,3},{8,12},{12,8},{9,1... | collective-permute-start | bytes 2752520 | tf_op jit(solution)/shard_map/ppermute | solution.py:290
  16.9 4.5 %collective-permute-start.3 = (bf16[1024,128]{1,0:T(8,128)(2,1)S(1)}, bf16[1024,128]{1,0:T(8,128)(2,1)S(1)}, u32[]{:S(2)}, u32[]{:S(2)}) collective-permute-start(bf16[1024,128]{1,0:T(8,128)(2,1)S(1)} %copy-done.5), channel_id=1, source_target_pairs={{0,4},{4,0},{1,5},{5,1},{2,6},{6,2},{3,7},{7,3},{8,12},{12,8},{9,1... | collective-permute-start | bytes 786440 | tf_op jit(solution)/shard_map/ppermute | solution.py:290
  19.1 2.0 %collective-permute-start = (bf16[136,128]{1,0:T(8,128)(2,1)S(1)}, bf16[136,128]{1,0:T(8,128)(2,1)S(1)}, u32[]{:S(2)}, u32[]{:S(2)}) collective-permute-start(bf16[136,128]{1,0:T(8,128)(2,1)S(1)} %shard_map.120), channel_id=1, source_target_pairs={{0,4},{4,0},{1,5},{5,1},{2,6},{6,2},{3,7},{7,3},{8,12},{12,8},{9,1... | collective-permute-start | bytes 104456 | tf_op jit(solution)/shard_map/ppermute | solution.py:290
  19.3 18.0 %copy-start.6 = (f32[1024]{0:T(1024)S(1)}, f32[1024]{0:T(1024)}, u32[]{:S(2)}) copy-start(f32[1024]{0:T(1024)} %param.20) | copy-start | bytes 12292
  19.3 40.4 %copy-start.2 = (bf16[4096,112]{0,1:T(8,128)(2,1)S(1)}, bf16[4096,112]{0,1:T(8,128)(2,1)}, u32[]{:S(2)}) copy-start(bf16[4096,112]{0,1:T(8,128)(2,1)} %param.21) | copy-start | bytes 2752516
  19.3 40.4 %copy-start.3 = (bf16[4096,112]{0,1:T(8,128)(2,1)S(1)}, bf16[4096,112]{0,1:T(8,128)(2,1)}, u32[]{:S(2)}) copy-start(bf16[4096,112]{0,1:T(8,128)(2,1)} %param.22) | copy-start | bytes 2752516
  19.3 40.4 %copy-start.4 = (bf16[112,4096]{1,0:T(8,128)(2,1)S(1)}, bf16[112,4096]{1,0:T(8,128)(2,1)}, u32[]{:S(2)}) copy-start(bf16[112,4096]{1,0:T(8,128)(2,1)} %down0.1) | copy-start | bytes 2752516

commit v7 on v5

--- a/solution.py
+++ b/solution.py
@@ -237,9 +237,12 @@
 
 
 def sum_kernel(parts, mid_row, out):
-    total = parts[0].astype(F32)
-    for s in range(1, CHIPS * TP):
-        total = total + parts[s].astype(F32)
+    chains = [parts[s].astype(F32) for s in range(8)]
+    for s in range(8, CHIPS * TP):
+        chains[s % 8] = chains[s % 8] + parts[s].astype(F32)
+    while len(chains) > 1:
+        chains = [x + y for x, y in zip(chains[::2], chains[1::2])]
+    total = chains[0]
     total = (mid_row[...] + total).astype(BF16)
     for r in range(8):
         out[:, r * HD : (r + 1) * HD] = total[r : r + 1, :]

time: 76.7 us -> 76.6 us (level)
  no operation moved by 1% of the time
where the time goes in v7:
time: 76.6 us; the launch traced here: 76.4 us
  blocking collectives  66.6 us (87%)
  Pallas kernels  7.95 us (10%)
  starting transfers between devices  1.2 us (2%)
    all_to_all x1, blocking collectives, shards(): columns = lax.all_to_all(columns, ('p', 't'), 0, 0, tiled=True)  21.4 us
    all_to_all x1, blocking collectives, shards(): blocks = lax.all_to_all(blocks, 'p', 0, 0, tiled=True)  15.5 us
    all_to_all x1, blocking collectives, shards(): gathered = lax.all_to_all(message, ('p', 'k'), 0, 0, tiled=True)  15.3 us
    all_to_all x1, blocking collectives, shards(): lax.all_to_all(partial.reshape(CHIPS * TP, 8, HD), ('p', 't'), 0, 0, tile...  14.5 us
    pallas_call x7, Pallas kernels, call(): pl.pallas_call(kernel, out_shape=out_shape, in_specs=specs, out_specs=jax...  7.95 us
  transfers between devices with their start and end apart: 5, of which 1 were waited for; matrix products, arithmetic and copies ran while one was open for 0% of the time, Pallas kernels for 5%

profile of v7, /device:TPU:0, one launch (start us, length us, event | category | flops | bytes accessed | tf_op | source)
XLA Modules:
  0.0 76.4 jit_solution(4629439716448275734)
XLA Ops:
  0.0 0.0 copy-start.1
  0.0 0.0 copy-start
  0.0 0.0 copy-start.5
  0.0 1.0 %shard_map.118 = (bf16[32,16,128]{2,1,0:T(8,128)(2,1)S(1)}, f32[2,8,128]{2,1,0:T(8,128)S(1)}, s32[32,128]{1,0:T(8,128)S(1)}) custom-call(bf16[1,1024]{1,0:T(2,128)(2,1)} %refs_0_.1, bf16[1,1024]{1,0:T(2,128)(2,1)} %refs_1_.1, bf16[1,256]{1,0:T(2,128)(2,1)} %refs_2_.1, bf16[1,256]{1,0:T(2,128)(2,1)} %refs_3_.1, s32[32]{0:T(128)} %refs_4_.1, ...), custom_call_target="tpu_custom_call" | custom-call | tf_op jit(solution)/shard_map/pallas_call | solution.py:266
  1.0 15.3 %all_to_all.20.gathered = bf16[32,16,128]{2,1,0:T(8,128)(2,1)S(1)} all-to-all(bf16[32,16,128]{2,1,0:T(8,128)(2,1)S(1)} %get-tuple-element.24), channel_id=1, replica_groups=mesh['p'=16,'k'=2,'t'=4] {'p','k'}, dimensions={0} | all-to-all | bytes 262144 | tf_op jit(solution)/shard_map/all_to_all | solution.py:308
  16.3 0.1 collective-permute-start.1
  16.4 0.4 collective-permute-start.2
  16.8 0.1 collective-permute-start.3
  16.9 0.0 copy-done.5
  16.9 0.4 collective-permute-start.4
  17.3 0.0 copy-done.1
  17.3 0.0 copy-done
  17.3 1.8 %shard_map.120 = bf16[136,128]{1,0:T(8,128)(2,1)S(1)} custom-call(s32[32,128]{1,0:T(8,128)S(1)} %get-tuple-element.23.limits, bf16[32,16,128]{2,1,0:T(8,128)(2,1)S(1)} %all_to_all.20.gathered, bf16[32,512,256]{2,1,0:T(8,128)(2,1)S(1)} %copy-done, bf16[32,512,256]{2,1,0:T(8,128)(2,1)S(1)} %copy-done.1), custom_call_target="tpu_custom_call" | custom-call | tf_op jit(solution)/shard_map/pallas_call | solution.py:266
  19.1 0.2 collective-permute-start
  19.3 0.0 copy-start.6
  19.3 0.0 copy-start.2
  19.3 0.0 copy-start.3
  19.3 0.0 copy-start.4
  19.3 1.8 %shard_map.119 = (f32[128,128]{1,0:T(8,128)S(1)}, f32[128,128]{1,0:T(8,128)S(1)}, f32[2,16,128]{2,1,0:T(8,128)S(1)}) custom-call(s32[32,128]{1,0:T(8,128)S(1)} %get-tuple-element.23.limits, bf16[32,16,128]{2,1,0:T(8,128)(2,1)S(1)} %all_to_all.20.gathered, f32[2,8,128]{2,1,0:T(8,128)S(1)} %get-tuple-element.26.own, bf16[32,512,256]{2,1,0:T(8,128)(2,1)S(1)} %copy-done, ...), custom_call_target="tpu_custom_call" | custom-call | tf_op jit(solution)/shard_map/pallas_call | solution.py:266
  21.1 0.0 collective-permute-done.came
  21.1 0.4 shard_map.121
  21.5 0.0 collective-permute-done.4.other_weight
  21.5 0.0 collective-permute-done.1.gate1
  21.5 0.0 collective-permute-done.2.up1
  21.5 0.6 collective-permute-done.3.down1
  22.0 15.5 %all_to_all.21.blocks = bf16[16,136,128]{2,1,0:T(8,128)(2,1)S(1)} all-to-all(bf16[16,136,128]{2,1,0:T(8,128)(2,1)S(1)} %shard_map.121), channel_id=1, replica_groups=mesh['p'=16,'k'=2,'t'=4] {'p'}, dimensions={0} | all-to-all | bytes 1114112 | tf_op jit(solution)/shard_map/all_to_all | solution.py:333
  37.5 0.0 copy-done.6
  37.5 0.8 %shard_map.122 = bf16[64,40,128]{2,1,0:T(8,128)(2,1)S(1)} custom-call(bf16[16,136,128]{2,1,0:T(8,128)(2,1)S(1)} %all_to_all.21.blocks, f32[2,16,128]{2,1,0:T(8,128)S(1)} %get-tuple-element.34.hidden_part, f32[8,128]{1,0:T(8,128)S(1)} %bitcast.9, bf16[1024,128]{1,0:T(8,128)(2,1)S(1)} %copy-done.5, bf16[1024,128]{1,0:T(8,128)(2,1)S(1)} %collective-permute-done.4.other_weight), custom_call_target="tpu_custom_call" | custom-call | tf_op jit(solution)/shard_map/pallas_call | solution.py:266
  38.4 21.4 %all_to_all.22.parts = bf16[64,40,128]{2,1,0:T(8,128)(2,1)S(1)} all-to-all(bf16[64,40,128]{2,1,0:T(8,128)(2,1)S(1)} %shard_map.122), channel_id=1, replica_groups=mesh['p'=16,'k'=2,'t'=4] {'p','t'}, dimensions={0} | all-to-all | bytes 1310720 | tf_op jit(solution)/shard_map/all_to_all | solution.py:339
  59.7 0.0 copy-done.2
  59.7 0.0 copy-done.3
  59.7 0.0 copy-done.4
  59.7 1.6 %shard_map.123 = (bf16[512,128]{1,0:T(8,128)(2,1)S(1)}, f32[8,128]{1,0:T(8,128)S(1)}) custom-call(bf16[64,40,128]{2,1,0:T(8,128)(2,1)S(1)} %all_to_all.22.parts, bf16[112,4096]{1,0:T(8,128)(2,1)S(1)} %bitcast.5, bf16[112,4096]{1,0:T(8,128)(2,1)S(1)} %bitcast.7, bf16[112,4096]{1,0:T(8,128)(2,1)S(1)} %collective-permute-done.1.gate1, ...), custom_call_target="tpu_custom_call" | custom-call | tf_op jit(solution)/shard_map/pallas_call | solution.py:266
  61.3 14.5 %all_to_all.23.parts = bf16[64,8,128]{2,1,0:T(8,128)(2,1)S(1)} all-to-all(bf16[64,8,128]{2,1,0:T(8,128)(2,1)S(1)} %bitcast.8), channel_id=1, replica_groups=mesh['p'=16,'k'=2,'t'=4] {'p','t'}, dimensions={0} | all-to-all | bytes 262144 | tf_op jit(solution)/shard_map/all_to_all | solution.py:350
  75.8 0.6 shard_map.124
Async XLA Ops:
  0.0 17.3 %copy-start.1 = (bf16[32,512,256]{2,1,0:T(8,128)(2,1)S(1)}, bf16[32,512,256]{2,1,0:T(8,128)(2,1)}, u32[]{:S(2)}) copy-start(bf16[32,512,256]{2,1,0:T(8,128)(2,1)} %values.3) | copy-start | bytes 25165828
  0.0 17.3 %copy-start = (bf16[32,512,256]{2,1,0:T(8,128)(2,1)S(1)}, bf16[32,512,256]{2,1,0:T(8,128)(2,1)}, u32[]{:S(2)}) copy-start(bf16[32,512,256]{2,1,0:T(8,128)(2,1)} %keys.3) | copy-start | bytes 25165828
  0.0 16.9 %copy-start.5 = (bf16[1024,128]{1,0:T(8,128)(2,1)S(1)}, bf16[1024,128]{1,0:T(8,128)(2,1)}, u32[]{:S(2)}) copy-start(bf16[1024,128]{1,0:T(8,128)(2,1)} %weight.1) | copy-start | bytes 786436
  16.3 5.2 %collective-permute-start.1 = (bf16[112,4096]{1,0:T(8,128)(2,1)}, bf16[112,4096]{1,0:T(8,128)(2,1)S(1)}, u32[]{:S(2)}, u32[]{:S(2)}) collective-permute-start(bf16[112,4096]{1,0:T(8,128)(2,1)} %bitcast.4), channel_id=1, source_target_pairs={{0,4},{4,0},{1,5},{5,1},{2,6},{6,2},{3,7},{7,3},{8,12},{12,8},{9,1... | collective-permute-start | bytes 2752520 | tf_op jit(solution)/shard_map/ppermute | solution.py:292
  16.4 5.1 %collective-permute-start.2 = (bf16[112,4096]{1,0:T(8,128)(2,1)}, bf16[112,4096]{1,0:T(8,128)(2,1)S(1)}, u32[]{:S(2)}, u32[]{:S(2)}) collective-permute-start(bf16[112,4096]{1,0:T(8,128)(2,1)} %bitcast.6), channel_id=1, source_target_pairs={{0,4},{4,0},{1,5},{5,1},{2,6},{6,2},{3,7},{7,3},{8,12},{12,8},{9,1... | collective-permute-start | bytes 2752520 | tf_op jit(solution)/shard_map/ppermute | solution.py:292
  16.8 5.2 %collective-permute-start.3 = (bf16[112,4096]{1,0:T(8,128)(2,1)}, bf16[112,4096]{1,0:T(8,128)(2,1)S(1)}, u32[]{:S(2)}, u32[]{:S(2)}) collective-permute-start(bf16[112,4096]{1,0:T(8,128)(2,1)} %down0.1), channel_id=1, source_target_pairs={{0,4},{4,0},{1,5},{5,1},{2,6},{6,2},{3,7},{7,3},{8,12},{12,8},{9,1... | collective-permute-start | bytes 2752520 | tf_op jit(solution)/shard_map/ppermute | solution.py:292
  16.9 4.5 %collective-permute-start.4 = (bf16[1024,128]{1,0:T(8,128)(2,1)S(1)}, bf16[1024,128]{1,0:T(8,128)(2,1)S(1)}, u32[]{:S(2)}, u32[]{:S(2)}) collective-permute-start(bf16[1024,128]{1,0:T(8,128)(2,1)S(1)} %copy-done.5), channel_id=1, source_target_pairs={{0,4},{4,0},{1,5},{5,1},{2,6},{6,2},{3,7},{7,3},{8,12},{12,8},{9,1... | collective-permute-start | bytes 786440 | tf_op jit(solution)/shard_map/ppermute | solution.py:292
  19.1 2.0 %collective-permute-start = (bf16[136,128]{1,0:T(8,128)(2,1)S(1)}, bf16[136,128]{1,0:T(8,128)(2,1)S(1)}, u32[]{:S(2)}, u32[]{:S(2)}) collective-permute-start(bf16[136,128]{1,0:T(8,128)(2,1)S(1)} %shard_map.120), channel_id=1, source_target_pairs={{0,4},{4,0},{1,5},{5,1},{2,6},{6,2},{3,7},{7,3},{8,12},{12,8},{9,1... | collective-permute-start | bytes 104456 | tf_op jit(solution)/shard_map/ppermute | solution.py:292
  19.3 18.3 %copy-start.6 = (f32[1024]{0:T(1024)S(1)}, f32[1024]{0:T(1024)}, u32[]{:S(2)}) copy-start(f32[1024]{0:T(1024)} %param.20) | copy-start | bytes 12292
  19.3 40.4 %copy-start.2 = (bf16[4096,112]{0,1:T(8,128)(2,1)S(1)}, bf16[4096,112]{0,1:T(8,128)(2,1)}, u32[]{:S(2)}) copy-start(bf16[4096,112]{0,1:T(8,128)(2,1)} %param.21) | copy-start | bytes 2752516
  19.3 40.4 %copy-start.3 = (bf16[4096,112]{0,1:T(8,128)(2,1)S(1)}, bf16[4096,112]{0,1:T(8,128)(2,1)}, u32[]{:S(2)}) copy-start(bf16[4096,112]{0,1:T(8,128)(2,1)} %param.22) | copy-start | bytes 2752516
  19.3 40.4 %copy-start.4 = (bf16[112,4096]{1,0:T(8,128)(2,1)S(1)}, bf16[112,4096]{1,0:T(8,128)(2,1)}, u32[]{:S(2)}) copy-start(bf16[112,4096]{1,0:T(8,128)(2,1)} %down0.1) | copy-start | bytes 2752516

commit v8 on v5

--- a/solution.py
+++ b/solution.py
@@ -58,7 +58,8 @@
 
 def start_kernel(*refs):
     sources, (message, own, limits), landed, arrived = refs[:5], refs[7:10], refs[10:15], refs[15]
-    for copy in copy_in(sources, landed, arrived):
+    copies = copy_in(sources, landed, arrived)
+    for copy in copies[:2]:
         copy.wait()
     query, hidden, own_key, own_value, lengths = landed
 
@@ -73,6 +74,8 @@
     queries = rows(query)
     both = jnp.concatenate([queries, rows(hidden)], axis=0).astype(BF16)
     message[...] = jnp.broadcast_to(both[None], message.shape)
+    for copy in copies[2:]:
+        copy.wait()
     score = jnp.sum(queries * heads(own_key), axis=1, keepdims=True) * (1.0 / math.sqrt(HD))
     own[0] = jnp.broadcast_to(score, (HEADS, HD))
     own[1] = heads(own_value)

time: 76.7 us -> 76.7 us (level)
  no operation moved by 1% of the time
where the time goes in v8:
time: 76.7 us; the launch traced here: 76.5 us
  blocking collectives  66.6 us (87%)
  Pallas kernels  8 us (10%)
  starting transfers between devices  1.2 us (2%)
    all_to_all x1, blocking collectives, shards(): columns = lax.all_to_all(columns, ('p', 't'), 0, 0, tiled=True)  21.4 us
    all_to_all x1, blocking collectives, shards(): blocks = lax.all_to_all(blocks, 'p', 0, 0, tiled=True)  15.5 us
    all_to_all x1, blocking collectives, shards(): gathered = lax.all_to_all(message, ('p', 'k'), 0, 0, tiled=True)  15.3 us
    all_to_all x1, blocking collectives, shards(): lax.all_to_all(partial.reshape(CHIPS * TP, 8, HD), ('p', 't'), 0, 0, tile...  14.5 us
    pallas_call x7, Pallas kernels, call(): pl.pallas_call(kernel, out_shape=out_shape, in_specs=specs, out_specs=jax...  8 us
  transfers between devices with their start and end apart: 5, of which 1 were waited for; matrix products, arithmetic and copies ran while one was open for 0% of the time, Pallas kernels for 5%

profile of v8, /device:TPU:0, one launch (start us, length us, event | category | flops | bytes accessed | tf_op | source)
XLA Modules:
  0.0 76.5 jit_solution(1129650274978080178)
XLA Ops:
  0.0 0.0 copy-start.1
  0.0 0.0 copy-start
  0.0 0.0 copy-start.5
  0.0 1.0 %shard_map.118 = (bf16[32,16,128]{2,1,0:T(8,128)(2,1)S(1)}, f32[2,8,128]{2,1,0:T(8,128)S(1)}, s32[32,128]{1,0:T(8,128)S(1)}) custom-call(bf16[1,1024]{1,0:T(2,128)(2,1)} %refs_0_.1, bf16[1,1024]{1,0:T(2,128)(2,1)} %refs_1_.1, bf16[1,256]{1,0:T(2,128)(2,1)} %refs_2_.1, bf16[1,256]{1,0:T(2,128)(2,1)} %refs_3_.1, s32[32]{0:T(128)} %refs_4_.1, ...), custom_call_target="tpu_custom_call" | custom-call | tf_op jit(solution)/shard_map/pallas_call | solution.py:266
  1.0 15.3 %all_to_all.20.gathered = bf16[32,16,128]{2,1,0:T(8,128)(2,1)S(1)} all-to-all(bf16[32,16,128]{2,1,0:T(8,128)(2,1)S(1)} %get-tuple-element.24), channel_id=1, replica_groups=mesh['p'=16,'k'=2,'t'=4] {'p','k'}, dimensions={0} | all-to-all | bytes 262144 | tf_op jit(solution)/shard_map/all_to_all | solution.py:308
  16.3 0.1 collective-permute-start.1
  16.4 0.4 collective-permute-start.2
  16.8 0.1 collective-permute-start.3
  16.9 0.0 copy-done.5
  16.9 0.4 collective-permute-start.4
  17.3 0.0 copy-done.1
  17.3 0.0 copy-done
  17.3 1.8 %shard_map.120 = bf16[136,128]{1,0:T(8,128)(2,1)S(1)} custom-call(s32[32,128]{1,0:T(8,128)S(1)} %get-tuple-element.23.limits, bf16[32,16,128]{2,1,0:T(8,128)(2,1)S(1)} %all_to_all.20.gathered, bf16[32,512,256]{2,1,0:T(8,128)(2,1)S(1)} %copy-done, bf16[32,512,256]{2,1,0:T(8,128)(2,1)S(1)} %copy-done.1), custom_call_target="tpu_custom_call" | custom-call | tf_op jit(solution)/shard_map/pallas_call | solution.py:266
  19.1 0.2 collective-permute-start
  19.3 0.0 copy-start.6
  19.3 0.0 copy-start.2
  19.3 0.0 copy-start.3
  19.3 0.0 copy-start.4
  19.3 1.8 %shard_map.119 = (f32[128,128]{1,0:T(8,128)S(1)}, f32[128,128]{1,0:T(8,128)S(1)}, f32[2,16,128]{2,1,0:T(8,128)S(1)}) custom-call(s32[32,128]{1,0:T(8,128)S(1)} %get-tuple-element.23.limits, bf16[32,16,128]{2,1,0:T(8,128)(2,1)S(1)} %all_to_all.20.gathered, f32[2,8,128]{2,1,0:T(8,128)S(1)} %get-tuple-element.26.own, bf16[32,512,256]{2,1,0:T(8,128)(2,1)S(1)} %copy-done, ...), custom_call_target="tpu_custom_call" | custom-call | tf_op jit(solution)/shard_map/pallas_call | solution.py:266
  21.1 0.0 collective-permute-done.came
  21.1 0.4 shard_map.121
  21.5 0.0 collective-permute-done.4.other_weight
  21.5 0.0 collective-permute-done.1.gate1
  21.5 0.0 collective-permute-done.2.up1
  21.5 0.6 collective-permute-done.3.down1
  22.0 15.5 %all_to_all.21.blocks = bf16[16,136,128]{2,1,0:T(8,128)(2,1)S(1)} all-to-all(bf16[16,136,128]{2,1,0:T(8,128)(2,1)S(1)} %shard_map.121), channel_id=1, replica_groups=mesh['p'=16,'k'=2,'t'=4] {'p'}, dimensions={0} | all-to-all | bytes 1114112 | tf_op jit(solution)/shard_map/all_to_all | solution.py:333
  37.5 0.0 copy-done.6
  37.5 0.8 %shard_map.122 = bf16[64,40,128]{2,1,0:T(8,128)(2,1)S(1)} custom-call(bf16[16,136,128]{2,1,0:T(8,128)(2,1)S(1)} %all_to_all.21.blocks, f32[2,16,128]{2,1,0:T(8,128)S(1)} %get-tuple-element.34.hidden_part, f32[8,128]{1,0:T(8,128)S(1)} %bitcast.9, bf16[1024,128]{1,0:T(8,128)(2,1)S(1)} %copy-done.5, bf16[1024,128]{1,0:T(8,128)(2,1)S(1)} %collective-permute-done.4.other_weight), custom_call_target="tpu_custom_call" | custom-call | tf_op jit(solution)/shard_map/pallas_call | solution.py:266
  38.4 21.4 %all_to_all.22.parts = bf16[64,40,128]{2,1,0:T(8,128)(2,1)S(1)} all-to-all(bf16[64,40,128]{2,1,0:T(8,128)(2,1)S(1)} %shard_map.122), channel_id=1, replica_groups=mesh['p'=16,'k'=2,'t'=4] {'p','t'}, dimensions={0} | all-to-all | bytes 1310720 | tf_op jit(solution)/shard_map/all_to_all | solution.py:339
  59.7 0.0 copy-done.2
  59.7 0.0 copy-done.3
  59.7 0.0 copy-done.4
  59.7 1.6 %shard_map.123 = (bf16[512,128]{1,0:T(8,128)(2,1)S(1)}, f32[8,128]{1,0:T(8,128)S(1)}) custom-call(bf16[64,40,128]{2,1,0:T(8,128)(2,1)S(1)} %all_to_all.22.parts, bf16[112,4096]{1,0:T(8,128)(2,1)S(1)} %bitcast.5, bf16[112,4096]{1,0:T(8,128)(2,1)S(1)} %bitcast.7, bf16[112,4096]{1,0:T(8,128)(2,1)S(1)} %collective-permute-done.1.gate1, ...), custom_call_target="tpu_custom_call" | custom-call | tf_op jit(solution)/shard_map/pallas_call | solution.py:266
  61.3 14.5 %all_to_all.23.parts = bf16[64,8,128]{2,1,0:T(8,128)(2,1)S(1)} all-to-all(bf16[64,8,128]{2,1,0:T(8,128)(2,1)S(1)} %bitcast.8), channel_id=1, replica_groups=mesh['p'=16,'k'=2,'t'=4] {'p','t'}, dimensions={0} | all-to-all | bytes 262144 | tf_op jit(solution)/shard_map/all_to_all | solution.py:350
  75.8 0.7 shard_map.124
Async XLA Ops:
  0.0 17.3 %copy-start.1 = (bf16[32,512,256]{2,1,0:T(8,128)(2,1)S(1)}, bf16[32,512,256]{2,1,0:T(8,128)(2,1)}, u32[]{:S(2)}) copy-start(bf16[32,512,256]{2,1,0:T(8,128)(2,1)} %values.3) | copy-start | bytes 25165828
  0.0 17.3 %copy-start = (bf16[32,512,256]{2,1,0:T(8,128)(2,1)S(1)}, bf16[32,512,256]{2,1,0:T(8,128)(2,1)}, u32[]{:S(2)}) copy-start(bf16[32,512,256]{2,1,0:T(8,128)(2,1)} %keys.3) | copy-start | bytes 25165828
  0.0 16.9 %copy-start.5 = (bf16[1024,128]{1,0:T(8,128)(2,1)S(1)}, bf16[1024,128]{1,0:T(8,128)(2,1)}, u32[]{:S(2)}) copy-start(bf16[1024,128]{1,0:T(8,128)(2,1)} %weight.1) | copy-start | bytes 786436
  16.3 5.2 %collective-permute-start.1 = (bf16[112,4096]{1,0:T(8,128)(2,1)}, bf16[112,4096]{1,0:T(8,128)(2,1)S(1)}, u32[]{:S(2)}, u32[]{:S(2)}) collective-permute-start(bf16[112,4096]{1,0:T(8,128)(2,1)} %bitcast.4), channel_id=1, source_target_pairs={{0,4},{4,0},{1,5},{5,1},{2,6},{6,2},{3,7},{7,3},{8,12},{12,8},{9,1... | collective-permute-start | bytes 2752520 | tf_op jit(solution)/shard_map/ppermute | solution.py:292
  16.4 5.1 %collective-permute-start.2 = (bf16[112,4096]{1,0:T(8,128)(2,1)}, bf16[112,4096]{1,0:T(8,128)(2,1)S(1)}, u32[]{:S(2)}, u32[]{:S(2)}) collective-permute-start(bf16[112,4096]{1,0:T(8,128)(2,1)} %bitcast.6), channel_id=1, source_target_pairs={{0,4},{4,0},{1,5},{5,1},{2,6},{6,2},{3,7},{7,3},{8,12},{12,8},{9,1... | collective-permute-start | bytes 2752520 | tf_op jit(solution)/shard_map/ppermute | solution.py:292
  16.8 5.2 %collective-permute-start.3 = (bf16[112,4096]{1,0:T(8,128)(2,1)}, bf16[112,4096]{1,0:T(8,128)(2,1)S(1)}, u32[]{:S(2)}, u32[]{:S(2)}) collective-permute-start(bf16[112,4096]{1,0:T(8,128)(2,1)} %down0.1), channel_id=1, source_target_pairs={{0,4},{4,0},{1,5},{5,1},{2,6},{6,2},{3,7},{7,3},{8,12},{12,8},{9,1... | collective-permute-start | bytes 2752520 | tf_op jit(solution)/shard_map/ppermute | solution.py:292
  16.9 4.5 %collective-permute-start.4 = (bf16[1024,128]{1,0:T(8,128)(2,1)S(1)}, bf16[1024,128]{1,0:T(8,128)(2,1)S(1)}, u32[]{:S(2)}, u32[]{:S(2)}) collective-permute-start(bf16[1024,128]{1,0:T(8,128)(2,1)S(1)} %copy-done.5), channel_id=1, source_target_pairs={{0,4},{4,0},{1,5},{5,1},{2,6},{6,2},{3,7},{7,3},{8,12},{12,8},{9,1... | collective-permute-start | bytes 786440 | tf_op jit(solution)/shard_map/ppermute | solution.py:292
  19.1 2.0 %collective-permute-start = (bf16[136,128]{1,0:T(8,128)(2,1)S(1)}, bf16[136,128]{1,0:T(8,128)(2,1)S(1)}, u32[]{:S(2)}, u32[]{:S(2)}) collective-permute-start(bf16[136,128]{1,0:T(8,128)(2,1)S(1)} %shard_map.120), channel_id=1, source_target_pairs={{0,4},{4,0},{1,5},{5,1},{2,6},{6,2},{3,7},{7,3},{8,12},{12,8},{9,1... | collective-permute-start | bytes 104456 | tf_op jit(solution)/shard_map/ppermute | solution.py:292
  19.3 18.3 %copy-start.6 = (f32[1024]{0:T(1024)S(1)}, f32[1024]{0:T(1024)}, u32[]{:S(2)}) copy-start(f32[1024]{0:T(1024)} %param.20) | copy-start | bytes 12292
  19.3 40.4 %copy-start.2 = (bf16[4096,112]{0,1:T(8,128)(2,1)S(1)}, bf16[4096,112]{0,1:T(8,128)(2,1)}, u32[]{:S(2)}) copy-start(bf16[4096,112]{0,1:T(8,128)(2,1)} %param.21) | copy-start | bytes 2752516
  19.3 40.4 %copy-start.3 = (bf16[4096,112]{0,1:T(8,128)(2,1)S(1)}, bf16[4096,112]{0,1:T(8,128)(2,1)}, u32[]{:S(2)}) copy-start(bf16[4096,112]{0,1:T(8,128)(2,1)} %param.22) | copy-start | bytes 2752516
  19.3 40.4 %copy-start.4 = (bf16[112,4096]{1,0:T(8,128)(2,1)S(1)}, bf16[112,4096]{1,0:T(8,128)(2,1)}, u32[]{:S(2)}) copy-start(bf16[112,4096]{1,0:T(8,128)(2,1)} %down0.1) | copy-start | bytes 2752516
